TPU v7x, 128 devices: a whole 4x4x4 slice. The times are simulated.
128 devices in a mesh: dp: 16 (over z_hi, x, core), row: 2 (over z_lo), col: 4 (over y).
Axes of the slice: x: 4, y: 4, z: 4 (z_hi: 2, z_lo: 2; z = z_hi * 2 + z_lo), core: 2. Of those that a mesh axis runs over, the one named last changes fastest.
Arguments:
- block_in: bfloat16 [16384, 1536], P(('dp', 'row'), 'col'), may hold values from -16 to 16
- norm_gain: bfloat16 [1536], P('col'), may hold values from 0.25 to 1.75
- in_weight: bfloat16 [3, 1536, 1536], P(None, 'col', 'row'), may hold values from -0.15625 to 0.15625
- conv_weight: bfloat16 [3, 1536], P(None, ('row', 'col')), may hold values from -3 to 3
- out_weight: bfloat16 [1536, 1536], P('row', 'col'), may hold values from -0.15625 to 0.15625
- ffn_gain: bfloat16 [1536], P('col'), may hold values from 0.25 to 1.75
- gate_up_weight: bfloat16 [2, 1536, 6912], P(None, 'col', 'row'), may hold values from -0.15625 to 0.15625
- down_weight: bfloat16 [6912, 1536], P('row', 'col'), may hold values from -0.15625 to 0.15625
- out_grad: bfloat16 [16384, 1536], P(('dp', 'row'), 'col'), may hold values from -5 to 5
Outputs:
- block_out: bfloat16 [16384, 1536], P(('dp', 'row'), 'col')
- in_grad: bfloat16 [16384, 1536], P(('dp', 'row'), 'col')
- norm_gain_grad: float32 [1536], P('col')
- in_weight_grad: float32 [3, 1536, 1536], P(None, 'col', 'row')
- conv_grad: float32 [3, 1536], P(None, ('row', 'col'))
- out_weight_grad: float32 [1536, 1536], P('row', 'col')
- ffn_gain_grad: float32 [1536], P('col')
- gate_up_grad: float32 [2, 1536, 6912], P(None, 'col', 'row')
- down_grad: float32 [6912, 1536], P('row', 'col')
All inputs are finite; a program needn't handle non-finite values.
Results may differ from a plain program's by a relative error of at most 0.0095.
Values may be sent and summed in bfloat16 or wider, within the bound.
No kernel may reach another device: no remote copies, remote signals or barrier semaphores. Data moves between devices by JAX's collectives and lax.ppermute only.
A program may use at most 256 MiB of HBM per device.

v0:
```python
import jax
import jax.numpy as jnp
from jax import lax
from jax.sharding import PartitionSpec as P

D = 1536
KERNEL = 3
LEN = 1024


EPSILON = 1e-05


def feature_total(values):
    return lax.psum(jnp.sum(values, axis=1), "col")


def norm_forward(stream, gain_vec):
    inv_rms = lax.rsqrt(feature_total(stream * stream) / D + EPSILON)
    normed_hat = stream * inv_rms[:, None]
    return (inv_rms, normed_hat, (normed_hat * gain_vec).astype(jnp.bfloat16))


def norm_backward(gradient, inv_rms, normed_hat, gain_vec):
    weighted = gradient * gain_vec
    inner_mean = feature_total(weighted * normed_hat) / D
    stream_part = inv_rms[:, None] * (weighted - normed_hat * inner_mean[:, None])
    return (stream_part, jnp.sum(gradient * normed_hat, axis=0))


def project_in(normed, weight):
    gathered = lax.all_gather(normed, "row", axis=0, tiled=True)
    partial_sum = jnp.einsum("td,jde->jte", gathered, weight, preferred_element_type=jnp.float32)
    result = lax.psum_scatter(partial_sum, "col", scatter_dimension=2, tiled=True)
    return (gathered, result)


def gather_features(active):
    return lax.all_gather(active, "col", axis=1, tiled=True)


def project_out(gathered, weight):
    return lax.psum_scatter(
        jnp.dot(gathered, weight, preferred_element_type=jnp.float32),
        "row",
        scatter_dimension=0,
        tiled=True,
    )


def back_out(grad_half, gathered, weight):
    grad_all = lax.all_gather(grad_half, "row", axis=0, tiled=True)
    weight_grad = jnp.einsum("tf,td->fd", gathered, grad_all, preferred_element_type=jnp.float32)
    partial_sum = jnp.einsum("td,fd->tf", grad_all, weight, preferred_element_type=jnp.float32)
    return (weight_grad, lax.psum_scatter(partial_sum, "col", scatter_dimension=1, tiled=True))


def back_in(grad_part, gathered, weight):
    grad_all = lax.all_gather(grad_part, "col", axis=2, tiled=True)
    weight_grad = jnp.einsum("td,jte->jde", gathered, grad_all, preferred_element_type=jnp.float32)
    partial_sum = jnp.einsum("jte,jde->td", grad_all, weight, preferred_element_type=jnp.float32)
    return (weight_grad, lax.psum_scatter(partial_sum, "row", scatter_dimension=0, tiled=True))


def shifted(signal, offset):
    if offset > 0:
        return jnp.pad(signal[:, :-offset], ((0, 0), (offset, 0), (0, 0)))
    if offset < 0:
        return jnp.pad(signal[:, -offset:], ((0, 0), (0, -offset), (0, 0)))
    return signal


def body(
    block_in,
    norm_gain,
    in_weight,
    conv_weight,
    out_weight,
    ffn_gain,
    gate_up_weight,
    down_weight,
    out_grad,
):
    stream_in = block_in.astype(jnp.float32)
    gain_one = norm_gain.astype(jnp.float32)
    gain_two = ffn_gain.astype(jnp.float32)
    kernel = conv_weight.astype(jnp.float32)
    inv_one, hat_one, normed_one = norm_forward(stream_in, gain_one)
    tokens_one, projected = project_in(normed_one, in_weight)
    channels = projected.shape[2]
    mixed_in = (projected[0] * projected[2]).reshape(-1, LEN, channels)
    convolved = kernel[0] * mixed_in
    for lag in range(1, KERNEL):
        convolved = convolved + kernel[lag] * shifted(mixed_in, lag)
    convolved = convolved.reshape(-1, channels)
    mixer_act = (projected[1] * convolved).astype(jnp.bfloat16)
    feats_mixer = gather_features(mixer_act)
    stream = stream_in + project_out(feats_mixer, out_weight)
    inv_two, hat_two, normed_two = norm_forward(stream, gain_two)
    tokens_two, gate_up = project_in(normed_two, gate_up_weight)
    sigmoid_gate = jax.nn.sigmoid(gate_up[0])
    silu_gate = gate_up[0] * sigmoid_gate
    hidden = (silu_gate * gate_up[1]).astype(jnp.bfloat16)
    feats_hidden = gather_features(hidden)
    block_out = (stream + project_out(feats_hidden, down_weight)).astype(jnp.bfloat16)
    down_grad, hidden_grad = back_out(out_grad, feats_hidden, down_weight)
    gate_back = hidden_grad * gate_up[1] * sigmoid_gate * (1.0 + gate_up[0] * (1.0 - sigmoid_gate))
    up_back = hidden_grad * silu_gate
    gate_up_back = jnp.stack([gate_back, up_back]).astype(jnp.bfloat16)
    gate_up_grad, normed_two_grad = back_in(gate_up_back, tokens_two, gate_up_weight)
    stream_part, gain_two_part = norm_backward(normed_two_grad, inv_two, hat_two, gain_two)
    stream_grad = out_grad.astype(jnp.float32) + stream_part
    out_weight_grad, mixer_grad = back_out(
        stream_grad.astype(jnp.bfloat16), feats_mixer, out_weight
    )
    conv_back = (mixer_grad * projected[1]).reshape(-1, LEN, channels)
    c_back = mixer_grad * convolved
    mixed_grad = kernel[0] * conv_back
    for lag in range(1, KERNEL):
        mixed_grad = mixed_grad + kernel[lag] * shifted(conv_back, -lag)
    kernel_grad = jnp.stack(
        [jnp.sum(conv_back * shifted(mixed_in, lag), axis=(0, 1)) for lag in range(KERNEL)]
    )
    mixed_grad = mixed_grad.reshape(-1, channels)
    proj_back = jnp.stack([mixed_grad * projected[2], c_back, mixed_grad * projected[0]]).astype(
        jnp.bfloat16
    )
    in_weight_grad, normed_one_grad = back_in(proj_back, tokens_one, in_weight)
    input_part, gain_one_part = norm_backward(normed_one_grad, inv_one, hat_one, gain_one)
    in_grad = (stream_grad + input_part).astype(jnp.bfloat16)
    gain_one_grad, gain_two_grad = lax.psum((gain_one_part, gain_two_part), "row")
    (
        in_weight_grad,
        kernel_grad,
        out_weight_grad,
        gate_up_grad,
        down_grad,
        gain_one_grad,
        gain_two_grad,
    ) = lax.psum(
        (
            in_weight_grad,
            kernel_grad,
            out_weight_grad,
            gate_up_grad,
            down_grad,
            gain_one_grad,
            gain_two_grad,
        ),
        "dp",
    )
    return (
        block_out,
        in_grad,
        gain_one_grad,
        in_weight_grad,
        kernel_grad,
        out_weight_grad,
        gain_two_grad,
        gate_up_grad,
        down_grad,
    )


def solution(mesh):
    in_specs = (
        P(("dp", "row"), "col"),
        P("col"),
        P(None, "col", "row"),
        P(None, ("row", "col")),
        P("row", "col"),
        P("col"),
        P(None, "col", "row"),
        P("row", "col"),
        P(("dp", "row"), "col"),
    )
    out_specs = (
        P(("dp", "row"), "col"),
        P(("dp", "row"), "col"),
        P("col"),
        P(None, "col", "row"),
        P(None, ("row", "col")),
        P("row", "col"),
        P("col"),
        P(None, "col", "row"),
        P("row", "col"),
    )
    return jax.shard_map(body, mesh=mesh, in_specs=in_specs, out_specs=out_specs, check_vma=False)
```

profile of v0, /device:TPU:0, one launch (start us, length us, event | category | flops | bytes accessed | tf_op | source)
XLA Modules:
  0.0 1663.4 jit_solution(14617562106535328185)
XLA Ops:
  8.5 10.8 psum.91
  21.2 9.7 all_gather.24
  38.5 14.0 copy.41
  52.5 17.6 %copy.52 = f32[96,8,3,1024]{3,1,2,0:T(8,128)} copy(f32[96,8,3,1024]{3,2,1,0:T(4,128)} %bitcast.127) | data formatting | bytes 18874368
  70.8 88.4 %reduce-scatter.22.cloned.1.call-done = f32[192,3072]{1,0:T(8,128)} async-done(((f32[768,3072]{1,0:T(8,128)}), f32[192,3072]{1,0:T(8,128)}) %reduce-scatter.22.cloned.1.call-update) | async-done | bytes 2359312
  163.9 7.3 fusion.41
  184.8 26.3 %all-gather.5.cloned.1.call-done = bf16[1024,768]{0,1:T(8,128)(2,1)} async-done(((bf16[1024,192]{0,1:T(8,128)(2,1)}), bf16[1024,768]{0,1:T(8,128)(2,1)}) %all-gather.5.cloned.1.call-update) | async-done | bytes 1572880 | tf_op jit(solution)/shard_map/all_gather | solution.py:39
  214.9 28.8 %reduce-scatter.14.cloned.1.call-done = f32[512,384]{1,0:T(8,128)} async-done(((f32[1024,384]{1,0:T(8,128)}), f32[512,384]{1,0:T(8,128)}) %reduce-scatter.14.cloned.1.call-update) | async-done | bytes 786448 | tf_op jit(solution)/shard_map/reduce_scatter | solution.py:43
  245.1 10.5 psum.92
  255.8 9.5 all_gather.26
  266.2 15.5 convolution_bitcast_fusion
  281.7 41.9 %copy.27 = f32[2,1024,3456]{1,0,2:T(2,128)} copy(f32[2,1024,3456]{2,1,0:T(8,128)} %convolution_bitcast_fusion) | data formatting | bytes 56623104 | tf_op jit(solution)/shard_map/td,jde->jte/transpose | solution.py:33
  323.7 8.8 all_gather.28
  333.3 7.1 convolution_bitcast_fusion.1
  342.3 461.2 %all-reduce.11.cloned.1.call-done = f32[2,1024,3456]{1,0,2:T(2,128)} async-done(((f32[2,1024,3456]{1,0,2:T(2,128)}), f32[2,1024,3456]{1,0,2:T(2,128)}) %all-reduce.11.cloned.1.call-update) | async-done | bytes 28311568
  803.5 10.1 constant_dynamic-slice_fusion
  813.7 119.4 %reduce-scatter.24.cloned.1.call-done = f32[864,1024]{1,0:T(8,128)} async-done(((f32[3456,1024]{1,0:T(8,128)}), f32[864,1024]{1,0:T(8,128)}) %reduce-scatter.24.cloned.1.call-update) | async-done | bytes 3538960
  945.7 131.7 %all-gather.9.cloned.1.call-done = bf16[2,1024,3456]{1,0,2:T(2,128)(2,1)} async-done(((bf16[2,1024,864]{1,0,2:T(2,128)(2,1)}), bf16[2,1024,3456]{1,0,2:T(2,128)(2,1)}) %all-gather.9.cloned.1.call-update) | async-done | bytes 14155792 | tf_op jit(solution)/shard_map/all_gather | solution.py:59
  1077.4 14.0 fusion.15
  1091.5 29.7 %reduce-scatter.18.cloned.1.call-done = f32[512,384]{1,0:T(8,128)} async-done(((f32[1024,384]{1,0:T(8,128)}), f32[512,384]{1,0:T(8,128)}) %reduce-scatter.18.cloned.1.call-update) | async-done | bytes 786448 | tf_op jit(solution)/shard_map/reduce_scatter | solution.py:62
  1122.7 10.7 psum.93
  1134.9 9.5 all_gather.30
  1148.1 37.2 %reduce-scatter.26.cloned.1.call-done = f32[192,1024]{1,0:T(8,128)} async-done(((f32[768,1024]{1,0:T(8,128)}), f32[192,1024]{1,0:T(8,128)}) %reduce-scatter.26.cloned.1.call-update) | async-done | bytes 786448
  1197.8 51.9 %all-gather.11.cloned.1.call-done = bf16[3,1024,768]{1,2,0:T(8,128)(2,1)} async-done(((bf16[3,1024,192]{1,2,0:T(8,128)(2,1)}), bf16[3,1024,768]{1,2,0:T(8,128)(2,1)}) %all-gather.11.cloned.1.call-update) | async-done | bytes 4718608 | tf_op jit(solution)/shard_map/all_gather | solution.py:59
  1256.5 68.1 %all-gather.7.cloned.1.call-done = bf16[1024,3456]{0,1:T(8,128)(2,1)} async-done(((bf16[1024,864]{0,1:T(8,128)(2,1)}), bf16[1024,3456]{0,1:T(8,128)(2,1)}) %all-gather.7.cloned.1.call-update) | async-done | bytes 7077904 | tf_op jit(solution)/shard_map/all_gather | solution.py:39
  1324.6 7.3 fusion.44
  1332.0 9.5 fusion.46
  1341.5 16.2 fusion.4
  1371.4 38.0 %all-reduce.5 = (f32[384]{0:T(512)}, f32[3,192]{1,0:T(4,128)}, f32[384]{0:T(512)}) all-reduce(f32[384]{0:T(512)S(1)} %get-tuple-element.40, f32[3,192]{1,0:T(4,128)S(1)} %pad_maximum_fusion.2, f32[384]{0:T(512)S(1)} %get-tuple-element.41), channel_id=1, replica_groups=mesh['dp'=16,'row'=2,'col'=4] {'dp'}, use_global_device_ids=true, to_apply=%region_18.19 | all-reduce | flops 1344 | bytes 10752 | tf_op jit(solution)/shard_map/psum | solution.py:140
  1409.4 9.2 psum.94
  1421.9 210.2 %all-reduce.13.cloned.1.call-done = (f32[3,384,768]{1,2,0:T(8,128)}, f32[768,384]{1,0:T(8,128)}, f32[2,384,3456]{1,2,0:T(8,128)}, f32[3456,384]{1,0:T(8,128)}) async-done(((f32[3,384,768]{1,2,0:T(8,128)}, f32[768,384]{1,0:T(8,128)}, f32[2,384,3456]{1,2,0:T(8,128)}, f32[3456,384]{1,0:T(8,128)}), (f32[3,384,768]{1,2,0:T(8,128)}, f32[768,384]{1,0:T(8,128)}, f32[2,384,3456]{1,2,0:T(8,128)}, ...) | async-done | bytes 20643856 | tf_op jit(solution)/shard_map/psum | solution.py:140
  1632.1 11.6 copy.38
  (122 shorter events, 106.4 us)
Async XLA Ops:
  7.2 326.2 %copy-start = (bf16[3456,384]{1,0:T(8,128)(2,1)S(1)}, bf16[3456,384]{1,0:T(8,128)(2,1)}, u32[]{:S(2)}) copy-start(bf16[3456,384]{1,0:T(8,128)(2,1)} %param.16) | copy-start | bytes 7962628
  7.2 152.0 %reduce-scatter.22.cloned.1.call-start = ((), (), s32[]{:S(2)}) async-start(), calls=%async_computation.15 | async-start | bytes 11796480
  20.1 1.2 copy-start.16
  30.9 1.0 copy-start.11
  70.1 141.0 %all-gather.5.cloned.1.call-start = ((), (), s32[]{:S(2)}) async-start(), calls=%async_computation.7 | async-start | bytes 1966080 | tf_op jit(solution)/shard_map/all_gather | solution.py:39
  179.6 2.8 copy-start.5
  181.4 1.0 copy-start.1
  184.7 30.2 %copy-start.19 = (bf16[384]{0:T(512)(128)(2,1)S(1)}, bf16[384]{0:T(512)(128)(2,1)}, u32[]{:S(2)}) copy-start(bf16[384]{0:T(512)(128)(2,1)} %param.14) | copy-start | bytes 2308
  184.7 59.0 %reduce-scatter.14.cloned.1.call-start = ((), (), s32[]{:S(2)}) async-start(), calls=%async_computation.8 | async-start | bytes 2359296 | tf_op jit(solution)/shard_map/reduce_scatter | solution.py:43
  214.9 588.7 %all-reduce.11.cloned.1.call-start = ((), (), s32[]{:S(2)}) async-start(), calls=%async_computation.18 | async-start | bytes 56623104
  265.3 0.9 copy-start.8
  323.6 609.5 %reduce-scatter.24.cloned.1.call-start = ((), (), s32[]{:S(2)}) async-start(), calls=%async_computation.16 | async-start | bytes 17694720
  332.5 0.9 copy-start.10
  340.4 737.0 %all-gather.9.cloned.1.call-start = ((), (), s32[]{:S(2)}) async-start(), calls=%async_computation.11 | async-start | bytes 17694720 | tf_op jit(solution)/shard_map/all_gather | solution.py:59
  945.7 175.6 %reduce-scatter.18.cloned.1.call-start = ((), (), s32[]{:S(2)}) async-start(), calls=%async_computation.12 | async-start | bytes 2359296 | tf_op jit(solution)/shard_map/reduce_scatter | solution.py:62
  1091.4 93.8 %reduce-scatter.26.cloned.1.call-start = ((), (), s32[]{:S(2)}) async-start(), calls=%async_computation.17 | async-start | bytes 3932160
  1133.4 12.0 copy-start.13
  1144.4 0.9 copy-start.6
  1148.0 101.7 %all-gather.11.cloned.1.call-start = ((), (), s32[]{:S(2)}) async-start(), calls=%async_computation.13 | async-start | bytes 5898240 | tf_op jit(solution)/shard_map/all_gather | solution.py:59
  1190.2 1.2 copy-start.2
  1190.2 1.5 copy-start.4
  1191.8 1.2 copy-start.3
  1197.2 127.4 %all-gather.7.cloned.1.call-start = ((), (), s32[]{:S(2)}) async-start(), calls=%async_computation.9 | async-start | bytes 8847360 | tf_op jit(solution)/shard_map/all_gather | solution.py:39
  1197.8 166.5 %reduce-scatter.20.cloned.1.call-start = ((), (), s32[]{:S(2)}) async-start(), calls=%async_computation.14 | async-start | bytes 2359296 | tf_op jit(solution)/shard_map/reduce_scatter | solution.py:62
  1256.4 162.3 %reduce-scatter.16.cloned.1.call-start = ((), (), s32[]{:S(2)}) async-start(), calls=%async_computation.10 | async-start | bytes 2359296 | tf_op jit(solution)/shard_map/reduce_scatter | solution.py:43
  1331.9 300.2 %all-reduce.13.cloned.1.call-start = ((), (), s32[]{:S(2)}) async-start(), calls=%async_computation.19 | async-start | bytes 41287680 | tf_op jit(solution)/shard_map/psum | solution.py:140
  1332.0 9.5 copy-start.9
  1332.0 27.7 %slice-start = ((s8[4718592]{0:T(1024)(128)(4,1)}), s8[4194304]{0:T(1024)(128)(4,1)S(1)}, s32[]{:S(2)}) async-start(s8[4718592]{0:T(1024)(128)(4,1)} %bitcast.142), calls=%async_computation.20 | async-start | bytes 8388608
  1341.5 16.2 copy-start.7
  1341.5 16.2 copy-start.20
  1341.5 18.2 %slice-start.1 = ((s8[4718592]{0:T(1024)(128)(4,1)}), s8[524288]{0:T(1024)(128)(4,1)S(1)}, s32[]{:S(2)}) async-start(s8[4718592]{0:T(1024)(128)(4,1)} %bitcast.142), calls=%async_computation.21 | async-start | bytes 1048576
  1357.7 2.0 copy-start.12
  (5 other events, 3.4 us)
Sparse Core Ops, SparseCore 0:
  70.3 88.8 reduce-scatter.21
  184.9 26.2 all-gather.4
  215.0 28.7 reduce-scatter.13
  323.7 479.7 all-reduce.10
  805.8 127.1 reduce-scatter.23
  945.8 131.6 all-gather.8
  1091.6 29.6 reduce-scatter.17
  1148.2 37.0 reduce-scatter.25
  1197.3 52.3 all-gather.10
  1251.9 72.6 all-gather.6
  1327.1 29.3 reduce-scatter.19
  1358.7 29.8 reduce-scatter.15
  1392.8 239.3 all-reduce.12
where the time goes:
time: 1670 us; the launch traced here: 1660 us
  waiting for transfers between devices  1250 us (75%)
  local copies, waits for them, and re-layouts  148 us (9%)
  blocking collectives  122 us (7%)
  matrix products  95.8 us (6%)
  other arithmetic  27.7 us (2%)
    unnamed x17, waiting for transfers between devices  707 us
    psum x1, waiting for transfers between devices, body(): lax.psum((in_weight_grad, kernel_grad, out_weight_grad, gate_up_grad, dow...  210 us
    all_gather x2, waiting for transfers between devices, back_in(): grad_all = lax.all_gather(grad_part, 'col', axis=2, tiled=True)  184 us
    all_gather x2, waiting for transfers between devices, gather_features(): return lax.all_gather(active, 'col', axis=1, tiled=True)  94.4 us
    unnamed x60, local copies, waits for them, and re-layouts  79.8 us
    transpose x1, local copies, waits for them, and re-layouts, project_in(): jnp.einsum('td,jde->jte', gathered, weight, preferred_element_type=jnp.fl...  41.9 us
    psum x4, blocking collectives, feature_total(): return lax.psum(jnp.sum(values, axis=1), 'col')  41.3 us
    psum x1, blocking collectives, body(): lax.psum((in_weight_grad, kernel_grad, out_weight_grad, gate_up_grad, dow...  38 us
  transfers between devices with their start and end apart: 13, of which 11 were waited for; matrix products, arithmetic and copies ran while one was open for 4% of the time, Pallas kernels for 0%

commit v1 on v0

v1 whole, which is shorter than its diff:
```python
import jax
import jax.numpy as jnp
from jax import lax
from jax.sharding import Mesh, PartitionSpec as P

D = 1536
LEN = 1024
EPSILON = 1e-05
FB = 896
FSTARTS = (0, 896, 1792, 2560)

bf16 = jnp.bfloat16
f32 = jnp.float32


def yshift(v, d):
    return lax.ppermute(v, "y", [(i, (i + d) % 4) for i in range(4)])


def xshift(v, d):
    return lax.ppermute(v, "x", [(i, (i + d) % 4) for i in range(4)])


def zshift(v, d):
    return lax.ppermute(v, ("zh", "zl"), [(i, (i + d) % 4) for i in range(4)])


def kswap(v):
    return lax.ppermute(v, "k", [(0, 1), (1, 0)])


def ygather(v):
    two = yshift(v, 2)
    return [v, yshift(v, 3), two, yshift(v, 1)]


def yexchange(block_for):
    two = yshift(block_for(2), 2)
    one = yshift(block_for(1), 1)
    three = yshift(block_for(3), 3)
    return [block_for(0), three, two, one]


def yreduce(pieces):
    got = yexchange(lambda j: pieces[j].astype(bf16) if j else pieces[0])
    return got[0].astype(f32) + got[1].astype(f32) + got[2].astype(f32) + got[3].astype(f32)


def zexchange(v):
    half = v.shape[0] // 2
    up = zshift(v[:half], 1)
    down = zshift(v[half:], 3)
    return jnp.concatenate([up, down], axis=0)


def pick(stacked, index):
    return lax.dynamic_index_in_dim(stacked, index, 0, keepdims=False)


def dot(a, b):
    return jnp.dot(a, b, preferred_element_type=f32)


def dot_t(a, b):
    return lax.dot_general(a, b, (((1,), (1,)), ((), ())), preferred_element_type=f32)


def t_dot(a, b):
    return lax.dot_general(a, b, (((0,), (0,)), ((), ())), preferred_element_type=f32)


def both(k, mine, other, axis):
    return jnp.where(
        k == 0,
        jnp.concatenate([mine, other], axis=axis),
        jnp.concatenate([other, mine], axis=axis),
    )


def fetch_in(weight, k, y):
    rows = lax.dynamic_slice_in_dim(weight, k * 192, 192, axis=1)
    blocks = jnp.stack([rows[:, :, 192 * b : 192 * b + 192] for b in range(4)])
    own = jnp.stack(yexchange(lambda j: pick(blocks, (y + j) % 4)))
    other = zexchange(own)
    halves = jnp.stack([own, other])
    swapped = kswap(halves)
    full = both(k, halves, swapped, 3)
    return [full[r].transpose(0, 2, 1, 3).reshape(D, 3 * 192) for r in range(2)]


def fetch_out(weight, k, y):
    rows = lax.dynamic_slice_in_dim(weight, k * 384, 384, axis=0)
    own = jnp.stack(ygather(rows))
    other = zexchange(own)
    halves = jnp.stack([own, other])
    full = both(k, halves, kswap(halves), 2)
    full = full.transpose(2, 0, 1, 3).reshape(4, 192, 2, D)
    full = jnp.concatenate([full, full], axis=0)
    full = lax.dynamic_slice_in_dim(full, y, 4, axis=0)
    return full.transpose(0, 2, 1, 3).reshape(D, D)


def fetch_gate_up(weight, x, k, y):
    rows = lax.dynamic_slice(weight, (k, x * 96, 0), (1, 96, 3456))[0]
    blocks = jnp.stack([rows[:, s : s + FB] for s in FSTARTS])
    part = jnp.stack(yexchange(lambda j: pick(blocks, (y + j) % 4)))
    own = lax.all_gather(part, "x")
    other = zexchange(own)
    result = []
    for half in (own, other):
        theirs = kswap(half)
        result.append([v.transpose(1, 0, 2, 3).reshape(D, FB) for v in (half, theirs)])
    return result


def fetch_down(weight, x, k, y):
    blocks = jnp.stack([weight[s : s + FB] for s in FSTARTS])
    blocks = blocks.reshape(4, 8, 112, 384)
    blocks = lax.dynamic_index_in_dim(blocks, x * 2 + k, 1, keepdims=False)
    part = jnp.stack(yexchange(lambda j: pick(blocks, (y + j) % 4)))
    own = lax.all_gather(part, "x")
    other = zexchange(own)
    keep = (y < 3) | (jnp.arange(FB) >= 128)
    result = []
    for half in (own, other):
        full = both(k, half[:, :, None], kswap(half)[:, :, None], 2)
        full = full.transpose(0, 2, 3, 1, 4).reshape(FB, D)
        result.append(jnp.where(keep[:, None], full, 0))
    return result


def sum_over_x(pieces_of, x):
    got = [pieces_of(x).astype(f32)]
    for d in (2, 1, 3):
        got.append(xshift(pieces_of((x + d) % 4).astype(bf16), d).astype(f32))
    return got[0] + got[1] + got[2] + got[3]


def sum_over_z(own, other, zh, zl):
    z = 2 * zh + zl
    total = pick(own, zh).astype(f32)
    total = total + zshift(pick(own, 1 - zh).astype(bf16), 2).astype(f32)
    for d in (1, 3):
        total = total + zshift(pick(other, ((z + d) % 4) // 2).astype(bf16), d).astype(f32)
    return total


def to_columns(blocks, y):
    got = jnp.stack(yexchange(lambda j: blocks[j].astype(bf16)))
    return [pick(got, (b - y) % 4) for b in range(4)]


def reduce_gate_up(mine, theirs, zh, x, k, zl, y):
    total = mine + kswap(theirs.astype(bf16)).astype(f32)
    total = total.reshape(4, 4, 96, 2 * FB)
    total = sum_over_x(lambda i: lax.dynamic_index_in_dim(total, i, 1, keepdims=False), x)
    total = total.reshape(4, 2, 48, 2 * FB).swapaxes(0, 1)
    total = sum_over_z(total[..., :FB], total[..., FB:], zh, zl)
    cols = to_columns(total, y)
    part = jnp.concatenate(cols[:3] + [cols[3][:, 128:]], axis=1)
    full = lax.all_gather(part, ("k", "x", "zh"), axis=0, tiled=True)
    return full.reshape(2, 384, 3456).astype(f32)


def reduce_rows(own, other, zh, x, k, zl, y):
    rows = own.shape[0] // 16
    both_r = jnp.stack([own, other]).reshape(2, 2, 8 * rows, D)
    total = lax.dynamic_index_in_dim(both_r, k, 1, keepdims=False) + kswap(
        lax.dynamic_index_in_dim(both_r, 1 - k, 1, keepdims=False).astype(bf16)
    ).astype(f32)
    total = total.reshape(2, 4, 2 * rows, D)
    total = sum_over_x(lambda i: lax.dynamic_index_in_dim(total, i, 1, keepdims=False), x)
    total = total.reshape(2, 2, rows, D)
    total = sum_over_z(total[0], total[1], zh, zl)
    cols = to_columns([total[:, 384 * j : 384 * j + 384] for j in range(4)], y)
    full = lax.all_gather(jnp.stack(cols), ("k", "x", "zh"))
    full = full.transpose(1, 0, 2, 3).reshape(4, 16 * rows, 384)
    return full.astype(f32)


def reduce_in(own, other, zh, x, k, zl, y):
    both_r = jnp.stack([own, other]).reshape(2, 4, 2, 192, 576)
    total = lax.dynamic_index_in_dim(both_r, k, 2, keepdims=False) + kswap(
        lax.dynamic_index_in_dim(both_r, 1 - k, 2, keepdims=False).astype(bf16)
    ).astype(f32)
    total = total.reshape(2, 4, 4, 48, 576)
    total = sum_over_x(lambda i: lax.dynamic_index_in_dim(total, i, 2, keepdims=False), x)
    total = total.reshape(2, 4, 2, 24, 576).transpose(0, 2, 1, 3, 4)
    total = sum_over_z(total[0], total[1], zh, zl)
    cols = to_columns(total, y)
    part = jnp.stack(cols, axis=1)
    part = part.reshape(24, 4, 3, 192).transpose(2, 0, 1, 3).reshape(3, 24, 768)
    full = lax.all_gather(part, ("k", "x", "zh"))
    return full.transpose(1, 0, 2, 3).reshape(3, 384, 768).astype(f32)


def row_sum(v):
    return jnp.sum(v, axis=1, keepdims=True)


def body(
    block_in,
    norm_gain,
    in_weight,
    conv_weight,
    out_weight,
    ffn_gain,
    gate_up_weight,
    down_weight,
    out_grad,
):
    zh = lax.axis_index("zh")
    x = lax.axis_index("x")
    k = lax.axis_index("k")
    zl = lax.axis_index("zl")
    y = lax.axis_index("y")

    sent = jnp.concatenate(
        [block_in, norm_gain[None], ffn_gain[None], jnp.zeros((14, 384), bf16)], axis=0
    )
    gathered = jnp.concatenate(ygather(sent), axis=1)
    tokens = gathered[:512]
    gain_one = gathered[512].astype(f32)
    gain_two = gathered[513].astype(f32)
    tail = lax.ppermute(tokens[496:], "zl", [(0, 1)])
    taps_other = lax.ppermute(conv_weight, "zl", [(0, 1), (1, 0)])

    w_in = fetch_in(in_weight, k, y)
    w_out = fetch_out(out_weight, k, y)
    w_gate_up = fetch_gate_up(gate_up_weight, x, k, y)
    w_down = fetch_down(down_weight, x, k, y)

    def norm_one(values):
        wide = values.astype(f32)
        inv = lax.rsqrt(row_sum(wide * wide) / D + EPSILON)
        hat = wide * inv
        return inv, hat, (hat * gain_one).astype(bf16)

    inv_one, hat_one, normed_one = norm_one(tokens)
    _, _, normed_tail = norm_one(tail)

    parts = []
    acts = []
    taps_both = [conv_weight.astype(f32), taps_other.astype(f32)]
    for r in range(2):
        proj = dot(normed_one, w_in[r])
        proj_tail = dot(normed_tail, w_in[r])
        b_part, c_part, x_part = (proj[:, 192 * i : 192 * i + 192] for i in range(3))
        before = proj_tail[8:, :192] * proj_tail[8:, 384:]
        mixed = jnp.concatenate([before, b_part * x_part], axis=0)
        taps = taps_both[r]
        conv = (
            taps[0] * mixed[8:520] + taps[1] * mixed[7:519] + taps[2] * mixed[6:518]
        )
        acts.append((c_part * conv).astype(bf16))
        parts.append((b_part, c_part, x_part, mixed, conv))

    act = jnp.concatenate(acts, axis=1)
    act_all = jnp.concatenate(ygather(act), axis=1)
    stream = tokens.astype(f32) + dot(act_all, w_out)
    inv_two = lax.rsqrt(row_sum(stream * stream) / D + EPSILON)
    hat_two = stream * inv_two
    normed_two = (hat_two * gain_two).astype(bf16)

    grads_all = jnp.concatenate(ygather(out_grad), axis=1)

    hidden = []
    back = []
    for r in range(2):
        first = dot(normed_two, w_gate_up[r][0])
        second = dot(normed_two, w_gate_up[r][1])
        gate = jnp.where(k == 0, first, second)
        up = jnp.where(k == 0, second, first)
        sig = jax.nn.sigmoid(gate)
        silu = gate * sig
        hidden.append((silu * up).astype(bf16))
        hidden_grad = dot_t(grads_all, w_down[r])
        gate_back = (hidden_grad * up * sig * (1.0 + gate * (1.0 - sig))).astype(bf16)
        up_back = (hidden_grad * silu).astype(bf16)
        back.append(
            (jnp.where(k == 0, gate_back, up_back), jnp.where(k == 0, up_back, gate_back))
        )

    hidden_all = jnp.concatenate(hidden, axis=1)
    down_all = jnp.concatenate(w_down, axis=0)
    out_parts = dot(hidden_all, down_all)
    out_sum = yreduce([out_parts[:, 384 * j : 384 * j + 384] for j in range(4)])
    block_out = (stream[:, :384] + out_sum).astype(bf16)

    back_mine = jnp.concatenate([back[0][0], back[1][0]], axis=1)
    back_theirs = jnp.concatenate([back[0][1], back[1][1]], axis=1)
    back_all = jnp.concatenate([back_mine, back_theirs], axis=1)
    w_back = jnp.concatenate(
        [w_gate_up[0][0], w_gate_up[1][0], w_gate_up[0][1], w_gate_up[1][1]], axis=1
    )
    two_parts = [
        dot_t(back_all, w_back[384 * j : 384 * j + 384]) for j in range(4)
    ]
    two_grad = yreduce(two_parts)
    two_all = ygather(two_grad.astype(bf16))
    two_all = jnp.concatenate(two_all, axis=1).astype(f32)

    down_grad = t_dot(hidden_all, grads_all)
    down_grad = reduce_rows(down_grad[:FB], down_grad[FB:], zh, x, k, zl, y)
    down_grad = jnp.concatenate(
        [down_grad[0], down_grad[1], down_grad[2], down_grad[3][128:]], axis=0
    )
    gate_up_grad = reduce_gate_up(
        t_dot(normed_two, back_mine), t_dot(normed_two, back_theirs), zh, x, k, zl, y
    )

    weighted_two = gain_two * two_all
    mean_two = row_sum(weighted_two * hat_two) / D
    stream_grad = grads_all.astype(f32) + inv_two * (weighted_two - hat_two * mean_two)
    stream_back = stream_grad.astype(bf16)
    own_weighted = gain_two[:384] * two_grad
    own_stream_grad = out_grad.astype(f32) + inv_two * (
        own_weighted - hat_two[:, :384] * mean_two
    )
    gain_two_part = jnp.sum(two_grad * hat_two[:, :384], axis=0)

    mixer_grad = dot_t(stream_back, w_out[:384])
    out_weight_grad = t_dot(act, stream_back)
    conv_parts = []
    proj_back = []
    grads = [mixer_grad[:, 192 * r : 192 * r + 192] for r in range(2)]
    conv_backs = [grads[r] * parts[r][1] for r in range(2)]
    after_both = lax.ppermute(
        jnp.concatenate([conv_backs[1][:8], conv_backs[0][:8]], axis=1), "zl", [(1, 0)]
    )
    for r in range(2):
        b_part, c_part, x_part, mixed, conv = parts[r]
        taps = taps_both[r]
        grad = grads[r]
        conv_back = conv_backs[r]
        after = after_both[:, 192 * r : 192 * r + 192]
        longer = jnp.concatenate([conv_back, after], axis=0)
        mixed_grad = (
            taps[0] * conv_back + taps[1] * longer[1:513] + taps[2] * longer[2:514]
        )
        conv_parts.append(
            jnp.stack(
                [jnp.sum(conv_back * mixed[8 - lag : 520 - lag], axis=0) for lag in range(3)]
            )
        )
        proj_back.append(
            jnp.concatenate([mixed_grad * x_part, grad * conv, mixed_grad * b_part], axis=1).astype(
                bf16
            )
        )
    proj_all = jnp.concatenate(proj_back, axis=1)
    w_in_all = jnp.concatenate(w_in, axis=1)
    one_part = dot_t(proj_all, w_in_all)
    inner_one = lax.psum(jnp.sum(one_part * gain_one * hat_one, axis=1), "y")
    one_grad = yreduce([one_part[:, 384 * j : 384 * j + 384] for j in range(4)])
    in_own = t_dot(normed_one, proj_back[0])
    in_other = t_dot(normed_one, proj_back[1])
    in_weight_grad = reduce_in(in_own, in_other, zh, x, k, zl, y)
    out_weight_grad = reduce_rows(
        out_weight_grad[:192], out_weight_grad[192:], zh, x, k, zl, y
    ).reshape(768, 384)

    own_hat = hat_one[:, :384]
    gain_one_part = jnp.sum(one_grad * own_hat, axis=0)
    in_grad = own_stream_grad + inv_one * (
        gain_one[:384] * one_grad - own_hat * (inner_one / D)[:, None]
    )
    in_grad = in_grad.astype(bf16)

    conv_other = zshift_pair(conv_parts[1])
    small = jnp.concatenate(
        [
            (conv_parts[0] + conv_other).reshape(-1),
        ]
    )
    conv_grad = lax.psum(small, ("zh", "x", "k")).reshape(3, 192)
    gains = lax.psum(jnp.stack([gain_one_part, gain_two_part]), ("zh", "x", "k", "zl"))
    return (
        block_out,
        in_grad,
        gains[0],
        in_weight_grad,
        conv_grad,
        out_weight_grad,
        gains[1],
        gate_up_grad,
        down_grad,
    )


def zshift_pair(v):
    return lax.ppermute(v, "zl", [(0, 1), (1, 0)])


def solution(mesh):
    devices = mesh.devices.reshape(2, 4, 2, 2, 4)
    grid = Mesh(devices, ("zh", "x", "k", "zl", "y"))
    tokens = P(("zh", "x", "k", "zl"), "y")
    first = P(None, "y", "zl")
    second = P("zl", "y")
    in_specs = (
        tokens,
        P("y"),
        first,
        P(None, ("zl", "y")),
        second,
        P("y"),
        first,
        second,
        tokens,
    )
    out_specs = (
        tokens,
        tokens,
        P("y"),
        first,
        P(None, ("zl", "y")),
        second,
        P("y"),
        first,
        second,
    )
    return jax.shard_map(body, mesh=grid, in_specs=in_specs, out_specs=out_specs, check_vma=False)
```

time: 1670 us -> 833 us (0.50)
  waiting for transfers between devices: 1250 us -> 280 us
  starting transfers between devices: 1.18 us -> 125 us
  other arithmetic: 27.7 us -> 91.9 us
  local copies, waits for them, and re-layouts: 148 us -> 85.8 us
  blocking collectives: 122 us -> 154 us
  matrix products: 95.8 us -> 68.9 us
    unnamed x17 -> x5, waiting for transfers between devices: 707 us -> 0.08 us
    ppermute x0 -> x91, waiting for transfers between devices: none -> 280 us  [the longest x12 113 us: xshift(): return lax.ppermute(v, 'x', [(i, (i + d) % 4) for i in range(4)])]
    all_gather x4 -> x5, waiting for transfers between devices: 278 us -> 0.01 us  [the longest x1 0.01 us: fetch_gate_up(): own = lax.all_gather(part, 'x')]
    psum x1 -> x0, waiting for transfers between devices: 210 us -> none  [body(): lax.psum((in_weight_grad, kernel_grad, out_weight_grad, gate_up_grad, dow...]
    ppermute x0 -> x91, starting transfers between devices: none -> 125 us  [the longest x45 62 us: yshift(): return lax.ppermute(v, 'y', [(i, (i + d) % 4) for i in range(4)])]
    reduce_scatter x4 -> x0, waiting for transfers between devices: 58.6 us -> none  [the longest x2 29.8 us: back_in(): lax.psum_scatter(partial_sum, 'row', scatter_dimension=0, tiled=True)]
    unnamed x60 -> x165, local copies, waits for them, and re-layouts: 79.8 us -> 28.2 us
    psum x6 -> x3, blocking collectives: 84.2 us -> 117 us  [the longest x1 62.7 us: body(): lax.psum(jnp.stack([gain_one_part, gain_two_part]), ('zh', 'x', 'k', 'zl'))]
  transfers between devices with their start and end apart: 13 -> 96, of which waited for: 11 -> 48; matrix products, arithmetic and copies ran while one was open for 4% -> 23% of each run, Pallas kernels for 0% -> 0%
where the time goes in v1:
time: 833 us; the launch traced here: 822 us
  waiting for transfers between devices  280 us (34%)
  blocking collectives  154 us (18%)
  starting transfers between devices  125 us (15%)
  other arithmetic  91.9 us (11%)
  local copies, waits for them, and re-layouts  85.8 us (10%)
  matrix products  68.9 us (8%)
  between operations  16.1 us (2%)
    ppermute x12, waiting for transfers between devices, xshift(): return lax.ppermute(v, 'x', [(i, (i + d) % 4) for i in range(4)])  113 us
    ppermute x45, waiting for transfers between devices, yshift(): return lax.ppermute(v, 'y', [(i, (i + d) % 4) for i in range(4)])  109 us
    psum x1, blocking collectives, body(): lax.psum(jnp.stack([gain_one_part, gain_two_part]), ('zh', 'x', 'k', 'zl'))  62.7 us
    ppermute x45, starting transfers between devices, yshift(): return lax.ppermute(v, 'y', [(i, (i + d) % 4) for i in range(4)])  62 us
    ppermute x20, waiting for transfers between devices, zshift(): return lax.ppermute(v, ('zh', 'zl'), [(i, (i + d) % 4) for i in range(4)])  42.9 us
    all_gather x1, blocking collectives, reduce_rows(): full = lax.all_gather(jnp.stack(cols), ('k', 'x', 'zh'))  37.6 us
    psum x1, blocking collectives, body(): conv_grad = lax.psum(small, ('zh', 'x', 'k')).reshape(3, 192)  37.5 us
    ppermute x20, starting transfers between devices, zshift(): return lax.ppermute(v, ('zh', 'zl'), [(i, (i + d) % 4) for i in range(4)])  37.4 us
  transfers between devices with their start and end apart: 96, of which 48 were waited for; matrix products, arithmetic and copies ran while one was open for 23% of the time, Pallas kernels for 0%

profile of v1, /device:TPU:0, one launch (start us, length us, event | category | flops | bytes accessed | tf_op | source)
XLA Modules:
  0.0 821.8 jit_solution(17490342474266412575)
XLA Ops:
  35.2 9.1 %collective-permute-done.3 = bf16[3,192,192]{2,1,0:T(8,128)(2,1)S(1)} collective-permute-done((bf16[3,192,192]{2,1,0:T(8,128)(2,1)}, bf16[3,192,192]{2,1,0:T(8,128)(2,1)S(1)}, u32[]{:S(2)}, u32[]{:S(2)}) %collective-permute-start.3) | collective-permute-done | bytes 221216 | tf_op jit(solution)/shard_map/ppermute | solution.py:17
  60.0 5.4 collective-permute-done.16
  66.5 9.1 %collective-permute-done.14 = bf16[384,384]{1,0:T(8,128)(2,1)S(1)} collective-permute-done((bf16[384,384]{1,0:T(8,128)(2,1)}, bf16[384,384]{1,0:T(8,128)(2,1)S(1)}, u32[]{:S(2)}, u32[]{:S(2)}) %collective-permute-start.14) | collective-permute-done | bytes 294944 | tf_op jit(solution)/shard_map/ppermute | solution.py:17
  83.9 6.1 collective-permute-start.17
  96.0 7.5 collective-permute-done.9
  155.3 7.4 collective-permute-done.13
  168.9 5.8 copy.202
  174.7 8.8 %reshape.234 = bf16[4,192,2,1536]{3,1,0,2:T(8,128)(2,1)} reshape(bf16[768,2,4,384]{3,2,0,1:T(4,128)(2,1)} %copy.202) | data formatting | bytes 9437184 | tf_op jit(solution)/shard_map/reshape | solution.py:97
  215.2 16.5 %collective-permute-done.24 = bf16[2,4,96,896]{3,2,1,0:T(8,128)(2,1)S(1)} collective-permute-done((bf16[2,4,96,896]{3,2,1,0:T(8,128)(2,1)S(1)}, bf16[2,4,96,896]{3,2,1,0:T(8,128)(2,1)S(1)}, u32[]{:S(2)}, u32[]{:S(2)}) %collective-permute-start.24) | collective-permute-done | bytes 1376288 | tf_op jit(solution)/shard_map/ppermute | solution.py:25
  271.1 9.6 %collective-permute-done.42 = bf16[512,384]{1,0:T(8,128)(2,1)S(1)} collective-permute-done((bf16[512,384]{1,0:T(8,128)(2,1)S(1)}, bf16[512,384]{1,0:T(8,128)(2,1)S(1)}, u32[]{:S(2)}, u32[]{:S(2)}) %collective-permute-start.42) | collective-permute-done | bytes 393248 | tf_op jit(solution)/shard_map/ppermute | solution.py:17
  280.7 8.0 collective-permute-done.41
  296.3 8.2 collective-permute-done.45
  304.5 8.9 %collective-permute-done.44 = bf16[512,384]{1,0:T(8,128)(2,1)S(1)} collective-permute-done((bf16[512,384]{1,0:T(8,128)(2,1)S(1)}, bf16[512,384]{1,0:T(8,128)(2,1)S(1)}, u32[]{:S(2)}, u32[]{:S(2)}) %collective-permute-start.44) | collective-permute-done | bytes 393248 | tf_op jit(solution)/shard_map/ppermute | solution.py:17
  323.3 6.6 collective-permute-done.46
  343.7 5.8 fusion.70
  372.9 5.8 collective-permute-done.51
  378.7 10.2 %collective-permute-done.53 = bf16[2,4,48,576]{3,2,1,0:T(8,128)(2,1)S(1)} collective-permute-done((bf16[2,4,48,576]{3,2,1,0:T(8,128)(2,1)S(1)}, bf16[2,4,48,576]{3,2,1,0:T(8,128)(2,1)S(1)}, u32[]{:S(2)}, u32[]{:S(2)}) %collective-permute-start.53) | collective-permute-done | bytes 442400 | tf_op jit(solution)/shard_map/ppermute | solution.py:21
  419.9 15.3 %collective-permute-done.82 = bf16[2,112,1536]{2,1,0:T(8,128)(2,1)S(1)} collective-permute-done((bf16[2,112,1536]{2,1,0:T(8,128)(2,1)S(1)}, bf16[2,112,1536]{2,1,0:T(8,128)(2,1)S(1)}, u32[]{:S(2)}, u32[]{:S(2)}) %collective-permute-start.82) | collective-permute-done | bytes 688160 | tf_op jit(solution)/shard_map/ppermute | solution.py:21
  435.2 12.8 %collective-permute-done.83 = bf16[2,112,1536]{2,1,0:T(8,128)(2,1)S(1)} collective-permute-done((bf16[2,112,1536]{2,1,0:T(8,128)(2,1)S(1)}, bf16[2,112,1536]{2,1,0:T(8,128)(2,1)S(1)}, u32[]{:S(2)}, u32[]{:S(2)}) %collective-permute-start.83) | collective-permute-done | bytes 688160 | tf_op jit(solution)/shard_map/ppermute | solution.py:21
  469.0 5.6 convert_add_fusion
  480.2 31.5 %collective-permute-done.72 = bf16[4,96,1792]{2,1,0:T(8,128)(2,1)S(1)} collective-permute-done((bf16[4,96,1792]{2,1,0:T(8,128)(2,1)S(1)}, bf16[4,96,1792]{2,1,0:T(8,128)(2,1)S(1)}, u32[]{:S(2)}, u32[]{:S(2)}) %collective-permute-start.72) | collective-permute-done | bytes 1376288 | tf_op jit(solution)/shard_map/ppermute | solution.py:21
  511.6 33.6 %collective-permute-done.74 = bf16[4,96,1792]{2,1,0:T(8,128)(2,1)S(1)} collective-permute-done((bf16[4,96,1792]{2,1,0:T(8,128)(2,1)S(1)}, bf16[4,96,1792]{2,1,0:T(8,128)(2,1)S(1)}, u32[]{:S(2)}, u32[]{:S(2)}) %collective-permute-start.74) | collective-permute-done | bytes 1376288 | tf_op jit(solution)/shard_map/ppermute | solution.py:21
  551.1 7.7 collective-permute-done.75
  558.9 6.1 collective-permute-done.76
  574.6 5.3 fusion.180
  584.1 15.0 %collective-permute-done.34 = bf16[512,384]{1,0:T(8,128)(2,1)S(1)} collective-permute-done((bf16[512,384]{1,0:T(8,128)(2,1)S(1)}, bf16[512,384]{1,0:T(8,128)(2,1)S(1)}, u32[]{:S(2)}, u32[]{:S(2)}) %collective-permute-start.34) | collective-permute-done | bytes 393248 | tf_op jit(solution)/shard_map/ppermute | solution.py:17
  608.3 37.5 %psum.23 = f32[3,192]{1,0:T(4,128)} all-reduce(f32[3,192]{1,0:T(4,128)S(1)} %maximum_add_fusion), channel_id=1, replica_groups=mesh['zh'=2,'x'=4,'k'=2,'zl'=2,'y'=4] {'zh','x','k'}, use_global_device_ids=true, to_apply=%region_15.16 | all-reduce | flops 576 | bytes 4608 | tf_op jit(solution)/shard_map/psum | solution.py:376
  645.8 8.1 fusion.168
  657.7 16.4 %psum.21 = f32[512]{0:T(512)S(1)} all-reduce(f32[512]{0:T(512)S(1)} %get-tuple-element.69), channel_id=1, replica_groups=mesh['zh'=2,'x'=4,'k'=2,'zl'=2,'y'=4] {'y'}, use_global_device_ids=true, to_apply=%region_5.6 | all-reduce | flops 512 | bytes 4096 | tf_op jit(solution)/shard_map/psum | solution.py:354
  687.9 62.7 %psum.22 = f32[2,384]{1,0:T(2,128)S(1)} all-reduce(f32[2,384]{1,0:T(2,128)S(1)} %pad_maximum_fusion.35), channel_id=1, replica_groups=mesh['zh'=2,'x'=4,'k'=2,'zl'=2,'y'=4] {'zh','x','k','zl'}, use_global_device_ids=true, to_apply=%region_8.9 | all-reduce | flops 768 | bytes 6144 | tf_op jit(solution)/shard_map/psum | solution.py:377
  758.1 37.6 %all-gather.2 = bf16[64,12,384]{2,1,0:T(8,128)(2,1)S(1)} all-gather(bf16[4,12,384]{2,1,0:T(8,128)(2,1)S(1)} %pad_maximum_fusion.33), channel_id=4, replica_groups=mesh['zh'=2,'x'=4,'k'=2,'zl'=2,'y'=4] {'k','x','zh'}, dimensions={0}, use_global_device_ids=true | all-gather | bytes 626688 | tf_op jit(solution)/shard_map/all_gather | solution.py:176
  807.5 7.4 convert.77
  (532 shorter events, 364.2 us)
Async XLA Ops:
  7.2 130.2 %all-gather.16.cloned.1.call-start = ((), (), s32[]{:S(2)}) async-start(), calls=%async_computation.3 | async-start | bytes 1720320 | tf_op jit(solution)/shard_map/all_gather | solution.py:121
  7.2 26.6 %collective-permute-start.10 = (bf16[3,192]{1,0:T(4,128)(2,1)}, bf16[3,192]{1,0:T(4,128)(2,1)S(1)}, u32[]{:S(2)}, u32[]{:S(2)}) collective-permute-start(bf16[3,192]{1,0:T(4,128)(2,1)} %param.12), channel_id=1, source_target_pairs={{0,4},{4,0},{1,5},{5,1},{2,6},{6,2},{3,7},{7,3},{8,12},{12,8},{9,1... | collective-permute-start | bytes 3464 | tf_op jit(solution)/shard_map/ppermute | solution.py:226
  22.8 172.9 %all-gather.14.cloned.1.call-start = ((), (), s32[]{:S(2)}) async-start(), calls=%async_computation.2 | async-start | bytes 3440640 | tf_op jit(solution)/shard_map/all_gather | solution.py:107
  23.7 25.9 %collective-permute-start.22 = (bf16[96,896]{1,0:T(8,128)(2,1)}, bf16[96,896]{1,0:T(8,128)(2,1)S(1)}, u32[]{:S(2)}, u32[]{:S(2)}) collective-permute-start(bf16[96,896]{1,0:T(8,128)(2,1)} %get-tuple-element.109), channel_id=1, source_target_pairs={{0,1},{1,2},{2,3},{3,0},{4,5},{5,6},{6,7},{7,4},{8,9},{9,10},{10,1... | collective-permute-start | bytes 516104 | tf_op jit(solution)/shard_map/ppermute | solution.py:17
  24.3 28.2 %collective-permute-start.21 = (bf16[96,896]{1,0:T(8,128)(2,1)}, bf16[96,896]{1,0:T(8,128)(2,1)}, u32[]{:S(2)}, u32[]{:S(2)}) collective-permute-start(bf16[96,896]{1,0:T(8,128)(2,1)} %get-tuple-element.110), channel_id=1, source_target_pairs={{0,2},{1,3},{2,0},{3,1},{4,6},{5,7},{6,4},{7,5},{8,10},{9,11},{10,... | collective-permute-start | bytes 516104 | tf_op jit(solution)/shard_map/ppermute | solution.py:17
  49.7 25.9 %collective-permute-start.14 = (bf16[384,384]{1,0:T(8,128)(2,1)}, bf16[384,384]{1,0:T(8,128)(2,1)S(1)}, u32[]{:S(2)}, u32[]{:S(2)}) collective-permute-start(bf16[384,384]{1,0:T(8,128)(2,1)} %constant_dynamic-slice_fusion.13), channel_id=1, source_target_pairs={{0,3},{1,0},{2,1},{3,2},{4,7},{5,4},{6,5},{7,6},{8,11},{9,8},{10,9... | collective-permute-start | bytes 884744 | tf_op jit(solution)/shard_map/ppermute | solution.py:17
  52.5 25.1 %collective-permute-start.7 = (bf16[2,3,192,192]{3,2,1,0:T(8,128)(2,1)}, bf16[2,3,192,192]{3,2,1,0:T(8,128)(2,1)}, u32[]{:S(2)}, u32[]{:S(2)}) collective-permute-start(bf16[2,3,192,192]{3,2,1,0:T(8,128)(2,1)} %pad_maximum_fusion.15), channel_id=1, source_target_pairs={{0,68},{4,0},{64,4},{68,64},{1,69},{5,1},{65,5},{69,65},{2,70},{6,... | collective-permute-start | bytes 1327112 | tf_op jit(solution)/shard_map/ppermute | solution.py:25
  56.0 25.5 %collective-permute-start.6 = (bf16[2,3,192,192]{3,2,1,0:T(8,128)(2,1)}, bf16[2,3,192,192]{3,2,1,0:T(8,128)(2,1)}, u32[]{:S(2)}, u32[]{:S(2)}) collective-permute-start(bf16[2,3,192,192]{3,2,1,0:T(8,128)(2,1)} %pad_maximum_fusion.14), channel_id=1, source_target_pairs={{0,4},{4,64},{64,68},{68,0},{1,5},{5,65},{65,69},{69,1},{2,6},{6,6... | collective-permute-start | bytes 1327112 | tf_op jit(solution)/shard_map/ppermute | solution.py:25
  57.9 740.2 %all-gather.10.cloned.1.call-start = ((), (), s32[]{:S(2)}) async-start(), calls=%async_computation | async-start | bytes 1880064 | tf_op jit(solution)/shard_map/all_gather | solution.py:193
  59.5 79.4 %collective-permute-start.38 = (bf16[512,384]{1,0:T(8,128)(2,1)S(1)}, bf16[512,384]{1,0:T(8,128)(2,1)}, u32[]{:S(2)}, u32[]{:S(2)}) collective-permute-start(bf16[512,384]{1,0:T(8,128)(2,1)S(1)} %copy-done.42), channel_id=1, source_target_pairs={{0,2},{1,3},{2,0},{3,1},{4,6},{5,7},{6,4},{7,5},{8,10},{9,11},{10,... | collective-permute-start | bytes 1179656 | tf_op jit(solution)/shard_map/ppermute | solution.py:17
  83.4 24.2 %collective-permute-start.8 = (bf16[2,4,3,192,192]{4,3,2,1,0:T(8,128)(2,1)S(1)}, bf16[2,4,3,192,192]{4,3,2,1,0:T(8,128)(2,1)S(1)}, u32[]{:S(2)}, u32[]{:S(2)}) collective-permute-start(bf16[2,4,3,192,192]{4,3,2,1,0:T(8,128)(2,1)S(1)} %pad_maximum_fusion.4), channel_id=1, source_target_pairs={{0,8},{8,0},{1,9},{9,1},{2,10},{10,2},{3,11},{11,3},{4,12},{12,4},... | collective-permute-start | bytes 5308424 | tf_op jit(solution)/shard_map/ppermute | solution.py:29
  103.5 38.0 %collective-permute-start.37 = (bf16[512,384]{1,0:T(8,128)(2,1)S(1)}, bf16[512,384]{1,0:T(8,128)(2,1)}, u32[]{:S(2)}, u32[]{:S(2)}) collective-permute-start(bf16[512,384]{1,0:T(8,128)(2,1)S(1)} %copy-done.42), channel_id=1, source_target_pairs={{0,3},{1,0},{2,1},{3,2},{4,7},{5,4},{6,5},{7,6},{8,11},{9,8},{10,9... | collective-permute-start | bytes 1179656 | tf_op jit(solution)/shard_map/ppermute | solution.py:17
  103.7 39.8 %collective-permute-start.39 = (bf16[512,384]{1,0:T(8,128)(2,1)S(1)}, bf16[512,384]{1,0:T(8,128)(2,1)}, u32[]{:S(2)}, u32[]{:S(2)}) collective-permute-start(bf16[512,384]{1,0:T(8,128)(2,1)S(1)} %copy-done.42), channel_id=1, source_target_pairs={{0,1},{1,2},{2,3},{3,0},{4,5},{5,6},{6,7},{7,4},{8,9},{9,10},{10,1... | collective-permute-start | bytes 1179656 | tf_op jit(solution)/shard_map/ppermute | solution.py:17
  107.6 57.5 %collective-permute-start.19 = (bf16[2,4,384,384]{3,2,1,0:T(8,128)(2,1)}, bf16[2,4,384,384]{3,2,1,0:T(8,128)(2,1)}, u32[]{:S(2)}, u32[]{:S(2)}) collective-permute-start(bf16[2,4,384,384]{3,2,1,0:T(8,128)(2,1)} %pad_maximum_fusion.5), channel_id=1, source_target_pairs={{0,8},{8,0},{1,9},{9,1},{2,10},{10,2},{3,11},{11,3},{4,12},{12,4},... | collective-permute-start | bytes 7077896 | tf_op jit(solution)/shard_map/ppermute | solution.py:29
  155.2 49.5 %collective-permute-start.30 = (bf16[4,4,112,384]{3,2,1,0:T(8,128)(2,1)}, bf16[4,4,112,384]{3,2,1,0:T(8,128)(2,1)}, u32[]{:S(2)}, u32[]{:S(2)}) collective-permute-start(bf16[4,4,112,384]{3,2,1,0:T(8,128)(2,1)} %bitcast.65), channel_id=1, source_target_pairs={{0,8},{8,0},{1,9},{9,1},{2,10},{10,2},{3,11},{11,3},{4,12},{12,4},... | collective-permute-start | bytes 4128776 | tf_op jit(solution)/shard_map/ppermute | solution.py:29
  164.7 45.7 %collective-permute-start.33 = (bf16[4,4,112,384]{3,2,1,0:T(8,128)(2,1)}, bf16[4,4,112,384]{3,2,1,0:T(8,128)(2,1)}, u32[]{:S(2)}, u32[]{:S(2)}) collective-permute-start(bf16[4,4,112,384]{3,2,1,0:T(8,128)(2,1)} %constant_dynamic-update-slice_fusion.7), channel_id=1, source_target_pairs={{0,8},{8,0},{1,9},{9,1},{2,10},{10,2},{3,11},{11,3},{4,12},{12,4},... | collective-permute-start | bytes 4128776 | tf_op jit(solution)/shard_map/ppermute | solution.py:29
  197.8 33.8 %collective-permute-start.24 = (bf16[2,4,96,896]{3,2,1,0:T(8,128)(2,1)S(1)}, bf16[2,4,96,896]{3,2,1,0:T(8,128)(2,1)S(1)}, u32[]{:S(2)}, u32[]{:S(2)}) collective-permute-start(bf16[2,4,96,896]{3,2,1,0:T(8,128)(2,1)S(1)} %bitcast.470), channel_id=1, source_target_pairs={{0,4},{4,64},{64,68},{68,0},{1,5},{5,65},{65,69},{69,1},{2,6},{6,6... | collective-permute-start | bytes 4128776 | tf_op jit(solution)/shard_map/ppermute | solution.py:25
  198.3 37.1 %collective-permute-start.25 = (bf16[2,4,96,896]{3,2,1,0:T(8,128)(2,1)S(1)}, bf16[2,4,96,896]{3,2,1,0:T(8,128)(2,1)S(1)}, u32[]{:S(2)}, u32[]{:S(2)}) collective-permute-start(bf16[2,4,96,896]{3,2,1,0:T(8,128)(2,1)S(1)} %bitcast.469), channel_id=1, source_target_pairs={{0,68},{4,0},{64,4},{68,64},{1,69},{5,1},{65,5},{69,65},{2,70},{6,... | collective-permute-start | bytes 4128776 | tf_op jit(solution)/shard_map/ppermute | solution.py:25
  201.1 42.7 %collective-permute-start.23 = (bf16[4,4,96,896]{3,2,1,0:T(8,128)(2,1)S(1)}, bf16[4,4,96,896]{3,2,1,0:T(8,128)(2,1)S(1)}, u32[]{:S(2)}, u32[]{:S(2)}) collective-permute-start(bf16[4,4,96,896]{3,2,1,0:T(8,128)(2,1)S(1)} %bitcast.415), channel_id=1, source_target_pairs={{0,8},{8,0},{1,9},{9,1},{2,10},{10,2},{3,11},{11,3},{4,12},{12,4},... | collective-permute-start | bytes 8257544 | tf_op jit(solution)/shard_map/ppermute | solution.py:29
  359.6 49.8 %collective-permute-start.81 = (bf16[2,448,1536]{2,1,0:T(8,128)(2,1)}, bf16[2,448,1536]{2,1,0:T(8,128)(2,1)}, u32[]{:S(2)}, u32[]{:S(2)}) collective-permute-start(bf16[2,448,1536]{2,1,0:T(8,128)(2,1)} %fusion.22), channel_id=1, source_target_pairs={{0,8},{8,0},{1,9},{9,1},{2,10},{10,2},{3,11},{11,3},{4,12},{12,4},... | collective-permute-start | bytes 8257544 | tf_op jit(solution)/shard_map/ppermute | solution.py:29
  372.9 96.0 %collective-permute-start.71 = (bf16[1536,1792]{1,0:T(8,128)(2,1)}, bf16[1536,1792]{1,0:T(8,128)(2,1)}, u32[]{:S(2)}, u32[]{:S(2)}) collective-permute-start(bf16[1536,1792]{1,0:T(8,128)(2,1)} %convolution_convert_fusion), channel_id=1, source_target_pairs={{0,8},{8,0},{1,9},{9,1},{2,10},{10,2},{3,11},{11,3},{4,12},{12,4},... | collective-permute-start | bytes 16515080 | tf_op jit(solution)/shard_map/ppermute | solution.py:29
  409.3 392.3 %all-gather.18.cloned.1.call-start = ((), (), s32[]{:S(2)}) async-start(), calls=%async_computation.4 | async-start | bytes 2924544 | tf_op jit(solution)/shard_map/all_gather | solution.py:176
  416.7 31.3 %collective-permute-start.83 = (bf16[2,112,1536]{2,1,0:T(8,128)(2,1)S(1)}, bf16[2,112,1536]{2,1,0:T(8,128)(2,1)S(1)}, u32[]{:S(2)}, u32[]{:S(2)}) collective-permute-start(bf16[2,112,1536]{2,1,0:T(8,128)(2,1)S(1)} %get-tuple-element.60), channel_id=1, source_target_pairs={{0,16},{16,32},{32,48},{48,0},{1,17},{17,33},{33,49},{49,1},{2,18}... | collective-permute-start | bytes 2064392 | tf_op jit(solution)/shard_map/ppermute | solution.py:21
  417.6 31.3 %collective-permute-start.84 = (bf16[2,112,1536]{2,1,0:T(8,128)(2,1)S(1)}, bf16[2,112,1536]{2,1,0:T(8,128)(2,1)S(1)}, u32[]{:S(2)}, u32[]{:S(2)}) collective-permute-start(bf16[2,112,1536]{2,1,0:T(8,128)(2,1)S(1)} %get-tuple-element.61), channel_id=1, source_target_pairs={{0,48},{16,0},{32,16},{48,32},{1,49},{17,1},{33,17},{49,33},{2,50}... | collective-permute-start | bytes 2064392 | tf_op jit(solution)/shard_map/ppermute | solution.py:21
  468.9 338.5 %all-gather.12.cloned.1.call-start = ((), (), s32[]{:S(2)}) async-start(), calls=%async_computation.1 | async-start | bytes 5640192 | tf_op jit(solution)/shard_map/all_gather | solution.py:161
  475.1 36.5 %collective-permute-start.72 = (bf16[4,96,1792]{2,1,0:T(8,128)(2,1)S(1)}, bf16[4,96,1792]{2,1,0:T(8,128)(2,1)S(1)}, u32[]{:S(2)}, u32[]{:S(2)}) collective-permute-start(bf16[4,96,1792]{2,1,0:T(8,128)(2,1)S(1)} %get-tuple-element.51), channel_id=1, source_target_pairs={{0,32},{16,48},{32,0},{48,16},{1,33},{17,49},{33,1},{49,17},{2,34}... | collective-permute-start | bytes 4128776 | tf_op jit(solution)/shard_map/ppermute | solution.py:21
  478.1 67.1 %collective-permute-start.74 = (bf16[4,96,1792]{2,1,0:T(8,128)(2,1)S(1)}, bf16[4,96,1792]{2,1,0:T(8,128)(2,1)S(1)}, u32[]{:S(2)}, u32[]{:S(2)}) collective-permute-start(bf16[4,96,1792]{2,1,0:T(8,128)(2,1)S(1)} %get-tuple-element.52), channel_id=1, source_target_pairs={{0,48},{16,0},{32,16},{48,32},{1,49},{17,1},{33,17},{49,33},{2,50}... | collective-permute-start | bytes 4128776 | tf_op jit(solution)/shard_map/ppermute | solution.py:21
  479.3 66.0 %collective-permute-start.73 = (bf16[4,96,1792]{2,1,0:T(8,128)(2,1)S(1)}, bf16[4,96,1792]{2,1,0:T(8,128)(2,1)S(1)}, u32[]{:S(2)}, u32[]{:S(2)}) collective-permute-start(bf16[4,96,1792]{2,1,0:T(8,128)(2,1)S(1)} %get-tuple-element.53), channel_id=1, source_target_pairs={{0,16},{16,32},{32,48},{48,0},{1,17},{17,33},{33,49},{49,1},{2,18}... | collective-permute-start | bytes 4128776 | tf_op jit(solution)/shard_map/ppermute | solution.py:21
  607.5 66.7 %collective-permute-start.61 = (bf16[2,96,1536]{2,1,0:T(8,128)(2,1)}, bf16[2,96,1536]{2,1,0:T(8,128)(2,1)S(1)}, u32[]{:S(2)}, u32[]{:S(2)}) collective-permute-start(bf16[2,96,1536]{2,1,0:T(8,128)(2,1)} %fusion.90), channel_id=1, source_target_pairs={{0,8},{8,0},{1,9},{9,1},{2,10},{10,2},{3,11},{11,3},{4,12},{12,4},... | collective-permute-start | bytes 1769480 | tf_op jit(solution)/shard_map/ppermute | solution.py:29
  683.1 67.5 %collective-permute-start.65 = (bf16[12,1536]{1,0:T(8,128)(2,1)S(1)}, bf16[12,1536]{1,0:T(8,128)(2,1)S(1)}, u32[]{:S(2)}, u32[]{:S(2)}) collective-permute-start(bf16[12,1536]{1,0:T(8,128)(2,1)S(1)} %fusion.144), channel_id=1, source_target_pairs={{0,64},{4,68},{64,0},{68,4},{1,65},{5,69},{65,1},{69,5},{2,66},{6,... | collective-permute-start | bytes 110600 | tf_op jit(solution)/shard_map/ppermute | solution.py:25
  684.6 66.0 %collective-permute-start.66 = (bf16[12,1536]{1,0:T(8,128)(2,1)S(1)}, bf16[12,1536]{1,0:T(8,128)(2,1)S(1)}, u32[]{:S(2)}, u32[]{:S(2)}) collective-permute-start(bf16[12,1536]{1,0:T(8,128)(2,1)S(1)} %get-tuple-element.146), channel_id=1, source_target_pairs={{0,4},{4,64},{64,68},{68,0},{1,5},{5,65},{65,69},{69,1},{2,6},{6,6... | collective-permute-start | bytes 110600 | tf_op jit(solution)/shard_map/ppermute | solution.py:25
  685.7 64.9 %collective-permute-start.67 = (bf16[12,1536]{1,0:T(8,128)(2,1)S(1)}, bf16[12,1536]{1,0:T(8,128)(2,1)S(1)}, u32[]{:S(2)}, u32[]{:S(2)}) collective-permute-start(bf16[12,1536]{1,0:T(8,128)(2,1)S(1)} %get-tuple-element.147), channel_id=1, source_target_pairs={{0,68},{4,0},{64,4},{68,64},{1,69},{5,1},{65,5},{69,65},{2,70},{6,... | collective-permute-start | bytes 110600 | tf_op jit(solution)/shard_map/ppermute | solution.py:25
  (142 other events, 1734.4 us)
Sparse Core Ops, SparseCore 0:
  22.9 26.4 all-gather.15
  58.0 39.1 all-gather.13
  409.5 52.2 all-gather.9
  469.0 74.0 all-gather.17
  574.7 58.9 all-gather.11

commit v2 on v0

v2 whole, which is shorter than its diff:
```python
import functools

import jax
import jax.numpy as jnp
from jax import lax
from jax.experimental import pallas as pl
from jax.experimental.pallas import tpu as pltpu
from jax.sharding import Mesh, PartitionSpec as P

D = 1536
LEN = 1024
EPSILON = 1e-05
FB = 896
FSTARTS = (0, 896, 1792, 2560)

bf16 = jnp.bfloat16
f32 = jnp.float32


def yshift(v, d):
    return lax.ppermute(v, "y", [(i, (i + d) % 4) for i in range(4)])


def xshift(v, d):
    return lax.ppermute(v, "x", [(i, (i + d) % 4) for i in range(4)])


def zshift(v, d):
    return lax.ppermute(v, ("zh", "zl"), [(i, (i + d) % 4) for i in range(4)])


def zswap(v):
    return lax.ppermute(v, "zl", [(0, 1), (1, 0)])


def kswap(v):
    return lax.ppermute(v, "k", [(0, 1), (1, 0)])


def ygather(v):
    two = yshift(v, 2)
    return [v, yshift(v, 3), two, yshift(v, 1)]


def yexchange(block_for):
    two = yshift(block_for(2), 2)
    one = yshift(block_for(1), 1)
    three = yshift(block_for(3), 3)
    return [block_for(0), three, two, one]


def yreduce(pieces):
    got = yexchange(lambda j: pieces[j].astype(bf16) if j else pieces[0])
    return got[0].astype(f32) + got[1].astype(f32) + got[2].astype(f32) + got[3].astype(f32)


def zexchange(v):
    half = v.shape[0] // 2
    up = zshift(v[:half], 1)
    down = zshift(v[half:], 3)
    return jnp.concatenate([up, down], axis=0)


def pick(stacked, index):
    return lax.dynamic_index_in_dim(stacked, index, 0, keepdims=False)


def dot(a, b):
    return jnp.dot(a, b, preferred_element_type=f32)


def dot_t(a, b):
    return lax.dot_general(a, b, (((1,), (1,)), ((), ())), preferred_element_type=f32)


def t_dot(a, b):
    return lax.dot_general(a, b, (((0,), (0,)), ((), ())), preferred_element_type=f32)


def after(v, *deps):
    for dep in deps:
        last = lax.slice(dep, [n - 1 for n in dep.shape], dep.shape).reshape(())
        v = v + (last * 0).astype(v.dtype)
    return v


def both(k, mine, other, axis):
    return jnp.where(
        k == 0,
        jnp.concatenate([mine, other], axis=axis),
        jnp.concatenate([other, mine], axis=axis),
    )


def to_owners(blocks, y):
    return jnp.stack(yexchange(lambda j: pick(blocks, (y + j) % 4)))


def pack_mixer(in_weight, out_weight, first):
    rows = lax.dynamic_slice_in_dim(in_weight, first, 48, axis=1)
    turned = lax.dynamic_slice_in_dim(out_weight.T, first, 48, axis=0)
    blocks = []
    for b in range(4):
        cols = slice(192 * b, 192 * b + 192)
        blocks.append(
            jnp.concatenate(
                [
                    rows[0, :, cols],
                    rows[1, :, cols],
                    rows[2, :, cols],
                    jnp.zeros((48, 64), bf16),
                    turned[:, cols],
                ],
                axis=1,
            )
        )
    return jnp.stack(blocks)


def pack_ffn(gate_up_weight, down_weight, first):
    rows = lax.dynamic_slice_in_dim(gate_up_weight, first, 48, axis=1)
    turned = lax.dynamic_slice_in_dim(down_weight.T, first, 48, axis=0)
    blocks = []
    for start in FSTARTS:
        cols = slice(start, start + FB)
        down = turned[:, cols]
        if start % FB:
            down = jnp.concatenate([jnp.zeros((48, 128), bf16), down[:, 128:]], axis=1)
        blocks.append(jnp.concatenate([rows[0, :, cols], rows[1, :, cols], down], axis=1))
    return jnp.stack(blocks)


def x_terms(pieces_of, x):
    got = [pieces_of(x)]
    for d in (2, 1, 3):
        got.append(xshift(pieces_of((x + d) % 4).astype(bf16), d))
    return got


def z_terms(own, other, zh, zl):
    z = 2 * zh + zl
    got = [pick(own, zh)]
    got.append(zshift(pick(own, 1 - zh).astype(bf16), 2))
    for d in (1, 3):
        got.append(zshift(pick(other, ((z + d) % 4) // 2).astype(bf16), d))
    return got


def zh_terms(v, axis, zh):
    mine = lax.dynamic_index_in_dim(v, zh, axis, keepdims=False)
    theirs = lax.dynamic_index_in_dim(v, 1 - zh, axis, keepdims=False).astype(bf16)
    return [mine, lax.ppermute(theirs, "zh", [(0, 1), (1, 0)])]


def total_of(terms):
    total = terms[0].astype(f32)
    for term in terms[1:]:
        total = total + term.astype(f32)
    return total


def to_columns(blocks, y):
    got = jnp.stack(yexchange(lambda j: blocks[j].astype(bf16)))
    return [pick(got, (b - y) % 4) for b in range(4)]


def gather_zh(part, zh):
    other = lax.ppermute(part, "zh", [(0, 1), (1, 0)])
    return jnp.where(zh == 0, jnp.stack([part, other]), jnp.stack([other, part]))


def split_k(v, k, axis):
    mine = lax.dynamic_index_in_dim(v, k, axis, keepdims=False)
    theirs = lax.dynamic_index_in_dim(v, 1 - k, axis, keepdims=False)
    return mine.astype(f32) + kswap(theirs.astype(bf16)).astype(f32)


TILES = ((0, 256), (256, 256), (512, 256), (768, 128))
CHEAP = pl.CostEstimate(flops=1_000_000, bytes_accessed=1_000_000, transcendentals=0)
WIDE = pltpu.CompilerParams(
    dimension_semantics=("arbitrary",), vmem_limit_bytes=50 * 1024 * 1024
)


def load_mixer(source, rows, sems):
    copies = []
    for r in range(2):
        for b in range(4):
            for e in range(8):
                first = 384 * b + 48 * e
                copies.append(
                    pltpu.make_async_copy(
                        source.at[e, r, b],
                        rows.at[r, pl.ds(first, 48)],
                        sems.at[32 * r + 8 * b + e],
                    )
                )
    for copy in copies:
        copy.start()
    for copy in copies:
        copy.wait()


def mixer_kernel(
    half_ref, x0, x1, x2, x3, swap_ref, taps_ref, w_hbm, n_ref, inv_ref, proj0, proj1,
    conv0, conv1, before0, before1, act0, act1, wo0, wo1, p0, p1, p2, p3, w_ref, sems,
):
    load_mixer(w_hbm, w_ref, sems)
    xs = (x0, x1, x2, x3)
    gain = jnp.concatenate([ref[512:528, :] for ref in xs], axis=1)[:1].astype(f32)
    for i in range(4):
        rows = pl.ds(128 * i, 128)
        wide = jnp.concatenate([ref[rows, :] for ref in xs], axis=1).astype(f32)
        inv = lax.rsqrt(jnp.sum(wide * wide, axis=1, keepdims=True) / D + EPSILON)
        inv_ref[rows, :] = inv
        n_ref[rows, :] = (wide * inv * gain).astype(bf16)
    tail = swap_ref[:16, :].astype(f32)
    tail = jnp.where(half_ref[0] == 1, tail, 0.0)
    inv = lax.rsqrt(jnp.sum(tail * tail, axis=1, keepdims=True) / D + EPSILON)
    n_tail = (tail * inv * gain).astype(bf16)
    own_taps = taps_ref[...].astype(f32)
    other_taps = swap_ref[16:32, :192].astype(f32)
    line = lax.broadcasted_iota(jnp.int32, (512, 192), 0)
    acts = (act0, act1)
    for r, taps in ((0, own_taps), (1, other_taps)):
        proj_ref = (proj0, proj1)[r]
        proj_ref[...] = dot(n_ref[...], w_ref[r, :, :576])
        proj_tail = dot(n_tail, w_ref[r, :, :576])
        before = proj_tail[8:, :192] * proj_tail[8:, 384:]
        (before0, before1)[r][...] = before
        mixed = proj_ref[:, :192] * proj_ref[:, 384:576]
        one = jnp.where(line == 0, before[7:8], pltpu.roll(mixed, 1, 0))
        two = jnp.where(
            line == 0, before[6:7], jnp.where(line == 1, before[7:8], pltpu.roll(mixed, 2, 0))
        )
        conv = taps[0:1] * mixed + taps[1:2] * one + taps[2:3] * two
        (conv0, conv1)[r][...] = conv
        acts[r][...] = (proj_ref[:, 192:384] * conv).astype(bf16)
        (wo0, wo1)[r][...] = w_ref[r, :, 640:]
    for j, ref in enumerate((p0, p1, p2, p3)):
        rows = pl.ds(384 * j, 384)
        part = dot_t(act0[...], wo0[rows, :]) + dot_t(act1[...], wo1[rows, :])
        ref[...] = part.astype(ref.dtype)


def mixer_call(half, pieces, swapped, taps, weight, *deps):
    whole = pl.BlockSpec(memory_space=pltpu.VMEM)

    def kernel(*refs):
        mixer_kernel(*refs[:8], *refs[8 + len(deps) :])

    def shape(*dims, kind=f32):
        return jax.ShapeDtypeStruct(dims, kind)

    return pl.pallas_call(
        kernel,
        in_specs=[pl.BlockSpec(memory_space=pltpu.SMEM)]
        + [whole] * 6
        + [pl.BlockSpec(memory_space=pl.ANY)] * (1 + len(deps)),
        out_specs=[whole] * 16,
        out_shape=[shape(512, D, kind=bf16), shape(512, 1)]
        + [shape(512, 576)] * 2
        + [shape(512, 192)] * 2
        + [shape(8, 192)] * 2
        + [shape(512, 192, kind=bf16)] * 2
        + [shape(D, 192, kind=bf16)] * 2
        + [shape(512, 384)]
        + [shape(512, 384, kind=bf16)] * 3,
        scratch_shapes=[pltpu.VMEM((2, D, 832), bf16), pltpu.SemaphoreType.DMA((64,))],
        compiler_params=pltpu.CompilerParams(vmem_limit_bytes=50 * 1024 * 1024),
        cost_estimate=CHEAP,
        name="mixer",
    )(half, *pieces, swapped, taps, weight, *deps)


def stream_kernel(*refs):
    q_refs, s_refs, g_refs = refs[:4], refs[4:8], refs[8:12]
    own_ref, gain_ref, wo0, wo1, proj0, proj1 = refs[12:18]
    sb_ref, grad0, grad1, halo_ref, sg_ref, gain_out = refs[-6:]
    gain = gain_ref[...]
    sums = jnp.zeros((1, 384), f32)
    for i in range(4):
        rows = pl.ds(128 * i, 128)
        stream = jnp.concatenate([ref[rows, :] for ref in s_refs], axis=1).astype(f32)
        inv = lax.rsqrt(jnp.sum(stream * stream, axis=1, keepdims=True) / D + EPSILON)
        hat = stream * inv
        weighted = gain * jnp.concatenate([ref[rows, :] for ref in q_refs], axis=1).astype(f32)
        mean = jnp.sum(weighted * hat, axis=1, keepdims=True) / D
        grads = jnp.concatenate([ref[rows, :] for ref in g_refs], axis=1).astype(f32)
        sb_ref[rows, :] = (grads + inv * (weighted - hat * mean)).astype(bf16)
        own = own_ref[rows, :]
        own_hat = hat[:, :384]
        sg_ref[rows, :] = grads[:, :384] + inv * (gain[:, :384] * own - own_hat * mean)
        sums = sums + jnp.sum(own * own_hat, axis=0, keepdims=True)
    gain_out[...] = sums
    for r in range(2):
        grad_ref = (grad0, grad1)[r]
        grad_ref[...] = dot(sb_ref[...], (wo0, wo1)[r][...])
        halo_ref[1 - r] = grad_ref[:8, :] * (proj0, proj1)[r][:8, 192:384]


def stream_call(two_all, streams, grads, two_grad, gain, w_out, proj, *deps):
    whole = pl.BlockSpec(memory_space=pltpu.VMEM)
    return pl.pallas_call(
        stream_kernel,
        in_specs=[whole] * 18 + [pl.BlockSpec(memory_space=pl.ANY)] * len(deps),
        out_specs=[whole] * 6,
        out_shape=[
            jax.ShapeDtypeStruct((512, D), bf16),
            jax.ShapeDtypeStruct((512, 192), f32),
            jax.ShapeDtypeStruct((512, 192), f32),
            jax.ShapeDtypeStruct((2, 8, 192), f32),
            jax.ShapeDtypeStruct((512, 384), f32),
            jax.ShapeDtypeStruct((1, 384), f32),
        ],
        compiler_params=pltpu.CompilerParams(vmem_limit_bytes=50 * 1024 * 1024),
        cost_estimate=CHEAP,
        name="stream",
    )(*two_all, *streams, *grads, two_grad, gain, *w_out, *proj, *deps)


def back_kernel(
    x0, x1, x2, x3, grad0, grad1, proj0, proj1, conv0, conv1, before0, before1, halo_ref,
    swap_ref, taps_ref, w_hbm, pb0, pb1, p0, p1, p2, p3, gain_out, taps0, taps1, w_ref, sems,
):
    load_mixer(w_hbm, w_ref, sems)
    xs = (x0, x1, x2, x3)
    own_taps = taps_ref[...].astype(f32)
    other_taps = swap_ref[16:32, :192].astype(f32)
    line = lax.broadcasted_iota(jnp.int32, (512, 192), 0)
    for r, taps in ((0, own_taps), (1, other_taps)):
        grad_ref, proj_ref = (grad0, grad1)[r], (proj0, proj1)[r]
        before, halo = (before0, before1)[r][...], halo_ref[r]
        grad = grad_ref[...]
        b_part = proj_ref[:, :192]
        x_part = proj_ref[:, 384:576]
        conv_back = grad * proj_ref[:, 192:384]
        one = jnp.where(line == 511, halo[0:1], pltpu.roll(conv_back, 511, 0))
        two = jnp.where(
            line == 510,
            halo[0:1],
            jnp.where(line == 511, halo[1:2], pltpu.roll(conv_back, 510, 0)),
        )
        mixed_grad = taps[0:1] * conv_back + taps[1:2] * one + taps[2:3] * two
        (pb0, pb1)[r][...] = jnp.concatenate(
            [
                mixed_grad * x_part,
                grad * (conv0, conv1)[r][...],
                mixed_grad * b_part,
                jnp.zeros((512, 64), f32),
            ],
            axis=1,
        ).astype(bf16)
        mixed = b_part * x_part
        lag_one = jnp.where(line == 0, before[7:8], pltpu.roll(mixed, 1, 0))
        lag_two = jnp.where(
            line == 0, before[6:7], jnp.where(line == 1, before[7:8], pltpu.roll(mixed, 2, 0))
        )
        (taps0, taps1)[r][...] = jnp.concatenate(
            [
                jnp.sum(conv_back * lagged, axis=0, keepdims=True)
                for lagged in (mixed, lag_one, lag_two)
            ],
            axis=0,
        )
    gain = jnp.concatenate([ref[512:528, :] for ref in xs], axis=1)[:1].astype(f32)
    ones = jnp.ones((8, D), bf16)
    inner = []
    sums = jnp.zeros((1, D), f32)
    for i in range(4):
        rows = pl.ds(128 * i, 128)
        part = dot_t(pb0[rows, :576], w_ref[0, :, :576]) + dot_t(
            pb1[rows, :576], w_ref[1, :, :576]
        )
        for j, ref in enumerate((p0, p1, p2, p3)):
            ref[rows, :] = part[:, 384 * j : 384 * j + 384].astype(ref.dtype)
        wide = jnp.concatenate([ref[rows, :] for ref in xs], axis=1).astype(f32)
        inv = lax.rsqrt(jnp.sum(wide * wide, axis=1, keepdims=True) / D + EPSILON)
        product = part * (wide * inv)
        sums = sums + jnp.sum(product, axis=0, keepdims=True)
        product = product * gain
        high = product.astype(bf16)
        low = (product - high.astype(f32)).astype(bf16)
        inner.append(dot_t(ones, high) + dot_t(ones, low))
    gain_out[...] = sums
    empty = jnp.zeros((1, 256), f32)
    rows = []
    total = jnp.concatenate(inner, axis=1)[:1]
    high = total.astype(bf16).astype(f32)
    for term in (high, total - high):
        rows.append(term[:, :384])
        rows.append(jnp.concatenate([term[:, 384:], empty], axis=1))
    inner_rows = jnp.concatenate(rows + [jnp.zeros((12, 384), f32)], axis=0)
    for ref in (p0, p1, p2, p3):
        ref[512:528, :] = inner_rows.astype(ref.dtype)


def back_call(pieces, grads, proj, conv, before, halo, swapped, taps, weight, *deps):
    whole = pl.BlockSpec(memory_space=pltpu.VMEM)

    def kernel(*refs):
        back_kernel(*refs[:16], *refs[16 + len(deps) :])

    return pl.pallas_call(
        kernel,
        in_specs=[whole] * 15 + [pl.BlockSpec(memory_space=pl.ANY)] * (1 + len(deps)),
        out_specs=[whole] * 9,
        out_shape=[jax.ShapeDtypeStruct((512, 640), bf16)] * 2
        + [jax.ShapeDtypeStruct((528, 384), f32)]
        + [jax.ShapeDtypeStruct((528, 384), bf16)] * 3
        + [jax.ShapeDtypeStruct((1, D), f32)]
        + [jax.ShapeDtypeStruct((3, 192), f32)] * 2,
        scratch_shapes=[pltpu.VMEM((2, D, 832), bf16), pltpu.SemaphoreType.DMA((64,))],
        compiler_params=pltpu.CompilerParams(vmem_limit_bytes=50 * 1024 * 1024),
        cost_estimate=CHEAP,
        name="back",
    )(*pieces, *grads, *proj, *conv, *before, halo, swapped, taps, weight, *deps)


def ffn_finish(full):
    def kernel(full_ref, gate_ref, down_ref):
        wide = full_ref[...].astype(f32)
        gate_ref[...] = wide[:, :, :48].reshape(2, 384, 384)
        down_ref[...] = wide[:, :, 48:].reshape(384, 384).T

    return pl.pallas_call(
        kernel,
        grid=(9,),
        in_specs=[pl.BlockSpec((8, 2, 72, 384), lambda i: (0, 0, 0, i))],
        out_specs=[
            pl.BlockSpec((2, 384, 384), lambda i: (0, 0, i)),
            pl.BlockSpec((384, 384), lambda i: (i, 0)),
        ],
        out_shape=[
            jax.ShapeDtypeStruct((2, 384, 3456), f32),
            jax.ShapeDtypeStruct((3456, 384), f32),
        ],
        compiler_params=pltpu.CompilerParams(vmem_limit_bytes=50 * 1024 * 1024),
        name="ffn_finish",
    )(full)


def mixer_finish(full, y):
    def kernel(y_ref, full_ref, in_ref, out_ref, own_ref, sum_ref):
        own = jnp.zeros((384, 128), f32)
        total = jnp.zeros((384, 128), f32)
        for b in range(4):
            block = full_ref[:, :, b].astype(f32).reshape(384, FB)
            cols = slice(192 * b, 192 * b + 192)
            for j in range(3):
                in_ref[j, :, cols] = block[:, 192 * j : 192 * j + 192]
            out_ref[cols, :] = block[:, 640:896].T[:192]
            small = block[:, 512:640]
            own = own + jnp.where(y_ref[0] == b, small, 0.0)
            total = total + small
        own_ref[...] = own
        sum_ref[...] = total

    whole = pl.BlockSpec(memory_space=pltpu.VMEM)
    return pl.pallas_call(
        kernel,
        in_specs=[pl.BlockSpec(memory_space=pltpu.SMEM), whole],
        out_specs=[whole] * 4,
        out_shape=[
            jax.ShapeDtypeStruct((3, 384, 768), f32),
            jax.ShapeDtypeStruct((768, 384), f32),
            jax.ShapeDtypeStruct((384, 128), f32),
            jax.ShapeDtypeStruct((384, 128), f32),
        ],
        compiler_params=pltpu.CompilerParams(vmem_limit_bytes=50 * 1024 * 1024),
        name="mixer_finish",
    )(y.astype(jnp.int32)[None], full)


def load_rows(source, rows, sems):
    copies = []
    for b in range(4):
        for e in range(8):
            first = 384 * b + 48 * e
            copies.append(
                pltpu.make_async_copy(
                    source.at[e, b], rows.at[pl.ds(first, 48)], sems.at[8 * b + e]
                )
            )
    for copy in copies:
        copy.start()
    for copy in copies:
        copy.wait()


def ffn_kernel(*refs):
    s_refs, g_refs = refs[:4], refs[4:8]
    gain_ref, w_hbm = refs[8:10]
    n_ref, h_ref, gb_ref, ub_ref = refs[-10:-6]
    p_refs = refs[-6:-2]
    w_ref, sems = refs[-2:]

    @pl.when(pl.program_id(0) == 0)
    def _():
        load_rows(w_hbm, w_ref, sems)

    stream = jnp.concatenate([ref[...] for ref in s_refs], axis=1).astype(f32)
    inv = lax.rsqrt(jnp.sum(stream * stream, axis=1, keepdims=True) / D + EPSILON)
    n_ref[...] = (stream * inv * gain_ref[...]).astype(bf16)
    grads = jnp.concatenate([ref[...] for ref in g_refs], axis=1)
    for first, size in TILES:
        cols = pl.ds(first, size)
        w_pair = jnp.concatenate(
            [w_ref[:, cols], w_ref[:, pl.ds(FB + first, size)]], axis=1
        )
        gate_up = dot(n_ref[...], w_pair)
        gate = gate_up[:, :size]
        up = gate_up[:, size:]
        sig = 1.0 / (1.0 + jnp.exp(-gate))
        silu = gate * sig
        h_ref[:, cols] = (silu * up).astype(bf16)
        hidden_grad = dot(grads, w_ref[:, pl.ds(2 * FB + first, size)])
        gb_ref[:, cols] = (
            hidden_grad * up * sig * (1.0 + gate * (1.0 - sig))
        ).astype(bf16)
        ub_ref[:, cols] = (hidden_grad * silu).astype(bf16)
    back = jnp.concatenate([gb_ref[...], ub_ref[...]], axis=1)
    parts = jnp.concatenate(
        [dot_t(back, w_ref[pl.ds(512 * i, 512), : 2 * FB]) for i in range(3)], axis=1
    )
    for j in range(4):
        p_refs[j][...] = parts[:, 384 * j : 384 * j + 384].astype(p_refs[j].dtype)


def ffn_call(streams, grads, gain, weight, *deps):
    narrow = pl.BlockSpec((256, 384), lambda i: (i, 0))
    middle = pl.BlockSpec((256, FB), lambda i: (i, 0))
    wide = pl.BlockSpec((256, D), lambda i: (i, 0))
    whole = pl.BlockSpec(memory_space=pl.ANY)
    return pl.pallas_call(
        ffn_kernel,
        grid=(2,),
        in_specs=[narrow] * 8
        + [pl.BlockSpec((1, D), lambda i: (0, 0)), whole]
        + [whole] * len(deps),
        out_specs=[wide] + [middle] * 3 + [narrow] * 4,
        out_shape=[jax.ShapeDtypeStruct((512, D), bf16)]
        + [jax.ShapeDtypeStruct((512, FB), bf16)] * 3
        + [jax.ShapeDtypeStruct((512, 384), f32)]
        + [jax.ShapeDtypeStruct((512, 384), bf16)] * 3,
        scratch_shapes=[pltpu.VMEM((D, 3 * FB), bf16), pltpu.SemaphoreType.DMA((32,))],
        compiler_params=WIDE,
        cost_estimate=pl.CostEstimate(
            flops=8_400_000_000, bytes_accessed=16_000_000, transcendentals=500_000
        ),
        name="ffn",
    )(*streams, *grads, gain, weight, *deps)


def block_kernel(place, h0_ref, h1_ref, w_ref, out_ref):
    hidden = jnp.where(pl.program_id(1) < 1, h0_ref[...], h1_ref[...])
    out_ref[0, 0] = dot_t(hidden, w_ref[...].reshape(384, FB)).astype(bf16)


def block_call(own, other, weight, y, *deps):
    def where(j, t, place):
        return ((place[0] + j) % 4, t, 0, 0)

    def kernel(place, h0_ref, h1_ref, w_ref, *rest):
        block_kernel(place, h0_ref, h1_ref, w_ref, rest[-1])

    grid_spec = pltpu.PrefetchScalarGridSpec(
        num_scalar_prefetch=1,
        grid=(4, 2),
        in_specs=[
            pl.BlockSpec((512, FB), lambda j, t, place: (0, 0)),
            pl.BlockSpec((512, FB), lambda j, t, place: (0, 0)),
            pl.BlockSpec((8, None, 48, FB), lambda j, t, place: (0, j, 0, 2)),
        ]
        + [pl.BlockSpec(memory_space=pl.ANY)] * len(deps),
        out_specs=pl.BlockSpec((1, 1, 512, 384), where),
    )
    return pl.pallas_call(
        kernel,
        grid_spec=grid_spec,
        out_shape=jax.ShapeDtypeStruct((4, 2, 512, 384), bf16),
        compiler_params=pltpu.CompilerParams(vmem_limit_bytes=50 * 1024 * 1024),
        cost_estimate=pl.CostEstimate(
            flops=2_800_000_000, bytes_accessed=10_000_000, transcendentals=0
        ),
        name="block",
    )(y.astype(jnp.int32)[None], own, other, weight, *deps)


def row_sum(v):
    return jnp.sum(v, axis=1, keepdims=True)


def body(
    block_in,
    norm_gain,
    in_weight,
    conv_weight,
    out_weight,
    ffn_gain,
    gate_up_weight,
    down_weight,
    out_grad,
):
    zh = lax.axis_index("zh")
    x = lax.axis_index("x")
    k = lax.axis_index("k")
    zl = lax.axis_index("zl")
    y = lax.axis_index("y")

    first = (2 * x + k) * 48
    mixer_own = to_owners(pack_mixer(in_weight, out_weight, first), y)
    sent = jnp.concatenate(
        [block_in, norm_gain[None], ffn_gain[None], jnp.zeros((14, 384), bf16)], axis=0
    )
    sent = ygather(sent)
    gain_one = jnp.concatenate([v[512:513] for v in sent], axis=1).astype(f32)
    gain_two = jnp.concatenate([v[513:514] for v in sent], axis=1).astype(f32)

    swapped = jnp.concatenate(
        [
            jnp.concatenate([v[496:512] for v in sent], axis=1),
            jnp.pad(conv_weight, ((0, 13), (0, D - 192))),
        ],
        axis=0,
    )
    swapped = zswap(swapped)

    mixer_both = jnp.stack([mixer_own, zexchange(mixer_own)])
    w_mixer = lax.all_gather(mixer_both, ("x", "k"))

    blocks = pack_ffn(gate_up_weight, down_weight, first)
    blocks, sent = lax.optimization_barrier((blocks, sent))
    ffn = to_owners(blocks, y)
    ffn, swapped, out_grad_late = lax.optimization_barrier((ffn, swapped, out_grad))
    w_ffn = lax.all_gather(ffn, ("x", "k"))
    grad_pieces = ygather(out_grad_late)
    half = zl.astype(jnp.int32)[None]
    results = mixer_call(half, sent, swapped, conv_weight, w_mixer)
    normed_one, inv_one = results[:2]
    proj, conv, before, acts, w_out = (results[i : i + 2] for i in range(2, 12, 2))

    out_parts, grad_pieces = lax.optimization_barrier((results[12:], grad_pieces))
    stream_own = block_in.astype(f32) + yreduce(out_parts)
    grads_own = jnp.concatenate(grad_pieces, axis=1)
    grads_other = zswap(grads_own)
    stream_sent = stream_own.astype(bf16)
    other = zswap(stream_sent)
    pieces_own = ygather(stream_sent)
    pieces_other = ygather(other)
    other_grads = [grads_other[:, 384 * j : 384 * j + 384] for j in range(4)]
    half_own = ffn_call(pieces_own, grad_pieces, gain_two, w_ffn)
    half_other = ffn_call(pieces_other, other_grads, gain_two, w_ffn, half_own[0])
    own_terms = yexchange(lambda j: half_own[4 + j])
    own_terms, half_other = lax.optimization_barrier((own_terms, half_other))
    other_terms = yexchange(lambda j: half_other[4 + j])
    normed_two = jnp.concatenate([half_own[0], half_other[0]], axis=0)
    theirs = t_dot(
        normed_two,
        jnp.concatenate(
            [jnp.where(k == 0, half[3], half[2]) for half in (half_own, half_other)], axis=0
        ),
    ).astype(bf16)
    block_parts = block_call(half_own[1], half_other[1], w_ffn, y)
    other_terms, half_own, half_other, theirs, block_parts = lax.optimization_barrier(
        (other_terms, half_own, half_other, theirs, block_parts)
    )
    theirs = kswap(theirs)
    sum_other = total_of(other_terms)
    sum_own = total_of(own_terms)
    two_grad = sum_own + zswap(sum_other.astype(bf16)).astype(f32)

    two_all = ygather(two_grad.astype(bf16))

    hidden = jnp.concatenate([half_own[1], half_other[1]], axis=0)
    grads_all = jnp.concatenate([grads_own, grads_other], axis=0)
    mine = t_dot(
        normed_two,
        jnp.concatenate(
            [jnp.where(k == 0, half[2], half[3]) for half in (half_own, half_other)], axis=0
        ),
    )
    gate_up_grad = (mine + theirs.astype(f32)).reshape(4, 4, 2, 48, FB)
    down_grad = t_dot(grads_all, hidden).reshape(4, 2, 192, FB)
    down_grad = split_k(down_grad, k, 1).reshape(4, 4, 2, 24, FB)
    ffn = jnp.concatenate([gate_up_grad, down_grad], axis=3).astype(bf16)
    ffn = jnp.stack([pick(ffn, (b - y) % 4) for b in range(4)])
    ffn, two_all, block_parts = lax.optimization_barrier((ffn, two_all, block_parts))
    block_sum = lax.psum_scatter(block_parts, "y", scatter_dimension=0, tiled=False)
    ffn = ffn.transpose(2, 1, 0, 3, 4).reshape(32, 72, FB)
    ffn = lax.all_to_all(ffn, ("zh", "x", "y"), 0, 0, tiled=True)

    stream_back, *grads, halo, own_stream_grad, gain_two_part = stream_call(
        two_all, pieces_own, grad_pieces, two_grad, gain_two, w_out, proj
    )
    halo = lax.ppermute(halo, "zl", [(1, 0)])
    results = back_call(
        sent, grads, proj, conv, before, halo, swapped, conv_weight, w_mixer
    )
    proj_back = results[:2]
    gain_one_part, *conv_parts = results[6:]
    one_sum = yreduce(results[2:6])
    one_grad = one_sum[:512]
    inner_one = one_sum[512:514].reshape(-1)[:512] + one_sum[514:516].reshape(-1)[:512]
    own_hat = block_in.astype(f32) * inv_one
    in_grad = own_stream_grad + inv_one * (
        gain_one[:, :384] * one_grad - own_hat * (inner_one / D)[:, None]
    )
    in_grad = in_grad.astype(bf16)

    tails = []
    for r in range(2):
        taps_part = conv_parts[r].reshape(-1)
        rest = jnp.concatenate([taps_part[384:], jnp.zeros((192,), f32)])
        small = jnp.stack([gain_two_part[0], taps_part[:384], rest], axis=1)
        small = jnp.pad(small, ((0, D - 384), (577, 60)))
        small = small + jnp.pad(gain_one_part.T, ((0, 0), (576, 63)))
        padded = jnp.pad(acts[r], ((0, 0), (0, 64)))
        tails.append((t_dot(normed_one, proj_back[r]) + small, t_dot(stream_back, padded)))

    def tail_half(index):
        halves = []
        for pair in tails:
            rows = [
                lax.dynamic_index_in_dim(v.reshape(4, 2, 192, -1), index, 1, keepdims=False)
                for v in pair
            ]
            halves.append(jnp.concatenate(rows, axis=2))
        return jnp.stack(halves)

    theirs = tail_half(1 - k)
    theirs, ffn, block_sum = lax.optimization_barrier((theirs, ffn, block_sum))
    block_out = stream_own + total_of([block_sum[0], zswap(block_sum[1])])
    block_out = block_out.astype(bf16)
    mixer = tail_half(k) + kswap(theirs.astype(bf16)).astype(f32)
    cols = list(jnp.sum(ffn.reshape(8, 4, 72, FB).astype(f32), axis=0).astype(bf16))
    part = jnp.concatenate(cols[:3] + [cols[3][:, 128:]], axis=1)
    part = gather_zh(part, zh)
    mixer = jnp.stack([pick(mixer.swapaxes(0, 1), (b - y) % 4) for b in range(4)])
    mixer = jnp.where(zl == 0, mixer, mixer[:, ::-1]).astype(bf16)
    mixer, part = lax.optimization_barrier((mixer, part))
    full = lax.all_gather(part, ("k", "x"))
    gate_up_out, down_out = ffn_finish(full)
    mixer = mixer.reshape(4, 2, 4, 2, 24, FB).transpose(3, 2, 1, 0, 4, 5)
    mixer = lax.all_to_all(
        mixer.reshape(64, 24, FB), ("zh", "x", "zl", "y"), 0, 0, tiled=True
    )
    cols = jnp.sum(mixer.reshape(16, 4, 24, FB).astype(f32), axis=0).astype(bf16)
    part = gather_zh(cols, zh)
    full = lax.all_gather(part, ("k", "x"))
    full, gate_up_out, down_out, in_grad, block_out = lax.optimization_barrier(
        (full, gate_up_out, down_out, in_grad, block_out)
    )
    in_out, out_out, own_small, sum_small = mixer_finish(full, y)
    gain_one_out = sum_small[:, 64]
    gain_two_out = own_small[:, 65]
    conv_out = jnp.concatenate([own_small[:, 66], own_small[:192, 67]]).reshape(3, 192)
    return (
        block_out,
        in_grad,
        gain_one_out,
        in_out,
        conv_out,
        out_out,
        gain_two_out,
        gate_up_out,
        down_out,
    )


def solution(mesh):
    devices = mesh.devices.reshape(2, 4, 2, 2, 4)
    grid = Mesh(devices, ("zh", "x", "k", "zl", "y"))
    tokens = P(("zh", "x", "k", "zl"), "y")
    first = P(None, "y", "zl")
    second = P("zl", "y")
    in_specs = (
        tokens,
        P("y"),
        first,
        P(None, ("zl", "y")),
        second,
        P("y"),
        first,
        second,
        tokens,
    )
    out_specs = (
        tokens,
        tokens,
        P("y"),
        first,
        P(None, ("zl", "y")),
        second,
        P("y"),
        first,
        second,
    )
    return jax.shard_map(body, mesh=grid, in_specs=in_specs, out_specs=out_specs, check_vma=False)
```

time: 1670 us -> 521 us (0.31)
  waiting for transfers between devices: 1250 us -> 166 us
  local copies, waits for them, and re-layouts: 148 us -> 55.3 us
  Pallas kernels: 0 us -> 82.7 us
  matrix products: 95.8 us -> 22.5 us
  starting transfers between devices: 1.18 us -> 63.1 us
  blocking collectives: 122 us -> 73.7 us
    unnamed x17 -> x5, waiting for transfers between devices: 707 us -> 0.08 us
    all_gather x4, waiting for transfers between devices: 278 us -> 0.01 us  [the longest x2 0.01 us: body(): full = lax.all_gather(part, ('k', 'x'))]
    psum x1 -> x0, waiting for transfers between devices: 210 us -> none  [body(): lax.psum((in_weight_grad, kernel_grad, out_weight_grad, gate_up_grad, dow...]
    ppermute x0 -> x46, waiting for transfers between devices: none -> 135 us  [the longest x33 80.9 us: yshift(): return lax.ppermute(v, 'y', [(i, (i + d) % 4) for i in range(4)])]
    psum x6 -> x0, blocking collectives: 84.2 us -> none  [the longest x4 41.3 us: feature_total(): return lax.psum(jnp.sum(values, axis=1), 'col')]
    pallas_call x0 -> x8, Pallas kernels: none -> 82.7 us  [the longest x2 28 us: ffn_call(): pl.pallas_call(ffn_kernel, grid=(2,), in_specs=[narrow] * 8 + [pl.BlockSp...]
    all_to_all x0 -> x1, blocking collectives: none -> 73.7 us  [body(): lax.all_to_all(mixer.reshape(64, 24, FB), ('zh', 'x', 'zl', 'y'), 0, 0, t...]
    dot_general x10 -> x7, matrix products: 86 us -> 22.5 us  [t_dot(): lax.dot_general(a, b, (((0,), (0,)), ((), ())), preferred_element_type=f32)]
  transfers between devices with their start and end apart: 13 -> 52, of which waited for: 11 -> 28; matrix products, arithmetic and copies ran while one was open for 4% -> 15% of each run, Pallas kernels for 0% -> 16%
where the time goes in v2:
time: 521 us; the launch traced here: 514 us
  waiting for transfers between devices  166 us (32%)
  Pallas kernels  82.7 us (16%)
  blocking collectives  73.7 us (14%)
  starting transfers between devices  63.1 us (12%)
  local copies, waits for them, and re-layouts  55.3 us (11%)
  other arithmetic  34.3 us (7%)
  matrix products  22.5 us (4%)
  between operations  15.6 us (3%)
    ppermute x33, waiting for transfers between devices, yshift(): return lax.ppermute(v, 'y', [(i, (i + d) % 4) for i in range(4)])  80.9 us
    all_to_all x1, blocking collectives, body(): lax.all_to_all(mixer.reshape(64, 24, FB), ('zh', 'x', 'zl', 'y'), 0, 0, t...  73.7 us
    ppermute x5, waiting for transfers between devices, zswap(): return lax.ppermute(v, 'zl', [(0, 1), (1, 0)])  37.4 us
    ppermute x33, starting transfers between devices, yshift(): return lax.ppermute(v, 'y', [(i, (i + d) % 4) for i in range(4)])  34.6 us
    pallas_call x2, Pallas kernels, ffn_call(): pl.pallas_call(ffn_kernel, grid=(2,), in_specs=[narrow] * 8 + [pl.BlockSp...  28 us
    unnamed x168, local copies, waits for them, and re-layouts  23.4 us
    dot_general x7, matrix products, t_dot(): lax.dot_general(a, b, (((0,), (0,)), ((), ())), preferred_element_type=f32)  22.5 us
    all_to_all x1, waiting for transfers between devices, body(): ffn = lax.all_to_all(ffn, ('zh', 'x', 'y'), 0, 0, tiled=True)  15.9 us
  transfers between devices with their start and end apart: 52, of which 28 were waited for; matrix products, arithmetic and copies ran while one was open for 15% of the time, Pallas kernels for 16%

profile of v2, /device:TPU:0, one launch (start us, length us, event | category | flops | bytes accessed | tf_op | source)
XLA Modules:
  0.0 513.6 jit_solution(771751868025525276)
XLA Ops:
  21.0 4.1 collective-permute-start.11
  36.2 5.8 %collective-permute-done.refs_2_.refs_1_ = bf16[528,384]{1,0:T(8,128)(2,1)S(1)} collective-permute-done((bf16[528,384]{1,0:T(8,128)(2,1)S(1)}, bf16[528,384]{1,0:T(8,128)(2,1)S(1)}, u32[]{:S(2)}, u32[]{:S(2)}) %collective-permute-start) | collective-permute-done | bytes 405536 | tf_op jit(solution)/shard_map/ppermute | solution.py:21
  43.9 5.7 %collective-permute-done.2.refs_4_.refs_3_ = bf16[528,384]{1,0:T(8,128)(2,1)} collective-permute-done((bf16[528,384]{1,0:T(8,128)(2,1)S(1)}, bf16[528,384]{1,0:T(8,128)(2,1)}, u32[]{:S(2)}, u32[]{:S(2)}) %collective-permute-start.2) | collective-permute-done | bytes 405536 | tf_op jit(solution)/shard_map/ppermute | solution.py:21
  54.3 4.6 collective-permute-done.3
  70.0 12.2 %mixer.1 = (bf16[512,1536]{1,0:T(8,128)(2,1)}, f32[512,1]{1,0:T(8,128)S(1)}, f32[512,576]{1,0:T(8,128)}, f32[512,576]{1,0:T(8,128)}, f32[512,192]{1,0:T(8,128)},...) custom-call(s32[1]{0:T(128)} %bitcast.refs_0_, ...), custom_call_target="tpu_custom_call" | custom-call | flops 1000000 | bytes 1000000 | tf_op jit(solution)/shard_map/mixer/pallas_call | solution.py:255
  82.4 5.7 %collective-permute-done.14.refs_7_.refs_11_ = bf16[512,384]{1,0:T(8,128)(2,1)} collective-permute-done((bf16[512,384]{1,0:T(8,128)(2,1)S(1)}, bf16[512,384]{1,0:T(8,128)(2,1)}, u32[]{:S(2)}, u32[]{:S(2)}) %collective-permute-start.14) | collective-permute-done | bytes 393248 | tf_op jit(solution)/shard_map/ppermute | solution.py:21
  95.2 10.0 %collective-permute-done.15 = bf16[512,384]{1,0:T(8,128)(2,1)S(1)} collective-permute-done((bf16[512,384]{1,0:T(8,128)(2,1)S(1)}, bf16[512,384]{1,0:T(8,128)(2,1)S(1)}, u32[]{:S(2)}, u32[]{:S(2)}) %collective-permute-start.15) | collective-permute-done | bytes 393248 | tf_op jit(solution)/shard_map/ppermute | solution.py:21
  107.8 6.1 %collective-permute-done.17 = bf16[512,384]{1,0:T(8,128)(2,1)S(1)} collective-permute-done((bf16[512,384]{1,0:T(8,128)(2,1)S(1)}, bf16[512,384]{1,0:T(8,128)(2,1)S(1)}, u32[]{:S(2)}, u32[]{:S(2)}) %collective-permute-start.17) | collective-permute-done | bytes 393248 | tf_op jit(solution)/shard_map/ppermute | solution.py:21
  119.4 17.9 %collective-permute-done.24.refs_0_ = bf16[512,384]{1,0:T(8,128)(2,1)} collective-permute-done((bf16[512,384]{1,0:T(8,128)(2,1)S(1)}, bf16[512,384]{1,0:T(8,128)(2,1)}, u32[]{:S(2)}, u32[]{:S(2)}) %collective-permute-start.24) | collective-permute-done | bytes 393248 | tf_op jit(solution)/shard_map/ppermute | solution.py:33
  144.3 13.8 %ffn.2 = (bf16[512,1536]{1,0:T(8,128)(2,1)}, bf16[512,896]{1,0:T(8,128)(2,1)}, bf16[512,896]{1,0:T(8,128)(2,1)}, bf16[512,896]{1,0:T(8,128)(2,1)}, f32[512,384]{...) custom-call(bf16[512,384]{1,0:T(8,128)(2,1)S(1)} %fusion.42.refs_0_.refs_4_, ...), custom_call_target="tpu_custom_call" | custom-call | flops 8400000000 | bytes 16000000 | tf_op jit(solution)/shard_map/ffn/pallas_call | solution.py:535
  163.6 14.3 %ffn.3 = (bf16[512,1536]{1,0:T(8,128)(2,1)}, bf16[512,896]{1,0:T(8,128)(2,1)}, bf16[512,896]{1,0:T(8,128)(2,1)}, bf16[512,896]{1,0:T(8,128)(2,1)}, f32[512,384]{...) custom-call(bf16[512,384]{1,0:T(8,128)(2,1)} %collective-permute-done.24.refs_0_, ...), custom_call_target="tpu_custom_call" | custom-call | flops 8400000000 | bytes 16000000 | tf_op jit(solution)/shard_map/ffn/pallas_call | solution.py:535
  183.4 4.8 convolution_convert_fusion
  188.2 9.1 %block.1 = bf16[4,2,512,384]{3,2,1,0:T(8,128)(2,1)} custom-call(s32[1]{0:T(128)} %bitcast.47.place.y_ref, bf16[512,896]{1,0:T(8,128)(2,1)S(1)} %copy-done.5, bf16[512,896]{1,0:T(8,128)(2,1)S(1)} %copy-done.6, bf16[8,4,48,2688]{3,2,1,0:T(8,128)(2,1)} %bitcast.180), custom_call_target="tpu_custom_call" | custom-call | flops 2800000000 | bytes 10000000 | tf_op jit(solution)/shard_map/block/pallas_call | solution.py:578
  197.3 4.1 collective-permute-done.31
  201.6 5.4 %fusion.3 = f32[1536,896]{1,0:T(8,128)S(1)} fusion(bf16[512,1536]{1,0:T(8,128)(2,1)} %collective-permute-done.28, bf16[512,1536]{1,0:T(8,128)(2,1)} %constant_dynamic-update-slice_fusion, bf16[512,896]{1,0:T(8,128)(2,1)S(1)} %copy-done.6, bf16[512,896]{1,0:T(8,128)(2,1)} %get-tuple-element.168.h0_ref), kind=kOutput, calls=%fused_computation.20 | convolution fusion | flops 2828533760 | bytes 10485760 | tf_op jit(solution)/shard_map/dot_general | solution.py:77
  214.3 9.9 %collective-permute-done.34 = bf16[512,384]{1,0:T(8,128)(2,1)S(1)} collective-permute-done((bf16[512,384]{1,0:T(8,128)(2,1)S(1)}, bf16[512,384]{1,0:T(8,128)(2,1)S(1)}, u32[]{:S(2)}, u32[]{:S(2)}) %collective-permute-start.34) | collective-permute-done | bytes 393248 | tf_op jit(solution)/shard_map/ppermute | solution.py:33
  230.9 5.1 add_convert_fusion
  241.0 6.3 %collective-permute-done.37.refs_3_ = bf16[512,384]{1,0:T(8,128)(2,1)S(1)} collective-permute-done((bf16[512,384]{1,0:T(8,128)(2,1)S(1)}, bf16[512,384]{1,0:T(8,128)(2,1)S(1)}, u32[]{:S(2)}, u32[]{:S(2)}) %collective-permute-start.37) | collective-permute-done | bytes 393248 | tf_op jit(solution)/shard_map/ppermute | solution.py:21
  248.1 8.8 %all-to-all-start = ((bf16[32,72,896]{2,1,0:T(8,128)(2,1)}), bf16[32,72,896]{2,1,0:T(8,128)(2,1)}, u32[]{:S(2)}, u32[]{:S(2)}) async-start(bf16[32,72,896]{2,1,0:T(8,128)(2,1)} %bitcast.174), calls=%async_computation | async-start | bytes 8257536 | tf_op jit(solution)/shard_map/all_to_all | solution.py:691
  261.1 6.2 %stream.1 = (bf16[512,1536]{1,0:T(8,128)(2,1)}, f32[512,192]{1,0:T(8,128)}, f32[512,192]{1,0:T(8,128)}, f32[2,8,192]{2,1,0:T(8,128)S(1)}, f32[512,384]{1,0:T(8,128)}, /*index=5*/f32[1,384]{1,0:T(1,128)S(1)}) custom-call(bf16[512,384]{1,0:T(8,128)(2,1)S(1)} %get-tuple-element.179.refs_0_, bf16[512,384]{1,0:T(8,128)(2,1)S(1)} %copy-done.20, ...), custom_call_target="tpu_custom_call" | custom-call | flops 1000000 | bytes 1000000 | tf_op jit(solution)/shard_map/stream/pallas_call | solution.py:304
  275.8 13.2 %back.1 = (bf16[512,640]{1,0:T(8,128)(2,1)}, bf16[512,640]{1,0:T(8,128)(2,1)}, f32[528,384]{1,0:T(8,128)}, bf16[528,384]{1,0:T(8,128)(2,1)S(1)}, bf16[528,384]{1...) custom-call(bf16[528,384]{1,0:T(8,128)(2,1)S(1)} %maximum_maximum_fu, ...), custom_call_target="tpu_custom_call" | custom-call | flops 1000000 | bytes 1000000 | tf_op jit(solution)/shard_map/back/pallas_call | solution.py:404
  301.8 15.9 %all-to-all-done = bf16[32,72,896]{2,1,0:T(8,128)(2,1)} async-done(((bf16[32,72,896]{2,1,0:T(8,128)(2,1)}), bf16[32,72,896]{2,1,0:T(8,128)(2,1)}, u32[]{:S(2)}, u32[]{:S(2)}) %all-to-all-start) | async-done | bytes 4128800 | tf_op jit(solution)/shard_map/all_to_all | solution.py:691
  317.8 15.5 %reduce-scatter.2.cloned.1.call-done = bf16[1,2,512,384]{3,2,1,0:T(8,128)(2,1)} async-done(((bf16[4,2,512,384]{3,2,1,0:T(8,128)(2,1)}), bf16[1,2,512,384]{3,2,1,0:T(8,128)(2,1)}) %reduce-scatter.2.cloned.1.call-update) | async-done | bytes 786448 | tf_op jit(solution)/shard_map/reduce_scatter | solution.py:689
  350.2 7.0 %collective-permute-done.40 = bf16[72,3456]{1,0:T(8,128)(2,1)S(1)} collective-permute-done((bf16[72,3456]{1,0:T(8,128)(2,1)S(1)}, bf16[72,3456]{1,0:T(8,128)(2,1)S(1)}, u32[]{:S(2)}, u32[]{:S(2)}) %collective-permute-start.40) | collective-permute-done | bytes 497696 | tf_op jit(solution)/shard_map/ppermute | solution.py:168
  358.5 4.1 maximum_add_fusion
  367.6 73.7 %all_to_all.10 = bf16[64,24,896]{2,1,0:T(8,128)(2,1)} all-to-all(bf16[64,24,896]{2,1,0:T(8,128)(2,1)S(1)} %bitcast.177), channel_id=1, replica_groups=mesh['zh'=2,'x'=4,'k'=2,'zl'=2,'y'=4] {'zh','x','zl','y'}, dimensions={0} | all-to-all | bytes 5505024 | tf_op jit(solution)/shard_map/all_to_all | solution.py:745
  446.5 4.1 collective-permute-done.41
  451.5 3.9 collective-permute-start.42
  456.5 12.4 %collective-permute-done.42 = bf16[528,384]{1,0:T(8,128)(2,1)} collective-permute-done((bf16[528,384]{1,0:T(8,128)(2,1)S(1)}, bf16[528,384]{1,0:T(8,128)(2,1)}, u32[]{:S(2)}, u32[]{:S(2)}) %collective-permute-start.42) | collective-permute-done | bytes 405536 | tf_op jit(solution)/shard_map/ppermute | solution.py:21
  468.9 3.5 collective-permute-done.44
  475.8 9.7 %collective-permute-done.45 = bf16[512,384]{1,0:T(8,128)(2,1)} collective-permute-done((bf16[512,384]{1,0:T(8,128)(2,1)}, bf16[512,384]{1,0:T(8,128)(2,1)}, u32[]{:S(2)}, u32[]{:S(2)}) %collective-permute-start.45) | collective-permute-done | bytes 393248 | tf_op jit(solution)/shard_map/ppermute | solution.py:33
  488.4 11.2 %ffn_finish.1 = (f32[2,384,3456]{2,1,0:T(8,128)}, f32[3456,384]{1,0:T(8,128)}) custom-call(bf16[8,2,72,3456]{3,2,1,0:T(8,128)(2,1)} %bitcast.181), custom_call_target="tpu_custom_call" | custom-call | tf_op jit(solution)/shard_map/ffn_finish/pallas_call | solution.py:426
  (370 shorter events, 164.0 us)
Async XLA Ops:
  7.2 61.9 %all-gather.10.cloned.1.call-start = ((), (), s32[]{:S(2)}) async-start(), calls=%async_computation.5 | async-start | bytes 6193152 | tf_op jit(solution)/shard_map/all_gather | solution.py:630
  29.3 114.0 %all-gather.12.cloned.1.call-start = ((), (), s32[]{:S(2)}) async-start(), calls=%async_computation.6 | async-start | bytes 9289728 | tf_op jit(solution)/shard_map/all_gather | solution.py:636
  30.6 19.0 %collective-permute-start.2 = (bf16[528,384]{1,0:T(8,128)(2,1)S(1)}, bf16[528,384]{1,0:T(8,128)(2,1)}, u32[]{:S(2)}, u32[]{:S(2)}) collective-permute-start(bf16[528,384]{1,0:T(8,128)(2,1)S(1)} %maximum_maximum_fusion.refs_1_.refs_0_), channel_id=1, source_target_pairs={{0,1},{1,2},{2,3},{3,0},{4,5},{5,6},{6,7},{7,4},{8,9},{9,10},{10,1... | collective-permute-start | bytes 1216520 | tf_op jit(solution)/shard_map/ppermute | solution.py:21
  66.8 266.4 %reduce-scatter.2.cloned.1.call-start = ((), (), s32[]{:S(2)}) async-start(), calls=%async_computation.3 | async-start | bytes 3932160 | tf_op jit(solution)/shard_map/reduce_scatter | solution.py:689
  66.8 15.5 %collective-permute-start.12 = (bf16[512,384]{1,0:T(8,128)(2,1)S(1)}, bf16[512,384]{1,0:T(8,128)(2,1)S(1)}, u32[]{:S(2)}, u32[]{:S(2)}) collective-permute-start(bf16[512,384]{1,0:T(8,128)(2,1)S(1)} %copy-done.3), channel_id=1, source_target_pairs={{0,3},{1,0},{2,1},{3,2},{4,7},{5,4},{6,5},{7,6},{8,11},{9,8},{10,9... | collective-permute-start | bytes 1179656 | tf_op jit(solution)/shard_map/ppermute | solution.py:21
  67.9 14.4 %collective-permute-start.13 = (bf16[512,384]{1,0:T(8,128)(2,1)S(1)}, bf16[512,384]{1,0:T(8,128)(2,1)S(1)}, u32[]{:S(2)}, u32[]{:S(2)}) collective-permute-start(bf16[512,384]{1,0:T(8,128)(2,1)S(1)} %copy-done.3), channel_id=1, source_target_pairs={{0,2},{1,3},{2,0},{3,1},{4,6},{5,7},{6,4},{7,5},{8,10},{9,11},{10,... | collective-permute-start | bytes 1179656 | tf_op jit(solution)/shard_map/ppermute | solution.py:21
  68.1 20.0 %collective-permute-start.14 = (bf16[512,384]{1,0:T(8,128)(2,1)S(1)}, bf16[512,384]{1,0:T(8,128)(2,1)}, u32[]{:S(2)}, u32[]{:S(2)}) collective-permute-start(bf16[512,384]{1,0:T(8,128)(2,1)S(1)} %copy-done.3), channel_id=1, source_target_pairs={{0,1},{1,2},{2,3},{3,0},{4,5},{5,6},{6,7},{7,4},{8,9},{9,10},{10,1... | collective-permute-start | bytes 1179656 | tf_op jit(solution)/shard_map/ppermute | solution.py:21
  92.2 45.3 %collective-permute-start.28 = (bf16[512,1536]{1,0:T(8,128)(2,1)}, bf16[512,1536]{1,0:T(8,128)(2,1)}, u32[]{:S(2)}, u32[]{:S(2)}) collective-permute-start(bf16[512,1536]{1,0:T(8,128)(2,1)} %constant_dynamic-update-slice_fusion), channel_id=1, source_target_pairs={{0,4},{4,0},{1,5},{5,1},{2,6},{6,2},{3,7},{7,3},{8,12},{12,8},{9,1... | collective-permute-start | bytes 4718600 | tf_op jit(solution)/shard_map/ppermute | solution.py:33
  94.3 19.6 %collective-permute-start.17 = (bf16[512,384]{1,0:T(8,128)(2,1)S(1)}, bf16[512,384]{1,0:T(8,128)(2,1)S(1)}, u32[]{:S(2)}, u32[]{:S(2)}) collective-permute-start(bf16[512,384]{1,0:T(8,128)(2,1)S(1)} %get-tuple-element.133), channel_id=1, source_target_pairs={{0,1},{1,2},{2,3},{3,0},{4,5},{5,6},{6,7},{7,4},{8,9},{9,10},{10,1... | collective-permute-start | bytes 1179656 | tf_op jit(solution)/shard_map/ppermute | solution.py:21
  114.6 22.7 %collective-permute-start.24 = (bf16[512,384]{1,0:T(8,128)(2,1)S(1)}, bf16[512,384]{1,0:T(8,128)(2,1)}, u32[]{:S(2)}, u32[]{:S(2)}) collective-permute-start(bf16[512,384]{1,0:T(8,128)(2,1)S(1)} %fusion.42.refs_0_.refs_4_), channel_id=1, source_target_pairs={{0,4},{4,0},{1,5},{5,1},{2,6},{6,2},{3,7},{7,3},{8,12},{12,8},{9,1... | collective-permute-start | bytes 1179656 | tf_op jit(solution)/shard_map/ppermute | solution.py:33
  117.1 23.5 %collective-permute-start.18 = (bf16[512,384]{1,0:T(8,128)(2,1)S(1)}, bf16[512,384]{1,0:T(8,128)(2,1)S(1)}, u32[]{:S(2)}, u32[]{:S(2)}) collective-permute-start(bf16[512,384]{1,0:T(8,128)(2,1)S(1)} %fusion.42.refs_0_.refs_4_), channel_id=1, source_target_pairs={{0,3},{1,0},{2,1},{3,2},{4,7},{5,4},{6,5},{7,6},{8,11},{9,8},{10,9... | collective-permute-start | bytes 1179656 | tf_op jit(solution)/shard_map/ppermute | solution.py:21
  118.4 24.0 %collective-permute-start.19 = (bf16[512,384]{1,0:T(8,128)(2,1)S(1)}, bf16[512,384]{1,0:T(8,128)(2,1)S(1)}, u32[]{:S(2)}, u32[]{:S(2)}) collective-permute-start(bf16[512,384]{1,0:T(8,128)(2,1)S(1)} %fusion.42.refs_0_.refs_4_), channel_id=1, source_target_pairs={{0,2},{1,3},{2,0},{3,1},{4,6},{5,7},{6,4},{7,5},{8,10},{9,11},{10,... | collective-permute-start | bytes 1179656 | tf_op jit(solution)/shard_map/ppermute | solution.py:21
  118.4 24.0 %collective-permute-start.20 = (bf16[512,384]{1,0:T(8,128)(2,1)S(1)}, bf16[512,384]{1,0:T(8,128)(2,1)S(1)}, u32[]{:S(2)}, u32[]{:S(2)}) collective-permute-start(bf16[512,384]{1,0:T(8,128)(2,1)S(1)} %fusion.42.refs_0_.refs_4_), channel_id=1, source_target_pairs={{0,1},{1,2},{2,3},{3,0},{4,5},{5,6},{6,7},{7,4},{8,9},{9,10},{10,1... | collective-permute-start | bytes 1179656 | tf_op jit(solution)/shard_map/ppermute | solution.py:21
  137.3 25.0 %collective-permute-start.25 = (bf16[512,384]{1,0:T(8,128)(2,1)}, bf16[512,384]{1,0:T(8,128)(2,1)}, u32[]{:S(2)}, u32[]{:S(2)}) collective-permute-start(bf16[512,384]{1,0:T(8,128)(2,1)} %collective-permute-done.24.refs_0_), channel_id=1, source_target_pairs={{0,3},{1,0},{2,1},{3,2},{4,7},{5,4},{6,5},{7,6},{8,11},{9,8},{10,9... | collective-permute-start | bytes 1179656 | tf_op jit(solution)/shard_map/ppermute | solution.py:21
  137.6 26.0 %collective-permute-start.26 = (bf16[512,384]{1,0:T(8,128)(2,1)}, bf16[512,384]{1,0:T(8,128)(2,1)}, u32[]{:S(2)}, u32[]{:S(2)}) collective-permute-start(bf16[512,384]{1,0:T(8,128)(2,1)} %collective-permute-done.24.refs_0_), channel_id=1, source_target_pairs={{0,2},{1,3},{2,0},{3,1},{4,6},{5,7},{6,4},{7,5},{8,10},{9,11},{10,... | collective-permute-start | bytes 1179656 | tf_op jit(solution)/shard_map/ppermute | solution.py:21
  140.6 23.0 %collective-permute-start.27 = (bf16[512,384]{1,0:T(8,128)(2,1)}, bf16[512,384]{1,0:T(8,128)(2,1)}, u32[]{:S(2)}, u32[]{:S(2)}) collective-permute-start(bf16[512,384]{1,0:T(8,128)(2,1)} %collective-permute-done.24.refs_0_), channel_id=1, source_target_pairs={{0,1},{1,2},{2,3},{3,0},{4,5},{5,6},{6,7},{7,4},{8,9},{9,10},{10,1... | collective-permute-start | bytes 1179656 | tf_op jit(solution)/shard_map/ppermute | solution.py:21
  158.1 21.4 %collective-permute-start.21 = (bf16[512,384]{1,0:T(8,128)(2,1)S(1)}, bf16[512,384]{1,0:T(8,128)(2,1)S(1)}, u32[]{:S(2)}, u32[]{:S(2)}) collective-permute-start(bf16[512,384]{1,0:T(8,128)(2,1)S(1)} %get-tuple-element.141), channel_id=1, source_target_pairs={{0,3},{1,0},{2,1},{3,2},{4,7},{5,4},{6,5},{7,6},{8,11},{9,8},{10,9... | collective-permute-start | bytes 1179656 | tf_op jit(solution)/shard_map/ppermute | solution.py:21
  160.7 18.8 %collective-permute-start.22 = (bf16[512,384]{1,0:T(8,128)(2,1)S(1)}, bf16[512,384]{1,0:T(8,128)(2,1)S(1)}, u32[]{:S(2)}, u32[]{:S(2)}) collective-permute-start(bf16[512,384]{1,0:T(8,128)(2,1)S(1)} %get-tuple-element.142), channel_id=1, source_target_pairs={{0,2},{1,3},{2,0},{3,1},{4,6},{5,7},{6,4},{7,5},{8,10},{9,11},{10,... | collective-permute-start | bytes 1179656 | tf_op jit(solution)/shard_map/ppermute | solution.py:21
  162.3 17.9 %collective-permute-start.23 = (bf16[512,384]{1,0:T(8,128)(2,1)S(1)}, bf16[512,384]{1,0:T(8,128)(2,1)}, u32[]{:S(2)}, u32[]{:S(2)}) collective-permute-start(bf16[512,384]{1,0:T(8,128)(2,1)S(1)} %get-tuple-element.143), channel_id=1, source_target_pairs={{0,1},{1,2},{2,3},{3,0},{4,5},{5,6},{6,7},{7,4},{8,9},{9,10},{10,1... | collective-permute-start | bytes 1179656 | tf_op jit(solution)/shard_map/ppermute | solution.py:21
  180.1 17.2 %collective-permute-start.29 = (bf16[512,384]{1,0:T(8,128)(2,1)}, bf16[512,384]{1,0:T(8,128)(2,1)}, u32[]{:S(2)}, u32[]{:S(2)}) collective-permute-start(bf16[512,384]{1,0:T(8,128)(2,1)} %get-tuple-element.154), channel_id=1, source_target_pairs={{0,3},{1,0},{2,1},{3,2},{4,7},{5,4},{6,5},{7,6},{8,11},{9,8},{10,9... | collective-permute-start | bytes 1179656 | tf_op jit(solution)/shard_map/ppermute | solution.py:21
  181.5 15.8 %collective-permute-start.30 = (bf16[512,384]{1,0:T(8,128)(2,1)}, bf16[512,384]{1,0:T(8,128)(2,1)}, u32[]{:S(2)}, u32[]{:S(2)}) collective-permute-start(bf16[512,384]{1,0:T(8,128)(2,1)} %get-tuple-element.155), channel_id=1, source_target_pairs={{0,2},{1,3},{2,0},{3,1},{4,6},{5,7},{6,4},{7,5},{8,10},{9,11},{10,... | collective-permute-start | bytes 1179656 | tf_op jit(solution)/shard_map/ppermute | solution.py:21
  182.3 19.1 %collective-permute-start.31 = (bf16[512,384]{1,0:T(8,128)(2,1)}, bf16[512,384]{1,0:T(8,128)(2,1)}, u32[]{:S(2)}, u32[]{:S(2)}) collective-permute-start(bf16[512,384]{1,0:T(8,128)(2,1)} %get-tuple-element.156), channel_id=1, source_target_pairs={{0,1},{1,2},{2,3},{3,0},{4,5},{5,6},{6,7},{7,4},{8,9},{9,10},{10,1... | collective-permute-start | bytes 1179656 | tf_op jit(solution)/shard_map/ppermute | solution.py:21
  201.4 29.5 %collective-permute-start.32 = (bf16[1536,896]{1,0:T(8,128)(2,1)}, bf16[1536,896]{1,0:T(8,128)(2,1)}, u32[]{:S(2)}, u32[]{:S(2)}) collective-permute-start(bf16[1536,896]{1,0:T(8,128)(2,1)} %convolution_convert_fusion), channel_id=1, source_target_pairs={{0,8},{8,0},{1,9},{9,1},{2,10},{10,2},{3,11},{11,3},{4,12},{12,4},... | collective-permute-start | bytes 8257544 | tf_op jit(solution)/shard_map/ppermute | solution.py:37
  210.7 18.5 %collective-permute-start.33 = (bf16[4,192,896]{2,1,0:T(8,128)(2,1)}, bf16[4,192,896]{2,1,0:T(8,128)(2,1)}, u32[]{:S(2)}, u32[]{:S(2)}) collective-permute-start(bf16[4,192,896]{2,1,0:T(8,128)(2,1)} %fusion.17), channel_id=1, source_target_pairs={{0,8},{8,0},{1,9},{9,1},{2,10},{10,2},{3,11},{11,3},{4,12},{12,4},... | collective-permute-start | bytes 4128776 | tf_op jit(solution)/shard_map/ppermute | solution.py:37
  228.4 18.9 %collective-permute-start.37 = (bf16[512,384]{1,0:T(8,128)(2,1)S(1)}, bf16[512,384]{1,0:T(8,128)(2,1)S(1)}, u32[]{:S(2)}, u32[]{:S(2)}) collective-permute-start(bf16[512,384]{1,0:T(8,128)(2,1)S(1)} %get-tuple-element.179.refs_0_), channel_id=1, source_target_pairs={{0,1},{1,2},{2,3},{3,0},{4,5},{5,6},{6,7},{7,4},{8,9},{9,10},{10,1... | collective-permute-start | bytes 1179656 | tf_op jit(solution)/shard_map/ppermute | solution.py:21
  248.1 69.6 %all-to-all-start = ((bf16[32,72,896]{2,1,0:T(8,128)(2,1)}), bf16[32,72,896]{2,1,0:T(8,128)(2,1)}, u32[]{:S(2)}, u32[]{:S(2)}) async-start(bf16[32,72,896]{2,1,0:T(8,128)(2,1)} %bitcast.174), calls=%async_computation | async-start | bytes 8257536 | tf_op jit(solution)/shard_map/all_to_all | solution.py:691
  256.9 231.5 %all-gather.14.cloned.1.call-start = ((), (), s32[]{:S(2)}) async-start(), calls=%async_computation.7 | async-start | bytes 8957952 | tf_op jit(solution)/shard_map/all_gather | solution.py:742
  333.2 25.2 %collective-permute-start.39 = (bf16[2,4,192,896]{3,2,0,1:T(8,128)(2,1)}, bf16[2,4,192,896]{3,2,0,1:T(8,128)(2,1)}, u32[]{:S(2)}, u32[]{:S(2)}) collective-permute-start(bf16[2,4,192,896]{3,2,0,1:T(8,128)(2,1)} %pad_maximum_fusion), channel_id=1, source_target_pairs={{0,8},{8,0},{1,9},{9,1},{2,10},{10,2},{3,11},{11,3},{4,12},{12,4},... | collective-permute-start | bytes 8257544 | tf_op jit(solution)/shard_map/ppermute | solution.py:37
  341.7 15.5 %collective-permute-start.40 = (bf16[72,3456]{1,0:T(8,128)(2,1)S(1)}, bf16[72,3456]{1,0:T(8,128)(2,1)S(1)}, u32[]{:S(2)}, u32[]{:S(2)}) collective-permute-start(bf16[72,3456]{1,0:T(8,128)(2,1)S(1)} %get-tuple-element.274), channel_id=1, source_target_pairs={{0,64},{64,0},{1,65},{65,1},{2,66},{66,2},{3,67},{67,3},{4,68},{68... | collective-permute-start | bytes 1493000 | tf_op jit(solution)/shard_map/ppermute | solution.py:168
  365.4 134.2 %all-gather.8.cloned.1.call-start = ((), (), s32[]{:S(2)}) async-start(), calls=%async_computation.4 | async-start | bytes 3096576 | tf_op jit(solution)/shard_map/all_gather | solution.py:750
  451.5 17.5 %collective-permute-start.42 = (bf16[528,384]{1,0:T(8,128)(2,1)S(1)}, bf16[528,384]{1,0:T(8,128)(2,1)}, u32[]{:S(2)}, u32[]{:S(2)}) collective-permute-start(bf16[528,384]{1,0:T(8,128)(2,1)S(1)} %copy-done.38), channel_id=1, source_target_pairs={{0,3},{1,0},{2,1},{3,2},{4,7},{5,4},{6,5},{7,6},{8,11},{9,8},{10,9... | collective-permute-start | bytes 1216520 | tf_op jit(solution)/shard_map/ppermute | solution.py:21
  455.4 17.0 %collective-permute-start.44 = (bf16[528,384]{1,0:T(8,128)(2,1)S(1)}, bf16[528,384]{1,0:T(8,128)(2,1)}, u32[]{:S(2)}, u32[]{:S(2)}) collective-permute-start(bf16[528,384]{1,0:T(8,128)(2,1)S(1)} %get-tuple-element.216), channel_id=1, source_target_pairs={{0,1},{1,2},{2,3},{3,0},{4,5},{5,6},{6,7},{7,4},{8,9},{9,10},{10,1... | collective-permute-start | bytes 1216520 | tf_op jit(solution)/shard_map/ppermute | solution.py:21
  (102 other events, 1160.5 us)
Sparse Core Ops, SparseCore 0:
  29.4 37.1 all-gather.9
  68.9 49.1 all-gather.11
  248.2 84.9 reduce-scatter.1
  365.5 77.7 all-gather.13
  451.6 24.3 all-gather.7

commit v3 on v2

--- a/solution.py
+++ b/solution.py
@@ -511,7 +511,7 @@
         gate_up = dot(n_ref[...], w_pair)
         gate = gate_up[:, :size]
         up = gate_up[:, size:]
-        sig = 1.0 / (1.0 + jnp.exp(-gate))
+        sig = jax.nn.sigmoid(gate)
         silu = gate * sig
         h_ref[:, cols] = (silu * up).astype(bf16)
         hidden_grad = dot(grads, w_ref[:, pl.ds(2 * FB + first, size)])
@@ -552,39 +552,31 @@
     )(*streams, *grads, gain, weight, *deps)
 
 
-def block_kernel(place, h0_ref, h1_ref, w_ref, out_ref):
+def block_kernel(h0_ref, h1_ref, w_ref, out_ref):
     hidden = jnp.where(pl.program_id(1) < 1, h0_ref[...], h1_ref[...])
     out_ref[0, 0] = dot_t(hidden, w_ref[...].reshape(384, FB)).astype(bf16)
 
 
-def block_call(own, other, weight, y, *deps):
-    def where(j, t, place):
-        return ((place[0] + j) % 4, t, 0, 0)
-
-    def kernel(place, h0_ref, h1_ref, w_ref, *rest):
-        block_kernel(place, h0_ref, h1_ref, w_ref, rest[-1])
-
-    grid_spec = pltpu.PrefetchScalarGridSpec(
-        num_scalar_prefetch=1,
+def block_call(own, other, weight):
+    def where(j, t):
+        return (j, t, 0, 0)
+
+    return pl.pallas_call(
+        block_kernel,
         grid=(4, 2),
         in_specs=[
-            pl.BlockSpec((512, FB), lambda j, t, place: (0, 0)),
-            pl.BlockSpec((512, FB), lambda j, t, place: (0, 0)),
-            pl.BlockSpec((8, None, 48, FB), lambda j, t, place: (0, j, 0, 2)),
-        ]
-        + [pl.BlockSpec(memory_space=pl.ANY)] * len(deps),
+            pl.BlockSpec((512, FB), lambda j, t: (0, 0)),
+            pl.BlockSpec((512, FB), lambda j, t: (0, 0)),
+            pl.BlockSpec((8, None, 48, FB), lambda j, t: (0, j, 0, 2)),
+        ],
         out_specs=pl.BlockSpec((1, 1, 512, 384), where),
-    )
-    return pl.pallas_call(
-        kernel,
-        grid_spec=grid_spec,
         out_shape=jax.ShapeDtypeStruct((4, 2, 512, 384), bf16),
         compiler_params=pltpu.CompilerParams(vmem_limit_bytes=50 * 1024 * 1024),
         cost_estimate=pl.CostEstimate(
             flops=2_800_000_000, bytes_accessed=10_000_000, transcendentals=0
         ),
         name="block",
-    )(y.astype(jnp.int32)[None], own, other, weight, *deps)
+    )(own, other, weight)
 
 
 def row_sum(v):
@@ -661,19 +653,23 @@
             [jnp.where(k == 0, half[3], half[2]) for half in (half_own, half_other)], axis=0
         ),
     ).astype(bf16)
-    block_parts = block_call(half_own[1], half_other[1], w_ffn, y)
-    other_terms, half_own, half_other, theirs, block_parts = lax.optimization_barrier(
-        (other_terms, half_own, half_other, theirs, block_parts)
+    hidden = jnp.concatenate([half_own[1], half_other[1]], axis=0)
+    grads_all = jnp.concatenate([grads_own, grads_other], axis=0)
+    down_grad = t_dot(grads_all, hidden)
+    block_parts = block_call(half_own[1], half_other[1], w_ffn)
+    other_terms, half_own, half_other, theirs, down_grad, block_parts = (
+        lax.optimization_barrier(
+            (other_terms, half_own, half_other, theirs, down_grad, block_parts)
+        )
     )
     theirs = kswap(theirs)
     sum_other = total_of(other_terms)
     sum_own = total_of(own_terms)
-    two_grad = sum_own + zswap(sum_other.astype(bf16)).astype(f32)
+    from_other = zswap(sum_other.astype(bf16))
+    two_grad = sum_own + from_other.astype(f32)
 
     two_all = ygather(two_grad.astype(bf16))
 
-    hidden = jnp.concatenate([half_own[1], half_other[1]], axis=0)
-    grads_all = jnp.concatenate([grads_own, grads_other], axis=0)
     mine = t_dot(
         normed_two,
         jnp.concatenate(
@@ -681,12 +677,10 @@
         ),
     )
     gate_up_grad = (mine + theirs.astype(f32)).reshape(4, 4, 2, 48, FB)
-    down_grad = t_dot(grads_all, hidden).reshape(4, 2, 192, FB)
-    down_grad = split_k(down_grad, k, 1).reshape(4, 4, 2, 24, FB)
+    down_grad = split_k(down_grad.reshape(4, 2, 192, FB), k, 1).reshape(4, 4, 2, 24, FB)
     ffn = jnp.concatenate([gate_up_grad, down_grad], axis=3).astype(bf16)
     ffn = jnp.stack([pick(ffn, (b - y) % 4) for b in range(4)])
-    ffn, two_all, block_parts = lax.optimization_barrier((ffn, two_all, block_parts))
-    block_sum = lax.psum_scatter(block_parts, "y", scatter_dimension=0, tiled=False)
+    ffn, two_all = lax.optimization_barrier((ffn, two_all))
     ffn = ffn.transpose(2, 1, 0, 3, 4).reshape(32, 72, FB)
     ffn = lax.all_to_all(ffn, ("zh", "x", "y"), 0, 0, tiled=True)
 
@@ -699,15 +693,7 @@
     )
     proj_back = results[:2]
     gain_one_part, *conv_parts = results[6:]
-    one_sum = yreduce(results[2:6])
-    one_grad = one_sum[:512]
-    inner_one = one_sum[512:514].reshape(-1)[:512] + one_sum[514:516].reshape(-1)[:512]
-    own_hat = block_in.astype(f32) * inv_one
-    in_grad = own_stream_grad + inv_one * (
-        gain_one[:, :384] * one_grad - own_hat * (inner_one / D)[:, None]
-    )
-    in_grad = in_grad.astype(bf16)
-
+    one_parts = results[2:6]
     tails = []
     for r in range(2):
         taps_part = conv_parts[r].reshape(-1)
@@ -729,10 +715,12 @@
         return jnp.stack(halves)
 
     theirs = tail_half(1 - k)
-    theirs, ffn, block_sum = lax.optimization_barrier((theirs, ffn, block_sum))
-    block_out = stream_own + total_of([block_sum[0], zswap(block_sum[1])])
-    block_out = block_out.astype(bf16)
+    theirs, ffn, one_parts, block_parts = lax.optimization_barrier(
+        (theirs, ffn, one_parts, block_parts)
+    )
+    one_terms = yexchange(lambda j: one_parts[j])
     mixer = tail_half(k) + kswap(theirs.astype(bf16)).astype(f32)
+    mixer, one_terms = lax.optimization_barrier((mixer, one_terms))
     cols = list(jnp.sum(ffn.reshape(8, 4, 72, FB).astype(f32), axis=0).astype(bf16))
     part = jnp.concatenate(cols[:3] + [cols[3][:, 128:]], axis=1)
     part = gather_zh(part, zh)
@@ -745,8 +733,21 @@
     mixer = lax.all_to_all(
         mixer.reshape(64, 24, FB), ("zh", "x", "zl", "y"), 0, 0, tiled=True
     )
+    block_terms = yexchange(lambda j: block_parts[j])
+    one_sum = total_of(one_terms)
+    one_grad = one_sum[:512]
+    inner_one = one_sum[512:514].reshape(-1)[:512] + one_sum[514:516].reshape(-1)[:512]
+    own_hat = block_in.astype(f32) * inv_one
+    in_grad = own_stream_grad + inv_one * (
+        gain_one[:, :384] * one_grad - own_hat * (inner_one / D)[:, None]
+    )
+    in_grad = in_grad.astype(bf16)
     cols = jnp.sum(mixer.reshape(16, 4, 24, FB).astype(f32), axis=0).astype(bf16)
     part = gather_zh(cols, zh)
+    part, block_terms = lax.optimization_barrier((part, block_terms))
+    block_sum = total_of(block_terms)
+    block_out = stream_own + block_sum[0] + zswap(block_sum[1].astype(bf16)).astype(f32)
+    block_out = block_out.astype(bf16)
     full = lax.all_gather(part, ("k", "x"))
     full, gate_up_out, down_out, in_grad, block_out = lax.optimization_barrier(
         (full, gate_up_out, down_out, in_grad, block_out)

time: 521 us -> 506 us (0.971)
  blocking collectives: 73.7 us -> 0 us
  starting transfers between devices: 63.1 us -> 86.8 us
  waiting for transfers between devices: 166 us -> 186 us
  local copies, waits for them, and re-layouts: 55.3 us -> 62.1 us
  other arithmetic: 34.3 us -> 39.8 us
    all_to_all x1 -> x0, blocking collectives: 73.7 us -> none  [body(): lax.all_to_all(mixer.reshape(64, 24, FB), ('zh', 'x', 'zl', 'y'), 0, 0, t...]
    all_to_all x0 -> x1, waiting for transfers between devices: none -> 55 us  [body(): lax.all_to_all(mixer.reshape(64, 24, FB), ('zh', 'x', 'zl', 'y'), 0, 0, t...]
    ppermute x33 -> x36, starting transfers between devices: 34.6 us -> 50.4 us  [yshift(): return lax.ppermute(v, 'y', [(i, (i + d) % 4) for i in range(4)])]
    reduce_scatter x1 -> x0, waiting for transfers between devices: 15.5 us -> none  [body(): lax.psum_scatter(block_parts, 'y', scatter_dimension=0, tiled=False)]
    all_to_all x1, waiting for transfers between devices: 15.9 us -> 9.16 us  [body(): ffn = lax.all_to_all(ffn, ('zh', 'x', 'y'), 0, 0, tiled=True)]
    ppermute x33 -> x36, waiting for transfers between devices: 80.9 us -> 74.7 us  [yshift(): return lax.ppermute(v, 'y', [(i, (i + d) % 4) for i in range(4)])]
    all_to_all x0 -> x1, starting transfers between devices: none -> 5.59 us  [body(): lax.all_to_all(mixer.reshape(64, 24, FB), ('zh', 'x', 'zl', 'y'), 0, 0, t...]
    ppermute x2, waiting for transfers between devices: 11.1 us -> 5.54 us  [gather_zh(): other = lax.ppermute(part, 'zh', [(0, 1), (1, 0)])]
  transfers between devices with their start and end apart: 52 -> 55, of which waited for: 28 -> 27; matrix products, arithmetic and copies ran while one was open for 15% -> 20% of each run, Pallas kernels for 16% -> 16%
where the time goes in v3:
time: 506 us; the launch traced here: 498 us
  waiting for transfers between devices  186 us (37%)
  starting transfers between devices  86.8 us (17%)
  Pallas kernels  82.9 us (16%)
  local copies, waits for them, and re-layouts  62.1 us (12%)
  other arithmetic  39.8 us (8%)
  matrix products  24.4 us (5%)
  between operations  15.5 us (3%)
    ppermute x36, waiting for transfers between devices, yshift(): return lax.ppermute(v, 'y', [(i, (i + d) % 4) for i in range(4)])  74.7 us
    all_to_all x1, waiting for transfers between devices, body(): lax.all_to_all(mixer.reshape(64, 24, FB), ('zh', 'x', 'zl', 'y'), 0, 0, t...  55 us
    ppermute x36, starting transfers between devices, yshift(): return lax.ppermute(v, 'y', [(i, (i + d) % 4) for i in range(4)])  50.4 us
    ppermute x5, waiting for transfers between devices, zswap(): return lax.ppermute(v, 'zl', [(0, 1), (1, 0)])  35.1 us
    pallas_call x2, Pallas kernels, ffn_call(): pl.pallas_call(ffn_kernel, grid=(2,), in_specs=[narrow] * 8 + [pl.BlockSp...  28.1 us
    dot_general x7, matrix products, t_dot(): lax.dot_general(a, b, (((0,), (0,)), ((), ())), preferred_element_type=f32)  24.4 us
    unnamed x152, local copies, waits for them, and re-layouts  22.9 us
    pallas_call x1, Pallas kernels, back_call(): pl.pallas_call(kernel, in_specs=[whole] * 15 + [pl.BlockSpec(memory_space...  13.2 us
  transfers between devices with their start and end apart: 55, of which 27 were waited for; matrix products, arithmetic and copies ran while one was open for 20% of the time, Pallas kernels for 16%

profile of v3, /device:TPU:0, one launch (start us, length us, event | category | flops | bytes accessed | tf_op | source)
XLA Modules:
  0.0 498.0 jit_solution(12839781312721547911)
XLA Ops:
  21.0 4.1 collective-permute-start.11
  36.2 5.8 %collective-permute-done.refs_2_.refs_1_ = bf16[528,384]{1,0:T(8,128)(2,1)S(1)} collective-permute-done((bf16[528,384]{1,0:T(8,128)(2,1)S(1)}, bf16[528,384]{1,0:T(8,128)(2,1)S(1)}, u32[]{:S(2)}, u32[]{:S(2)}) %collective-permute-start) | collective-permute-done | bytes 405536 | tf_op jit(solution)/shard_map/ppermute | solution.py:21
  43.9 5.7 %collective-permute-done.2.refs_4_.refs_3_ = bf16[528,384]{1,0:T(8,128)(2,1)} collective-permute-done((bf16[528,384]{1,0:T(8,128)(2,1)S(1)}, bf16[528,384]{1,0:T(8,128)(2,1)}, u32[]{:S(2)}, u32[]{:S(2)}) %collective-permute-start.2) | collective-permute-done | bytes 405536 | tf_op jit(solution)/shard_map/ppermute | solution.py:21
  54.3 4.6 collective-permute-done.3
  68.6 12.1 %mixer.1 = (bf16[512,1536]{1,0:T(8,128)(2,1)}, f32[512,1]{1,0:T(8,128)S(1)}, f32[512,576]{1,0:T(8,128)}, f32[512,576]{1,0:T(8,128)}, f32[512,192]{1,0:T(8,128)},...) custom-call(s32[1]{0:T(128)} %bitcast.refs_0_, ...), custom_call_target="tpu_custom_call" | custom-call | flops 1000000 | bytes 1000000 | tf_op jit(solution)/shard_map/mixer/pallas_call | solution.py:255
  81.0 6.6 %collective-permute-done.14.refs_7_.refs_11_ = bf16[512,384]{1,0:T(8,128)(2,1)} collective-permute-done((bf16[512,384]{1,0:T(8,128)(2,1)S(1)}, bf16[512,384]{1,0:T(8,128)(2,1)}, u32[]{:S(2)}, u32[]{:S(2)}) %collective-permute-start.14) | collective-permute-done | bytes 393248 | tf_op jit(solution)/shard_map/ppermute | solution.py:21
  94.8 10.0 %collective-permute-done.15 = bf16[512,384]{1,0:T(8,128)(2,1)S(1)} collective-permute-done((bf16[512,384]{1,0:T(8,128)(2,1)S(1)}, bf16[512,384]{1,0:T(8,128)(2,1)S(1)}, u32[]{:S(2)}, u32[]{:S(2)}) %collective-permute-start.15) | collective-permute-done | bytes 393248 | tf_op jit(solution)/shard_map/ppermute | solution.py:21
  107.4 6.1 %collective-permute-done.17 = bf16[512,384]{1,0:T(8,128)(2,1)S(1)} collective-permute-done((bf16[512,384]{1,0:T(8,128)(2,1)S(1)}, bf16[512,384]{1,0:T(8,128)(2,1)S(1)}, u32[]{:S(2)}, u32[]{:S(2)}) %collective-permute-start.17) | collective-permute-done | bytes 393248 | tf_op jit(solution)/shard_map/ppermute | solution.py:21
  118.9 18.0 %collective-permute-done.24.refs_0_ = bf16[512,384]{1,0:T(8,128)(2,1)} collective-permute-done((bf16[512,384]{1,0:T(8,128)(2,1)S(1)}, bf16[512,384]{1,0:T(8,128)(2,1)}, u32[]{:S(2)}, u32[]{:S(2)}) %collective-permute-start.24) | collective-permute-done | bytes 393248 | tf_op jit(solution)/shard_map/ppermute | solution.py:33
  143.8 14.1 %ffn.2 = (bf16[512,1536]{1,0:T(8,128)(2,1)}, bf16[512,896]{1,0:T(8,128)(2,1)}, bf16[512,896]{1,0:T(8,128)(2,1)}, bf16[512,896]{1,0:T(8,128)(2,1)}, f32[512,384]{...) custom-call(bf16[512,384]{1,0:T(8,128)(2,1)S(1)} %fusion.44.refs_0_.refs_4_, ...), custom_call_target="tpu_custom_call" | custom-call | flops 8400000000 | bytes 16000000 | tf_op jit(solution)/shard_map/ffn/pallas_call | solution.py:535
  163.5 14.0 %ffn.3 = (bf16[512,1536]{1,0:T(8,128)(2,1)}, bf16[512,896]{1,0:T(8,128)(2,1)}, bf16[512,896]{1,0:T(8,128)(2,1)}, bf16[512,896]{1,0:T(8,128)(2,1)}, f32[512,384]{...) custom-call(bf16[512,384]{1,0:T(8,128)(2,1)} %collective-permute-done.24.refs, ...), custom_call_target="tpu_custom_call" | custom-call | flops 8400000000 | bytes 16000000 | tf_op jit(solution)/shard_map/ffn/pallas_call | solution.py:535
  183.1 9.2 %block.1 = bf16[4,2,512,384]{3,2,1,0:T(8,128)(2,1)} custom-call(bf16[512,896]{1,0:T(8,128)(2,1)S(1)} %copy-done.5, bf16[512,896]{1,0:T(8,128)(2,1)S(1)} %copy-done.6, bf16[8,4,48,2688]{3,2,1,0:T(8,128)(2,1)} %bitcast.193), custom_call_target="tpu_custom_call" | custom-call | flops 2800000000 | bytes 10000000 | tf_op jit(solution)/shard_map/block/pallas_call | solution.py:564
  193.8 4.8 convolution_convert_fusion
  198.7 7.3 %fusion.3 = f32[1536,896]{1,0:T(8,128)} fusion(bf16[512,1536]{1,0:T(8,128)(2,1)} %collective-permute-done.28, bf16[512,1536]{1,0:T(8,128)(2,1)} %constant_dynamic-update-slice_fusion, bf16[512,896]{1,0:T(8,128)(2,1)S(1)} %copy-done.6, bf16[512,896]{1,0:T(8,128)(2,1)S(1)} %copy-done.5), kind=kOutput, calls=%fused_computation.20 | convolution fusion | flops 2828533760 | bytes 10485760 | tf_op jit(solution)/shard_map/dot_general | solution.py:77
  213.8 8.8 %collective-permute-done.34 = bf16[512,384]{1,0:T(8,128)(2,1)S(1)} collective-permute-done((bf16[512,384]{1,0:T(8,128)(2,1)S(1)}, bf16[512,384]{1,0:T(8,128)(2,1)S(1)}, u32[]{:S(2)}, u32[]{:S(2)}) %collective-permute-start.34) | collective-permute-done | bytes 393248 | tf_op jit(solution)/shard_map/ppermute | solution.py:33
  231.2 5.1 %add_convert_fusion = bf16[1536,896]{1,0:T(8,128)(2,1)S(1)} fusion(bf16[1536,896]{1,0:T(8,128)(2,1)} %collective-permute-done.32, bf16[1024,1536]{1,0:T(8,128)(2,1)S(1)} %copy-done.61, bf16[512,896]{1,0:T(8,128)(2,1)S(1)} %broadcast_select_fusion, bf16[512,896]{1,0:T(8,128)(2,1)S(1)} %broadcast_select_fusion.1), kind=kOutput, calls=%fused_computation.9 | convolution fusion | flops 2826371072 | bytes 10485760 | tf_op jit(solution)/shard_map/dot_general | solution.py:77
  239.6 3.8 collective-permute-done.35.refs_1_
  247.9 9.2 %all-to-all-start = ((bf16[32,72,896]{2,1,0:T(8,128)(2,1)}), bf16[32,72,896]{2,1,0:T(8,128)(2,1)}, u32[]{:S(2)}, u32[]{:S(2)}) async-start(bf16[32,72,896]{2,1,0:T(8,128)(2,1)} %bitcast.188), calls=%async_computation | async-start | bytes 8257536 | tf_op jit(solution)/shard_map/all_to_all | solution.py:685
  261.2 6.3 %stream.1 = (bf16[512,1536]{1,0:T(8,128)(2,1)}, f32[512,192]{1,0:T(8,128)}, f32[512,192]{1,0:T(8,128)}, f32[2,8,192]{2,1,0:T(8,128)S(1)}, f32[512,384]{1,0:T(8,128)}, /*index=5*/f32[1,384]{1,0:T(1,128)S(1)}) custom-call(bf16[512,384]{1,0:T(8,128)(2,1)S(1)} %get-tuple-element.189.refs_0_, bf16[512,384]{1,0:T(8,128)(2,1)S(1)} %copy-done.15, ...), custom_call_target="tpu_custom_call" | custom-call | flops 1000000 | bytes 1000000 | tf_op jit(solution)/shard_map/stream/pallas_call | solution.py:304
  276.3 13.2 %back.1 = (bf16[512,640]{1,0:T(8,128)(2,1)}, bf16[512,640]{1,0:T(8,128)(2,1)}, f32[528,384]{1,0:T(8,128)}, bf16[528,384]{1,0:T(8,128)(2,1)S(1)}, bf16[528,384]{1...) custom-call(bf16[528,384]{1,0:T(8,128)(2,1)S(1)} %maximum_maximum_fu, ...), custom_call_target="tpu_custom_call" | custom-call | flops 1000000 | bytes 1000000 | tf_op jit(solution)/shard_map/back/pallas_call | solution.py:404
  300.9 9.2 %all-to-all-done = bf16[32,72,896]{2,1,0:T(8,128)(2,1)} async-done(((bf16[32,72,896]{2,1,0:T(8,128)(2,1)}), bf16[32,72,896]{2,1,0:T(8,128)(2,1)}, u32[]{:S(2)}, u32[]{:S(2)}) %all-to-all-start) | async-done | bytes 4128800 | tf_op jit(solution)/shard_map/all_to_all | solution.py:685
  315.4 3.7 reduce_sum.24
  320.3 5.4 %collective-permute-start.43 = (bf16[72,3456]{1,0:T(8,128)(2,1)S(1)}, bf16[72,3456]{1,0:T(8,128)(2,1)S(1)}, u32[]{:S(2)}, u32[]{:S(2)}) collective-permute-start(bf16[72,3456]{1,0:T(8,128)(2,1)S(1)} %get-tuple-element.302), channel_id=1, source_target_pairs={{0,64},{64,0},{1,65},{65,1},{2,66},{66,2},{3,67},{67,3},{4,68},{68... | collective-permute-start | bytes 1493000 | tf_op jit(solution)/shard_map/ppermute | solution.py:168
  330.8 13.8 %collective-permute-start.40 = (bf16[528,384]{1,0:T(8,128)(2,1)S(1)}, bf16[528,384]{1,0:T(8,128)(2,1)S(1)}, u32[]{:S(2)}, u32[]{:S(2)}) collective-permute-start(bf16[528,384]{1,0:T(8,128)(2,1)S(1)} %get-tuple-element.221), channel_id=1, source_target_pairs={{0,3},{1,0},{2,1},{3,2},{4,7},{5,4},{6,5},{7,6},{8,11},{9,8},{10,9... | collective-permute-start | bytes 1216520 | tf_op jit(solution)/shard_map/ppermute | solution.py:21
  346.8 4.1 maximum_add_fusion
  350.8 11.5 %collective-permute-done.40 = bf16[528,384]{1,0:T(8,128)(2,1)S(1)} collective-permute-done((bf16[528,384]{1,0:T(8,128)(2,1)S(1)}, bf16[528,384]{1,0:T(8,128)(2,1)S(1)}, u32[]{:S(2)}, u32[]{:S(2)}) %collective-permute-start.40) | collective-permute-done | bytes 405536 | tf_op jit(solution)/shard_map/ppermute | solution.py:21
  372.7 5.6 %all-to-all-start.1 = ((bf16[64,24,896]{2,1,0:T(8,128)(2,1)}), bf16[64,24,896]{2,1,0:T(8,128)(2,1)}, u32[]{:S(2)}, u32[]{:S(2)}) async-start(bf16[64,24,896]{2,1,0:T(8,128)(2,1)} %bitcast.189), calls=%async_computation.1 | async-start | bytes 5505024 | tf_op jit(solution)/shard_map/all_to_all | solution.py:733
  378.4 3.6 slice_bitcast_fusion.1
  386.4 55.0 %all-to-all-done.1 = bf16[64,24,896]{2,1,0:T(8,128)(2,1)} async-done(((bf16[64,24,896]{2,1,0:T(8,128)(2,1)}), bf16[64,24,896]{2,1,0:T(8,128)(2,1)}, u32[]{:S(2)}, u32[]{:S(2)}) %all-to-all-start.1) | async-done | bytes 2752544 | tf_op jit(solution)/shard_map/all_to_all | solution.py:733
  445.9 5.5 %collective-permute-done.44 = bf16[4,24,896]{2,1,0:T(8,128)(2,1)S(1)} collective-permute-done((bf16[4,24,896]{2,1,0:T(8,128)(2,1)}, bf16[4,24,896]{2,1,0:T(8,128)(2,1)S(1)}, u32[]{:S(2)}, u32[]{:S(2)}) %collective-permute-start.44) | collective-permute-done | bytes 172064 | tf_op jit(solution)/shard_map/ppermute | solution.py:168
  461.3 8.4 %collective-permute-done.48 = bf16[512,384]{1,0:T(8,128)(2,1)} collective-permute-done((bf16[512,384]{1,0:T(8,128)(2,1)}, bf16[512,384]{1,0:T(8,128)(2,1)}, u32[]{:S(2)}, u32[]{:S(2)}) %collective-permute-start.48) | collective-permute-done | bytes 393248 | tf_op jit(solution)/shard_map/ppermute | solution.py:33
  472.8 11.2 %ffn_finish.1 = (f32[2,384,3456]{2,1,0:T(8,128)}, f32[3456,384]{1,0:T(8,128)}) custom-call(bf16[8,2,72,3456]{3,2,1,0:T(8,128)(2,1)} %bitcast.194), custom_call_target="tpu_custom_call" | custom-call | tf_op jit(solution)/shard_map/ffn_finish/pallas_call | solution.py:426
  (360 shorter events, 176.6 us)
Async XLA Ops:
  7.2 61.4 %all-gather.9.cloned.1.call-start = ((), (), s32[]{:S(2)}) async-start(), calls=%async_computation.2 | async-start | bytes 6193152 | tf_op jit(solution)/shard_map/all_gather | solution.py:622
  29.3 113.5 %all-gather.11.cloned.1.call-start = ((), (), s32[]{:S(2)}) async-start(), calls=%async_computation.3 | async-start | bytes 9289728 | tf_op jit(solution)/shard_map/all_gather | solution.py:628
  30.6 19.0 %collective-permute-start.2 = (bf16[528,384]{1,0:T(8,128)(2,1)S(1)}, bf16[528,384]{1,0:T(8,128)(2,1)}, u32[]{:S(2)}, u32[]{:S(2)}) collective-permute-start(bf16[528,384]{1,0:T(8,128)(2,1)S(1)} %maximum_maximum_fusion.refs_1_.refs_0_), channel_id=1, source_target_pairs={{0,1},{1,2},{2,3},{3,0},{4,5},{5,6},{6,7},{7,4},{8,9},{9,10},{10,1... | collective-permute-start | bytes 1216520 | tf_op jit(solution)/shard_map/ppermute | solution.py:21
  67.6 20.0 %collective-permute-start.14 = (bf16[512,384]{1,0:T(8,128)(2,1)S(1)}, bf16[512,384]{1,0:T(8,128)(2,1)}, u32[]{:S(2)}, u32[]{:S(2)}) collective-permute-start(bf16[512,384]{1,0:T(8,128)(2,1)S(1)} %copy-done.3), channel_id=1, source_target_pairs={{0,1},{1,2},{2,3},{3,0},{4,5},{5,6},{6,7},{7,4},{8,9},{9,10},{10,1... | collective-permute-start | bytes 1179656 | tf_op jit(solution)/shard_map/ppermute | solution.py:21
  91.9 45.3 %collective-permute-start.28 = (bf16[512,1536]{1,0:T(8,128)(2,1)}, bf16[512,1536]{1,0:T(8,128)(2,1)}, u32[]{:S(2)}, u32[]{:S(2)}) collective-permute-start(bf16[512,1536]{1,0:T(8,128)(2,1)} %constant_dynamic-update-slice_fusion), channel_id=1, source_target_pairs={{0,4},{4,0},{1,5},{5,1},{2,6},{6,2},{3,7},{7,3},{8,12},{12,8},{9,1... | collective-permute-start | bytes 4718600 | tf_op jit(solution)/shard_map/ppermute | solution.py:33
  93.9 19.6 %collective-permute-start.17 = (bf16[512,384]{1,0:T(8,128)(2,1)S(1)}, bf16[512,384]{1,0:T(8,128)(2,1)S(1)}, u32[]{:S(2)}, u32[]{:S(2)}) collective-permute-start(bf16[512,384]{1,0:T(8,128)(2,1)S(1)} %get-tuple-element.145), channel_id=1, source_target_pairs={{0,1},{1,2},{2,3},{3,0},{4,5},{5,6},{6,7},{7,4},{8,9},{9,10},{10,1... | collective-permute-start | bytes 1179656 | tf_op jit(solution)/shard_map/ppermute | solution.py:21
  114.2 22.7 %collective-permute-start.24 = (bf16[512,384]{1,0:T(8,128)(2,1)S(1)}, bf16[512,384]{1,0:T(8,128)(2,1)}, u32[]{:S(2)}, u32[]{:S(2)}) collective-permute-start(bf16[512,384]{1,0:T(8,128)(2,1)S(1)} %fusion.44.refs_0_.refs_4_), channel_id=1, source_target_pairs={{0,4},{4,0},{1,5},{5,1},{2,6},{6,2},{3,7},{7,3},{8,12},{12,8},{9,1... | collective-permute-start | bytes 1179656 | tf_op jit(solution)/shard_map/ppermute | solution.py:33
  116.7 23.4 %collective-permute-start.18 = (bf16[512,384]{1,0:T(8,128)(2,1)S(1)}, bf16[512,384]{1,0:T(8,128)(2,1)S(1)}, u32[]{:S(2)}, u32[]{:S(2)}) collective-permute-start(bf16[512,384]{1,0:T(8,128)(2,1)S(1)} %fusion.44.refs_0_.refs_4_), channel_id=1, source_target_pairs={{0,3},{1,0},{2,1},{3,2},{4,7},{5,4},{6,5},{7,6},{8,11},{9,8},{10,9... | collective-permute-start | bytes 1179656 | tf_op jit(solution)/shard_map/ppermute | solution.py:21
  118.0 23.9 %collective-permute-start.19 = (bf16[512,384]{1,0:T(8,128)(2,1)S(1)}, bf16[512,384]{1,0:T(8,128)(2,1)S(1)}, u32[]{:S(2)}, u32[]{:S(2)}) collective-permute-start(bf16[512,384]{1,0:T(8,128)(2,1)S(1)} %fusion.44.refs_0_.refs_4_), channel_id=1, source_target_pairs={{0,2},{1,3},{2,0},{3,1},{4,6},{5,7},{6,4},{7,5},{8,10},{9,11},{10,... | collective-permute-start | bytes 1179656 | tf_op jit(solution)/shard_map/ppermute | solution.py:21
  118.1 23.9 %collective-permute-start.20 = (bf16[512,384]{1,0:T(8,128)(2,1)S(1)}, bf16[512,384]{1,0:T(8,128)(2,1)S(1)}, u32[]{:S(2)}, u32[]{:S(2)}) collective-permute-start(bf16[512,384]{1,0:T(8,128)(2,1)S(1)} %fusion.44.refs_0_.refs_4_), channel_id=1, source_target_pairs={{0,1},{1,2},{2,3},{3,0},{4,5},{5,6},{6,7},{7,4},{8,9},{9,10},{10,1... | collective-permute-start | bytes 1179656 | tf_op jit(solution)/shard_map/ppermute | solution.py:21
  136.9 25.2 %collective-permute-start.25 = (bf16[512,384]{1,0:T(8,128)(2,1)}, bf16[512,384]{1,0:T(8,128)(2,1)}, u32[]{:S(2)}, u32[]{:S(2)}) collective-permute-start(bf16[512,384]{1,0:T(8,128)(2,1)} %collective-permute-done.24.refs_0_), channel_id=1, source_target_pairs={{0,3},{1,0},{2,1},{3,2},{4,7},{5,4},{6,5},{7,6},{8,11},{9,8},{10,9... | collective-permute-start | bytes 1179656 | tf_op jit(solution)/shard_map/ppermute | solution.py:21
  137.2 26.2 %collective-permute-start.26 = (bf16[512,384]{1,0:T(8,128)(2,1)}, bf16[512,384]{1,0:T(8,128)(2,1)}, u32[]{:S(2)}, u32[]{:S(2)}) collective-permute-start(bf16[512,384]{1,0:T(8,128)(2,1)} %collective-permute-done.24.refs_0_), channel_id=1, source_target_pairs={{0,2},{1,3},{2,0},{3,1},{4,6},{5,7},{6,4},{7,5},{8,10},{9,11},{10,... | collective-permute-start | bytes 1179656 | tf_op jit(solution)/shard_map/ppermute | solution.py:21
  140.2 23.3 %collective-permute-start.27 = (bf16[512,384]{1,0:T(8,128)(2,1)}, bf16[512,384]{1,0:T(8,128)(2,1)}, u32[]{:S(2)}, u32[]{:S(2)}) collective-permute-start(bf16[512,384]{1,0:T(8,128)(2,1)} %collective-permute-done.24.refs_0_), channel_id=1, source_target_pairs={{0,1},{1,2},{2,3},{3,0},{4,5},{5,6},{6,7},{7,4},{8,9},{9,10},{10,1... | collective-permute-start | bytes 1179656 | tf_op jit(solution)/shard_map/ppermute | solution.py:21
  157.9 20.9 %collective-permute-start.21 = (bf16[512,384]{1,0:T(8,128)(2,1)S(1)}, bf16[512,384]{1,0:T(8,128)(2,1)S(1)}, u32[]{:S(2)}, u32[]{:S(2)}) collective-permute-start(bf16[512,384]{1,0:T(8,128)(2,1)S(1)} %get-tuple-element.153), channel_id=1, source_target_pairs={{0,3},{1,0},{2,1},{3,2},{4,7},{5,4},{6,5},{7,6},{8,11},{9,8},{10,9... | collective-permute-start | bytes 1179656 | tf_op jit(solution)/shard_map/ppermute | solution.py:21
  180.0 26.0 %collective-permute-start.29 = (bf16[512,384]{1,0:T(8,128)(2,1)S(1)}, bf16[512,384]{1,0:T(8,128)(2,1)}, u32[]{:S(2)}, u32[]{:S(2)}) collective-permute-start(bf16[512,384]{1,0:T(8,128)(2,1)S(1)} %get-tuple-element.166), channel_id=1, source_target_pairs={{0,3},{1,0},{2,1},{3,2},{4,7},{5,4},{6,5},{7,6},{8,11},{9,8},{10,9... | collective-permute-start | bytes 1179656 | tf_op jit(solution)/shard_map/ppermute | solution.py:21
  180.9 25.1 %collective-permute-start.30 = (bf16[512,384]{1,0:T(8,128)(2,1)S(1)}, bf16[512,384]{1,0:T(8,128)(2,1)}, u32[]{:S(2)}, u32[]{:S(2)}) collective-permute-start(bf16[512,384]{1,0:T(8,128)(2,1)S(1)} %get-tuple-element.167), channel_id=1, source_target_pairs={{0,2},{1,3},{2,0},{3,1},{4,6},{5,7},{6,4},{7,5},{8,10},{9,11},{10,... | collective-permute-start | bytes 1179656 | tf_op jit(solution)/shard_map/ppermute | solution.py:21
  182.1 23.9 %collective-permute-start.31 = (bf16[512,384]{1,0:T(8,128)(2,1)S(1)}, bf16[512,384]{1,0:T(8,128)(2,1)}, u32[]{:S(2)}, u32[]{:S(2)}) collective-permute-start(bf16[512,384]{1,0:T(8,128)(2,1)S(1)} %get-tuple-element.168), channel_id=1, source_target_pairs={{0,1},{1,2},{2,3},{3,0},{4,5},{5,6},{6,7},{7,4},{8,9},{9,10},{10,1... | collective-permute-start | bytes 1179656 | tf_op jit(solution)/shard_map/ppermute | solution.py:21
  206.0 25.2 %collective-permute-start.32 = (bf16[1536,896]{1,0:T(8,128)(2,1)}, bf16[1536,896]{1,0:T(8,128)(2,1)}, u32[]{:S(2)}, u32[]{:S(2)}) collective-permute-start(bf16[1536,896]{1,0:T(8,128)(2,1)} %convolution_convert_fusion), channel_id=1, source_target_pairs={{0,8},{8,0},{1,9},{9,1},{2,10},{10,2},{3,11},{11,3},{4,12},{12,4},... | collective-permute-start | bytes 8257544 | tf_op jit(solution)/shard_map/ppermute | solution.py:37
  209.2 20.2 %collective-permute-start.33 = (bf16[4,192,896]{2,1,0:T(8,128)(2,1)}, bf16[4,192,896]{2,1,0:T(8,128)(2,1)}, u32[]{:S(2)}, u32[]{:S(2)}) collective-permute-start(bf16[4,192,896]{2,1,0:T(8,128)(2,1)} %fusion.17), channel_id=1, source_target_pairs={{0,8},{8,0},{1,9},{9,1},{2,10},{10,2},{3,11},{11,3},{4,12},{12,4},... | collective-permute-start | bytes 4128776 | tf_op jit(solution)/shard_map/ppermute | solution.py:37
  224.8 18.7 %collective-permute-start.35 = (bf16[512,384]{1,0:T(8,128)(2,1)S(1)}, bf16[512,384]{1,0:T(8,128)(2,1)S(1)}, u32[]{:S(2)}, u32[]{:S(2)}) collective-permute-start(bf16[512,384]{1,0:T(8,128)(2,1)S(1)} %get-tuple-element.189.refs_0_), channel_id=1, source_target_pairs={{0,3},{1,0},{2,1},{3,2},{4,7},{5,4},{6,5},{7,6},{8,11},{9,8},{10,9... | collective-permute-start | bytes 1179656 | tf_op jit(solution)/shard_map/ppermute | solution.py:21
  228.3 18.8 %collective-permute-start.37 = (bf16[512,384]{1,0:T(8,128)(2,1)S(1)}, bf16[512,384]{1,0:T(8,128)(2,1)S(1)}, u32[]{:S(2)}, u32[]{:S(2)}) collective-permute-start(bf16[512,384]{1,0:T(8,128)(2,1)S(1)} %get-tuple-element.189.refs_0_), channel_id=1, source_target_pairs={{0,1},{1,2},{2,3},{3,0},{4,5},{5,6},{6,7},{7,4},{8,9},{9,10},{10,1... | collective-permute-start | bytes 1179656 | tf_op jit(solution)/shard_map/ppermute | solution.py:21
  247.9 62.2 %all-to-all-start = ((bf16[32,72,896]{2,1,0:T(8,128)(2,1)}), bf16[32,72,896]{2,1,0:T(8,128)(2,1)}, u32[]{:S(2)}, u32[]{:S(2)}) async-start(bf16[32,72,896]{2,1,0:T(8,128)(2,1)} %bitcast.188), calls=%async_computation | async-start | bytes 8257536 | tf_op jit(solution)/shard_map/all_to_all | solution.py:685
  257.1 215.7 %all-gather.15.cloned.1.call-start = ((), (), s32[]{:S(2)}) async-start(), calls=%async_computation.5 | async-start | bytes 8957952 | tf_op jit(solution)/shard_map/all_gather | solution.py:730
  310.0 36.7 %collective-permute-start.39 = (bf16[2,4,192,896]{3,2,0,1:T(8,128)(2,1)}, bf16[2,4,192,896]{3,2,0,1:T(8,128)(2,1)}, u32[]{:S(2)}, u32[]{:S(2)}) collective-permute-start(bf16[2,4,192,896]{3,2,0,1:T(8,128)(2,1)} %pad_maximum_fusion), channel_id=1, source_target_pairs={{0,8},{8,0},{1,9},{9,1},{2,10},{10,2},{3,11},{11,3},{4,12},{12,4},... | collective-permute-start | bytes 8257544 | tf_op jit(solution)/shard_map/ppermute | solution.py:37
  320.3 25.2 %collective-permute-start.43 = (bf16[72,3456]{1,0:T(8,128)(2,1)S(1)}, bf16[72,3456]{1,0:T(8,128)(2,1)S(1)}, u32[]{:S(2)}, u32[]{:S(2)}) collective-permute-start(bf16[72,3456]{1,0:T(8,128)(2,1)S(1)} %get-tuple-element.302), channel_id=1, source_target_pairs={{0,64},{64,0},{1,65},{65,1},{2,66},{66,2},{3,67},{67,3},{4,68},{68... | collective-permute-start | bytes 1493000 | tf_op jit(solution)/shard_map/ppermute | solution.py:168
  330.8 31.5 %collective-permute-start.40 = (bf16[528,384]{1,0:T(8,128)(2,1)S(1)}, bf16[528,384]{1,0:T(8,128)(2,1)S(1)}, u32[]{:S(2)}, u32[]{:S(2)}) collective-permute-start(bf16[528,384]{1,0:T(8,128)(2,1)S(1)} %get-tuple-element.221), channel_id=1, source_target_pairs={{0,3},{1,0},{2,1},{3,2},{4,7},{5,4},{6,5},{7,6},{8,11},{9,8},{10,9... | collective-permute-start | bytes 1216520 | tf_op jit(solution)/shard_map/ppermute | solution.py:21
  344.6 21.1 %collective-permute-start.42 = (bf16[528,384]{1,0:T(8,128)(2,1)S(1)}, bf16[528,384]{1,0:T(8,128)(2,1)S(1)}, u32[]{:S(2)}, u32[]{:S(2)}) collective-permute-start(bf16[528,384]{1,0:T(8,128)(2,1)S(1)} %get-tuple-element.223), channel_id=1, source_target_pairs={{0,1},{1,2},{2,3},{3,0},{4,5},{5,6},{6,7},{7,4},{8,9},{9,10},{10,1... | collective-permute-start | bytes 1216520 | tf_op jit(solution)/shard_map/ppermute | solution.py:21
  372.7 68.6 %all-to-all-start.1 = ((bf16[64,24,896]{2,1,0:T(8,128)(2,1)}), bf16[64,24,896]{2,1,0:T(8,128)(2,1)}, u32[]{:S(2)}, u32[]{:S(2)}) async-start(bf16[64,24,896]{2,1,0:T(8,128)(2,1)} %bitcast.189), calls=%async_computation.1 | async-start | bytes 5505024 | tf_op jit(solution)/shard_map/all_to_all | solution.py:733
  378.3 105.7 %all-gather.13.cloned.1.call-start = ((), (), s32[]{:S(2)}) async-start(), calls=%async_computation.4 | async-start | bytes 3096576 | tf_op jit(solution)/shard_map/all_gather | solution.py:751
  382.0 71.2 %collective-permute-start.45 = (bf16[2,512,384]{2,1,0:T(8,128)(2,1)}, bf16[2,512,384]{2,1,0:T(8,128)(2,1)S(1)}, u32[]{:S(2)}, u32[]{:S(2)}) collective-permute-start(bf16[2,512,384]{2,1,0:T(8,128)(2,1)} %get-tuple-element.269), channel_id=1, source_target_pairs={{0,3},{1,0},{2,1},{3,2},{4,7},{5,4},{6,5},{7,6},{8,11},{9,8},{10,9... | collective-permute-start | bytes 2359304 | tf_op jit(solution)/shard_map/ppermute | solution.py:21
  384.6 68.6 %collective-permute-start.46 = (bf16[2,512,384]{2,1,0:T(8,128)(2,1)}, bf16[2,512,384]{2,1,0:T(8,128)(2,1)S(1)}, u32[]{:S(2)}, u32[]{:S(2)}) collective-permute-start(bf16[2,512,384]{2,1,0:T(8,128)(2,1)} %get-tuple-element.268), channel_id=1, source_target_pairs={{0,2},{1,3},{2,0},{3,1},{4,6},{5,7},{6,4},{7,5},{8,10},{9,11},{10,... | collective-permute-start | bytes 2359304 | tf_op jit(solution)/shard_map/ppermute | solution.py:21
  385.5 67.7 %collective-permute-start.47 = (bf16[2,512,384]{2,1,0:T(8,128)(2,1)}, bf16[2,512,384]{2,1,0:T(8,128)(2,1)S(1)}, u32[]{:S(2)}, u32[]{:S(2)}) collective-permute-start(bf16[2,512,384]{2,1,0:T(8,128)(2,1)} %get-tuple-element.267), channel_id=1, source_target_pairs={{0,1},{1,2},{2,3},{3,0},{4,5},{5,6},{6,7},{7,4},{8,9},{9,10},{10,1... | collective-permute-start | bytes 2359304 | tf_op jit(solution)/shard_map/ppermute | solution.py:21
  (97 other events, 1185.1 us)
Sparse Core Ops, SparseCore 0:
  29.4 37.1 all-gather.8
  68.9 49.1 all-gather.10
  369.2 71.0 all-gather.14
  453.4 25.6 all-gather.12

commit v4 on v3

--- a/solution.py
+++ b/solution.py
@@ -715,12 +715,11 @@
         return jnp.stack(halves)
 
     theirs = tail_half(1 - k)
-    theirs, ffn, one_parts, block_parts = lax.optimization_barrier(
-        (theirs, ffn, one_parts, block_parts)
-    )
     one_terms = yexchange(lambda j: one_parts[j])
+    theirs, ffn, one_terms, block_parts = lax.optimization_barrier(
+        (theirs, ffn, one_terms, block_parts)
+    )
     mixer = tail_half(k) + kswap(theirs.astype(bf16)).astype(f32)
-    mixer, one_terms = lax.optimization_barrier((mixer, one_terms))
     cols = list(jnp.sum(ffn.reshape(8, 4, 72, FB).astype(f32), axis=0).astype(bf16))
     part = jnp.concatenate(cols[:3] + [cols[3][:, 128:]], axis=1)
     part = gather_zh(part, zh)
@@ -746,7 +745,11 @@
     part = gather_zh(cols, zh)
     part, block_terms = lax.optimization_barrier((part, block_terms))
     block_sum = total_of(block_terms)
-    block_out = stream_own + block_sum[0] + zswap(block_sum[1].astype(bf16)).astype(f32)
+    from_other = zswap(block_sum[1].astype(bf16))
+    from_other, gate_up_out, down_out = lax.optimization_barrier(
+        (from_other, gate_up_out, down_out)
+    )
+    block_out = stream_own + block_sum[0] + from_other.astype(f32)
     block_out = block_out.astype(bf16)
     full = lax.all_gather(part, ("k", "x"))
     full, gate_up_out, down_out, in_grad, block_out = lax.optimization_barrier(

time: 506 us -> 501 us (level)
  waiting for transfers between devices: 186 us -> 170 us
  starting transfers between devices: 86.8 us -> 99.7 us
    ppermute x36, starting transfers between devices: 50.4 us -> 61.1 us  [yshift(): return lax.ppermute(v, 'y', [(i, (i + d) % 4) for i in range(4)])]
    all_to_all x1, waiting for transfers between devices: 9.16 us -> 0.01 us  [body(): ffn = lax.all_to_all(ffn, ('zh', 'x', 'y'), 0, 0, tiled=True)]
    ppermute x36, waiting for transfers between devices: 74.7 us -> 65.8 us  [yshift(): return lax.ppermute(v, 'y', [(i, (i + d) % 4) for i in range(4)])]
    ppermute x5, waiting for transfers between devices: 35.1 us -> 26.8 us  [zswap(): return lax.ppermute(v, 'zl', [(0, 1), (1, 0)])]
    ppermute x2, waiting for transfers between devices: 5.54 us -> 11.8 us  [gather_zh(): other = lax.ppermute(part, 'zh', [(0, 1), (1, 0)])]
    unnamed x152 -> x162, local copies, waits for them, and re-layouts: 22.9 us -> 24.1 us
  transfers between devices with their start and end apart: 55 -> 55, of which waited for: 27 -> 27; matrix products, arithmetic and copies ran while one was open for 20% -> 18% of each run, Pallas kernels for 16% -> 16%
where the time goes in v4:
time: 501 us; the launch traced here: 491 us
  waiting for transfers between devices  170 us (34%)
  starting transfers between devices  99.7 us (20%)
  Pallas kernels  83.2 us (17%)
  local copies, waits for them, and re-layouts  62.1 us (12%)
  other arithmetic  36.7 us (7%)
  matrix products  24.4 us (5%)
  between operations  15.6 us (3%)
    ppermute x36, waiting for transfers between devices, yshift(): return lax.ppermute(v, 'y', [(i, (i + d) % 4) for i in range(4)])  65.8 us
    ppermute x36, starting transfers between devices, yshift(): return lax.ppermute(v, 'y', [(i, (i + d) % 4) for i in range(4)])  61.1 us
    all_to_all x1, waiting for transfers between devices, body(): lax.all_to_all(mixer.reshape(64, 24, FB), ('zh', 'x', 'zl', 'y'), 0, 0, t...  55.1 us
    pallas_call x2, Pallas kernels, ffn_call(): pl.pallas_call(ffn_kernel, grid=(2,), in_specs=[narrow] * 8 + [pl.BlockSp...  28.1 us
    ppermute x5, waiting for transfers between devices, zswap(): return lax.ppermute(v, 'zl', [(0, 1), (1, 0)])  26.8 us
    dot_general x7, matrix products, t_dot(): lax.dot_general(a, b, (((0,), (0,)), ((), ())), preferred_element_type=f32)  24.4 us
    unnamed x162, local copies, waits for them, and re-layouts  24.1 us
    pallas_call x1, Pallas kernels, back_call(): pl.pallas_call(kernel, in_specs=[whole] * 15 + [pl.BlockSpec(memory_space...  13.2 us
  transfers between devices with their start and end apart: 55, of which 27 were waited for; matrix products, arithmetic and copies ran while one was open for 18% of the time, Pallas kernels for 16%

profile of v4, /device:TPU:0, one launch (start us, length us, event | category | flops | bytes accessed | tf_op | source)
XLA Modules:
  0.0 491.5 jit_solution(4231196858243301438)
XLA Ops:
  21.0 4.1 collective-permute-start.11
  36.2 5.8 %collective-permute-done.refs_2_.refs_1_ = bf16[528,384]{1,0:T(8,128)(2,1)S(1)} collective-permute-done((bf16[528,384]{1,0:T(8,128)(2,1)S(1)}, bf16[528,384]{1,0:T(8,128)(2,1)S(1)}, u32[]{:S(2)}, u32[]{:S(2)}) %collective-permute-start) | collective-permute-done | bytes 405536 | tf_op jit(solution)/shard_map/ppermute | solution.py:21
  43.9 5.7 %collective-permute-done.2.refs_4_.refs_3_ = bf16[528,384]{1,0:T(8,128)(2,1)} collective-permute-done((bf16[528,384]{1,0:T(8,128)(2,1)S(1)}, bf16[528,384]{1,0:T(8,128)(2,1)}, u32[]{:S(2)}, u32[]{:S(2)}) %collective-permute-start.2) | collective-permute-done | bytes 405536 | tf_op jit(solution)/shard_map/ppermute | solution.py:21
  54.3 4.6 collective-permute-done.3
  61.6 3.5 collective-permute-done.5
  68.6 12.1 %mixer.1 = (bf16[512,1536]{1,0:T(8,128)(2,1)}, f32[512,1]{1,0:T(8,128)S(1)}, f32[512,576]{1,0:T(8,128)}, f32[512,576]{1,0:T(8,128)}, f32[512,192]{1,0:T(8,128)},...) custom-call(s32[1]{0:T(128)} %bitcast.refs_0_, ...), custom_call_target="tpu_custom_call" | custom-call | flops 1000000 | bytes 1000000 | tf_op jit(solution)/shard_map/mixer/pallas_call | solution.py:255
  81.0 6.6 %collective-permute-done.14.refs_7_.refs_11_ = bf16[512,384]{1,0:T(8,128)(2,1)} collective-permute-done((bf16[512,384]{1,0:T(8,128)(2,1)S(1)}, bf16[512,384]{1,0:T(8,128)(2,1)}, u32[]{:S(2)}, u32[]{:S(2)}) %collective-permute-start.14) | collective-permute-done | bytes 393248 | tf_op jit(solution)/shard_map/ppermute | solution.py:21
  94.9 10.0 %collective-permute-done.15 = bf16[512,384]{1,0:T(8,128)(2,1)S(1)} collective-permute-done((bf16[512,384]{1,0:T(8,128)(2,1)S(1)}, bf16[512,384]{1,0:T(8,128)(2,1)S(1)}, u32[]{:S(2)}, u32[]{:S(2)}) %collective-permute-start.15) | collective-permute-done | bytes 393248 | tf_op jit(solution)/shard_map/ppermute | solution.py:21
  107.4 6.1 %collective-permute-done.17 = bf16[512,384]{1,0:T(8,128)(2,1)S(1)} collective-permute-done((bf16[512,384]{1,0:T(8,128)(2,1)S(1)}, bf16[512,384]{1,0:T(8,128)(2,1)S(1)}, u32[]{:S(2)}, u32[]{:S(2)}) %collective-permute-start.17) | collective-permute-done | bytes 393248 | tf_op jit(solution)/shard_map/ppermute | solution.py:21
  119.0 18.0 %collective-permute-done.24.refs_0_ = bf16[512,384]{1,0:T(8,128)(2,1)} collective-permute-done((bf16[512,384]{1,0:T(8,128)(2,1)S(1)}, bf16[512,384]{1,0:T(8,128)(2,1)}, u32[]{:S(2)}, u32[]{:S(2)}) %collective-permute-start.24) | collective-permute-done | bytes 393248 | tf_op jit(solution)/shard_map/ppermute | solution.py:33
  143.8 14.1 %ffn.2 = (bf16[512,1536]{1,0:T(8,128)(2,1)}, bf16[512,896]{1,0:T(8,128)(2,1)}, bf16[512,896]{1,0:T(8,128)(2,1)}, bf16[512,896]{1,0:T(8,128)(2,1)}, f32[512,384]{...) custom-call(bf16[512,384]{1,0:T(8,128)(2,1)S(1)} %fusion.44.refs_0_.refs_4_, ...), custom_call_target="tpu_custom_call" | custom-call | flops 8400000000 | bytes 16000000 | tf_op jit(solution)/shard_map/ffn/pallas_call | solution.py:535
  163.5 14.0 %ffn.3 = (bf16[512,1536]{1,0:T(8,128)(2,1)}, bf16[512,896]{1,0:T(8,128)(2,1)}, bf16[512,896]{1,0:T(8,128)(2,1)}, bf16[512,896]{1,0:T(8,128)(2,1)}, f32[512,384]{...) custom-call(bf16[512,384]{1,0:T(8,128)(2,1)} %collective-permute-done.24.refs, ...), custom_call_target="tpu_custom_call" | custom-call | flops 8400000000 | bytes 16000000 | tf_op jit(solution)/shard_map/ffn/pallas_call | solution.py:535
  183.1 9.2 %block.1 = bf16[4,2,512,384]{3,2,1,0:T(8,128)(2,1)} custom-call(bf16[512,896]{1,0:T(8,128)(2,1)S(1)} %copy-done.5, bf16[512,896]{1,0:T(8,128)(2,1)S(1)} %copy-done.6, bf16[8,4,48,2688]{3,2,1,0:T(8,128)(2,1)} %bitcast.193), custom_call_target="tpu_custom_call" | custom-call | flops 2800000000 | bytes 10000000 | tf_op jit(solution)/shard_map/block/pallas_call | solution.py:564
  193.8 4.8 convolution_convert_fusion
  198.7 7.3 %fusion.3 = f32[1536,896]{1,0:T(8,128)} fusion(bf16[512,1536]{1,0:T(8,128)(2,1)} %collective-permute-done.28, bf16[512,1536]{1,0:T(8,128)(2,1)} %constant_dynamic-update-slice_fusion, bf16[512,896]{1,0:T(8,128)(2,1)S(1)} %copy-done.6, bf16[512,896]{1,0:T(8,128)(2,1)S(1)} %copy-done.5), kind=kOutput, calls=%fused_computation.20 | convolution fusion | flops 2828533760 | bytes 10485760 | tf_op jit(solution)/shard_map/dot_general | solution.py:77
  213.8 8.8 %collective-permute-done.34 = bf16[512,384]{1,0:T(8,128)(2,1)S(1)} collective-permute-done((bf16[512,384]{1,0:T(8,128)(2,1)S(1)}, bf16[512,384]{1,0:T(8,128)(2,1)S(1)}, u32[]{:S(2)}, u32[]{:S(2)}) %collective-permute-start.34) | collective-permute-done | bytes 393248 | tf_op jit(solution)/shard_map/ppermute | solution.py:33
  231.1 5.1 %add_convert_fusion = bf16[1536,896]{1,0:T(8,128)(2,1)S(1)} fusion(bf16[1536,896]{1,0:T(8,128)(2,1)} %collective-permute-done.32, bf16[1024,1536]{1,0:T(8,128)(2,1)S(1)} %copy-done.64, bf16[512,896]{1,0:T(8,128)(2,1)S(1)} %broadcast_select_fusion, bf16[512,896]{1,0:T(8,128)(2,1)S(1)} %broadcast_select_fusion.1), kind=kOutput, calls=%fused_computation.9 | convolution fusion | flops 2826371072 | bytes 10485760 | tf_op jit(solution)/shard_map/dot_general | solution.py:77
  239.6 3.8 collective-permute-done.35.refs_1_
  247.9 9.2 %all-to-all-start = ((bf16[32,72,896]{2,1,0:T(8,128)(2,1)}), bf16[32,72,896]{2,1,0:T(8,128)(2,1)}, u32[]{:S(2)}, u32[]{:S(2)}) async-start(bf16[32,72,896]{2,1,0:T(8,128)(2,1)} %bitcast.188), calls=%async_computation | async-start | bytes 8257536 | tf_op jit(solution)/shard_map/all_to_all | solution.py:685
  261.4 6.3 %stream.1 = (bf16[512,1536]{1,0:T(8,128)(2,1)}, f32[512,192]{1,0:T(8,128)}, f32[512,192]{1,0:T(8,128)}, f32[2,8,192]{2,1,0:T(8,128)S(1)}, f32[512,384]{1,0:T(8,128)}, /*index=5*/f32[1,384]{1,0:T(1,128)S(1)}) custom-call(bf16[512,384]{1,0:T(8,128)(2,1)S(1)} %get-tuple-element.187.refs_0_, bf16[512,384]{1,0:T(8,128)(2,1)S(1)} %copy-done.15, ...), custom_call_target="tpu_custom_call" | custom-call | flops 1000000 | bytes 1000000 | tf_op jit(solution)/shard_map/stream/pallas_call | solution.py:304
  272.7 3.7 collective-permute-done.38.refs_12_
  276.3 13.2 %back.1 = (bf16[512,640]{1,0:T(8,128)(2,1)}, bf16[512,640]{1,0:T(8,128)(2,1)}, f32[528,384]{1,0:T(8,128)}, bf16[528,384]{1,0:T(8,128)(2,1)S(1)}, bf16[528,384]{1...) custom-call(bf16[528,384]{1,0:T(8,128)(2,1)S(1)} %maximum_maximum_fu, ...), custom_call_target="tpu_custom_call" | custom-call | flops 1000000 | bytes 1000000 | tf_op jit(solution)/shard_map/back/pallas_call | solution.py:404
  291.8 24.1 %collective-permute-start.39 = (bf16[528,384]{1,0:T(8,128)(2,1)S(1)}, bf16[528,384]{1,0:T(8,128)(2,1)S(1)}, u32[]{:S(2)}, u32[]{:S(2)}) collective-permute-start(bf16[528,384]{1,0:T(8,128)(2,1)S(1)} %get-tuple-element.213), channel_id=1, source_target_pairs={{0,3},{1,0},{2,1},{3,2},{4,7},{5,4},{6,5},{7,6},{8,11},{9,8},{10,9... | collective-permute-start | bytes 1216520 | tf_op jit(solution)/shard_map/ppermute | solution.py:21
  342.6 3.8 collective-permute-start.43
  351.5 6.9 %collective-permute-done.43 = bf16[72,3456]{1,0:T(8,128)(2,1)S(1)} collective-permute-done((bf16[72,3456]{1,0:T(8,128)(2,1)S(1)}, bf16[72,3456]{1,0:T(8,128)(2,1)S(1)}, u32[]{:S(2)}, u32[]{:S(2)}) %collective-permute-start.43) | collective-permute-done | bytes 497696 | tf_op jit(solution)/shard_map/ppermute | solution.py:168
  359.7 4.1 maximum_add_fusion
  366.7 3.6 copy.59
  370.3 8.0 %all-to-all-start.1 = ((bf16[64,24,896]{2,1,0:T(8,128)(2,1)}), bf16[64,24,896]{2,1,0:T(8,128)(2,1)}, u32[]{:S(2)}, u32[]{:S(2)}) async-start(bf16[64,24,896]{2,1,0:T(8,128)(2,1)} %bitcast.189), calls=%async_computation.1 | async-start | bytes 5505024 | tf_op jit(solution)/shard_map/all_to_all | solution.py:732
  386.2 55.1 %all-to-all-done.1 = bf16[64,24,896]{2,1,0:T(8,128)(2,1)} async-done(((bf16[64,24,896]{2,1,0:T(8,128)(2,1)}), bf16[64,24,896]{2,1,0:T(8,128)(2,1)}, u32[]{:S(2)}, u32[]{:S(2)}) %all-to-all-start.1) | async-done | bytes 2752544 | tf_op jit(solution)/shard_map/all_to_all | solution.py:732
  445.7 4.9 collective-permute-done.44
  459.0 11.6 %ffn_finish.1 = (f32[2,384,3456]{2,1,0:T(8,128)}, f32[3456,384]{1,0:T(8,128)}) custom-call(bf16[8,2,72,3456]{3,2,1,0:T(8,128)(2,1)} %bitcast.194), custom_call_target="tpu_custom_call" | custom-call | tf_op jit(solution)/shard_map/ffn_finish/pallas_call | solution.py:426
  474.1 3.4 all-gather.13.cloned.1.call-done
  (370 shorter events, 174.4 us)
Async XLA Ops:
  7.2 61.4 %all-gather.9.cloned.1.call-start = ((), (), s32[]{:S(2)}) async-start(), calls=%async_computation.2 | async-start | bytes 6193152 | tf_op jit(solution)/shard_map/all_gather | solution.py:622
  29.3 113.5 %all-gather.11.cloned.1.call-start = ((), (), s32[]{:S(2)}) async-start(), calls=%async_computation.3 | async-start | bytes 9289728 | tf_op jit(solution)/shard_map/all_gather | solution.py:628
  30.6 19.0 %collective-permute-start.2 = (bf16[528,384]{1,0:T(8,128)(2,1)S(1)}, bf16[528,384]{1,0:T(8,128)(2,1)}, u32[]{:S(2)}, u32[]{:S(2)}) collective-permute-start(bf16[528,384]{1,0:T(8,128)(2,1)S(1)} %maximum_maximum_fusion.refs_1_.refs_0_), channel_id=1, source_target_pairs={{0,1},{1,2},{2,3},{3,0},{4,5},{5,6},{6,7},{7,4},{8,9},{9,10},{10,1... | collective-permute-start | bytes 1216520 | tf_op jit(solution)/shard_map/ppermute | solution.py:21
  67.6 20.0 %collective-permute-start.14 = (bf16[512,384]{1,0:T(8,128)(2,1)S(1)}, bf16[512,384]{1,0:T(8,128)(2,1)}, u32[]{:S(2)}, u32[]{:S(2)}) collective-permute-start(bf16[512,384]{1,0:T(8,128)(2,1)S(1)} %copy-done.3), channel_id=1, source_target_pairs={{0,1},{1,2},{2,3},{3,0},{4,5},{5,6},{6,7},{7,4},{8,9},{9,10},{10,1... | collective-permute-start | bytes 1179656 | tf_op jit(solution)/shard_map/ppermute | solution.py:21
  91.9 45.3 %collective-permute-start.28 = (bf16[512,1536]{1,0:T(8,128)(2,1)}, bf16[512,1536]{1,0:T(8,128)(2,1)}, u32[]{:S(2)}, u32[]{:S(2)}) collective-permute-start(bf16[512,1536]{1,0:T(8,128)(2,1)} %constant_dynamic-update-slice_fusion), channel_id=1, source_target_pairs={{0,4},{4,0},{1,5},{5,1},{2,6},{6,2},{3,7},{7,3},{8,12},{12,8},{9,1... | collective-permute-start | bytes 4718600 | tf_op jit(solution)/shard_map/ppermute | solution.py:33
  93.9 19.6 %collective-permute-start.17 = (bf16[512,384]{1,0:T(8,128)(2,1)S(1)}, bf16[512,384]{1,0:T(8,128)(2,1)S(1)}, u32[]{:S(2)}, u32[]{:S(2)}) collective-permute-start(bf16[512,384]{1,0:T(8,128)(2,1)S(1)} %get-tuple-element.143), channel_id=1, source_target_pairs={{0,1},{1,2},{2,3},{3,0},{4,5},{5,6},{6,7},{7,4},{8,9},{9,10},{10,1... | collective-permute-start | bytes 1179656 | tf_op jit(solution)/shard_map/ppermute | solution.py:21
  114.3 22.7 %collective-permute-start.24 = (bf16[512,384]{1,0:T(8,128)(2,1)S(1)}, bf16[512,384]{1,0:T(8,128)(2,1)}, u32[]{:S(2)}, u32[]{:S(2)}) collective-permute-start(bf16[512,384]{1,0:T(8,128)(2,1)S(1)} %fusion.44.refs_0_.refs_4_), channel_id=1, source_target_pairs={{0,4},{4,0},{1,5},{5,1},{2,6},{6,2},{3,7},{7,3},{8,12},{12,8},{9,1... | collective-permute-start | bytes 1179656 | tf_op jit(solution)/shard_map/ppermute | solution.py:33
  116.8 23.4 %collective-permute-start.18 = (bf16[512,384]{1,0:T(8,128)(2,1)S(1)}, bf16[512,384]{1,0:T(8,128)(2,1)S(1)}, u32[]{:S(2)}, u32[]{:S(2)}) collective-permute-start(bf16[512,384]{1,0:T(8,128)(2,1)S(1)} %fusion.44.refs_0_.refs_4_), channel_id=1, source_target_pairs={{0,3},{1,0},{2,1},{3,2},{4,7},{5,4},{6,5},{7,6},{8,11},{9,8},{10,9... | collective-permute-start | bytes 1179656 | tf_op jit(solution)/shard_map/ppermute | solution.py:21
  118.1 23.9 %collective-permute-start.19 = (bf16[512,384]{1,0:T(8,128)(2,1)S(1)}, bf16[512,384]{1,0:T(8,128)(2,1)S(1)}, u32[]{:S(2)}, u32[]{:S(2)}) collective-permute-start(bf16[512,384]{1,0:T(8,128)(2,1)S(1)} %fusion.44.refs_0_.refs_4_), channel_id=1, source_target_pairs={{0,2},{1,3},{2,0},{3,1},{4,6},{5,7},{6,4},{7,5},{8,10},{9,11},{10,... | collective-permute-start | bytes 1179656 | tf_op jit(solution)/shard_map/ppermute | solution.py:21
  118.1 23.9 %collective-permute-start.20 = (bf16[512,384]{1,0:T(8,128)(2,1)S(1)}, bf16[512,384]{1,0:T(8,128)(2,1)S(1)}, u32[]{:S(2)}, u32[]{:S(2)}) collective-permute-start(bf16[512,384]{1,0:T(8,128)(2,1)S(1)} %fusion.44.refs_0_.refs_4_), channel_id=1, source_target_pairs={{0,1},{1,2},{2,3},{3,0},{4,5},{5,6},{6,7},{7,4},{8,9},{9,10},{10,1... | collective-permute-start | bytes 1179656 | tf_op jit(solution)/shard_map/ppermute | solution.py:21
  137.0 25.1 %collective-permute-start.25 = (bf16[512,384]{1,0:T(8,128)(2,1)}, bf16[512,384]{1,0:T(8,128)(2,1)}, u32[]{:S(2)}, u32[]{:S(2)}) collective-permute-start(bf16[512,384]{1,0:T(8,128)(2,1)} %collective-permute-done.24.refs_0_), channel_id=1, source_target_pairs={{0,3},{1,0},{2,1},{3,2},{4,7},{5,4},{6,5},{7,6},{8,11},{9,8},{10,9... | collective-permute-start | bytes 1179656 | tf_op jit(solution)/shard_map/ppermute | solution.py:21
  137.2 26.2 %collective-permute-start.26 = (bf16[512,384]{1,0:T(8,128)(2,1)}, bf16[512,384]{1,0:T(8,128)(2,1)}, u32[]{:S(2)}, u32[]{:S(2)}) collective-permute-start(bf16[512,384]{1,0:T(8,128)(2,1)} %collective-permute-done.24.refs_0_), channel_id=1, source_target_pairs={{0,2},{1,3},{2,0},{3,1},{4,6},{5,7},{6,4},{7,5},{8,10},{9,11},{10,... | collective-permute-start | bytes 1179656 | tf_op jit(solution)/shard_map/ppermute | solution.py:21
  140.2 23.2 %collective-permute-start.27 = (bf16[512,384]{1,0:T(8,128)(2,1)}, bf16[512,384]{1,0:T(8,128)(2,1)}, u32[]{:S(2)}, u32[]{:S(2)}) collective-permute-start(bf16[512,384]{1,0:T(8,128)(2,1)} %collective-permute-done.24.refs_0_), channel_id=1, source_target_pairs={{0,1},{1,2},{2,3},{3,0},{4,5},{5,6},{6,7},{7,4},{8,9},{9,10},{10,1... | collective-permute-start | bytes 1179656 | tf_op jit(solution)/shard_map/ppermute | solution.py:21
  157.9 20.9 %collective-permute-start.21 = (bf16[512,384]{1,0:T(8,128)(2,1)S(1)}, bf16[512,384]{1,0:T(8,128)(2,1)S(1)}, u32[]{:S(2)}, u32[]{:S(2)}) collective-permute-start(bf16[512,384]{1,0:T(8,128)(2,1)S(1)} %get-tuple-element.151), channel_id=1, source_target_pairs={{0,3},{1,0},{2,1},{3,2},{4,7},{5,4},{6,5},{7,6},{8,11},{9,8},{10,9... | collective-permute-start | bytes 1179656 | tf_op jit(solution)/shard_map/ppermute | solution.py:21
  160.6 18.3 %collective-permute-start.22 = (bf16[512,384]{1,0:T(8,128)(2,1)S(1)}, bf16[512,384]{1,0:T(8,128)(2,1)S(1)}, u32[]{:S(2)}, u32[]{:S(2)}) collective-permute-start(bf16[512,384]{1,0:T(8,128)(2,1)S(1)} %get-tuple-element.152), channel_id=1, source_target_pairs={{0,2},{1,3},{2,0},{3,1},{4,6},{5,7},{6,4},{7,5},{8,10},{9,11},{10,... | collective-permute-start | bytes 1179656 | tf_op jit(solution)/shard_map/ppermute | solution.py:21
  180.0 26.0 %collective-permute-start.29 = (bf16[512,384]{1,0:T(8,128)(2,1)S(1)}, bf16[512,384]{1,0:T(8,128)(2,1)}, u32[]{:S(2)}, u32[]{:S(2)}) collective-permute-start(bf16[512,384]{1,0:T(8,128)(2,1)S(1)} %get-tuple-element.164), channel_id=1, source_target_pairs={{0,3},{1,0},{2,1},{3,2},{4,7},{5,4},{6,5},{7,6},{8,11},{9,8},{10,9... | collective-permute-start | bytes 1179656 | tf_op jit(solution)/shard_map/ppermute | solution.py:21
  180.9 25.1 %collective-permute-start.30 = (bf16[512,384]{1,0:T(8,128)(2,1)S(1)}, bf16[512,384]{1,0:T(8,128)(2,1)}, u32[]{:S(2)}, u32[]{:S(2)}) collective-permute-start(bf16[512,384]{1,0:T(8,128)(2,1)S(1)} %get-tuple-element.165), channel_id=1, source_target_pairs={{0,2},{1,3},{2,0},{3,1},{4,6},{5,7},{6,4},{7,5},{8,10},{9,11},{10,... | collective-permute-start | bytes 1179656 | tf_op jit(solution)/shard_map/ppermute | solution.py:21
  182.1 23.9 %collective-permute-start.31 = (bf16[512,384]{1,0:T(8,128)(2,1)S(1)}, bf16[512,384]{1,0:T(8,128)(2,1)}, u32[]{:S(2)}, u32[]{:S(2)}) collective-permute-start(bf16[512,384]{1,0:T(8,128)(2,1)S(1)} %get-tuple-element.166), channel_id=1, source_target_pairs={{0,1},{1,2},{2,3},{3,0},{4,5},{5,6},{6,7},{7,4},{8,9},{9,10},{10,1... | collective-permute-start | bytes 1179656 | tf_op jit(solution)/shard_map/ppermute | solution.py:21
  206.0 25.1 %collective-permute-start.32 = (bf16[1536,896]{1,0:T(8,128)(2,1)}, bf16[1536,896]{1,0:T(8,128)(2,1)}, u32[]{:S(2)}, u32[]{:S(2)}) collective-permute-start(bf16[1536,896]{1,0:T(8,128)(2,1)} %convolution_convert_fusion), channel_id=1, source_target_pairs={{0,8},{8,0},{1,9},{9,1},{2,10},{10,2},{3,11},{11,3},{4,12},{12,4},... | collective-permute-start | bytes 8257544 | tf_op jit(solution)/shard_map/ppermute | solution.py:37
  209.2 20.2 %collective-permute-start.33 = (bf16[4,192,896]{2,1,0:T(8,128)(2,1)}, bf16[4,192,896]{2,1,0:T(8,128)(2,1)}, u32[]{:S(2)}, u32[]{:S(2)}) collective-permute-start(bf16[4,192,896]{2,1,0:T(8,128)(2,1)} %fusion.17), channel_id=1, source_target_pairs={{0,8},{8,0},{1,9},{9,1},{2,10},{10,2},{3,11},{11,3},{4,12},{12,4},... | collective-permute-start | bytes 4128776 | tf_op jit(solution)/shard_map/ppermute | solution.py:37
  224.7 18.7 %collective-permute-start.35 = (bf16[512,384]{1,0:T(8,128)(2,1)S(1)}, bf16[512,384]{1,0:T(8,128)(2,1)S(1)}, u32[]{:S(2)}, u32[]{:S(2)}) collective-permute-start(bf16[512,384]{1,0:T(8,128)(2,1)S(1)} %get-tuple-element.187.refs_0_), channel_id=1, source_target_pairs={{0,3},{1,0},{2,1},{3,2},{4,7},{5,4},{6,5},{7,6},{8,11},{9,8},{10,9... | collective-permute-start | bytes 1179656 | tf_op jit(solution)/shard_map/ppermute | solution.py:21
  228.3 18.8 %collective-permute-start.37 = (bf16[512,384]{1,0:T(8,128)(2,1)S(1)}, bf16[512,384]{1,0:T(8,128)(2,1)S(1)}, u32[]{:S(2)}, u32[]{:S(2)}) collective-permute-start(bf16[512,384]{1,0:T(8,128)(2,1)S(1)} %get-tuple-element.187.refs_0_), channel_id=1, source_target_pairs={{0,1},{1,2},{2,3},{3,0},{4,5},{5,6},{6,7},{7,4},{8,9},{9,10},{10,1... | collective-permute-start | bytes 1179656 | tf_op jit(solution)/shard_map/ppermute | solution.py:21
  247.9 86.8 %all-to-all-start = ((bf16[32,72,896]{2,1,0:T(8,128)(2,1)}), bf16[32,72,896]{2,1,0:T(8,128)(2,1)}, u32[]{:S(2)}, u32[]{:S(2)}) async-start(bf16[32,72,896]{2,1,0:T(8,128)(2,1)} %bitcast.188), calls=%async_computation | async-start | bytes 8257536 | tf_op jit(solution)/shard_map/all_to_all | solution.py:685
  257.1 201.8 %all-gather.15.cloned.1.call-start = ((), (), s32[]{:S(2)}) async-start(), calls=%async_computation.5 | async-start | bytes 8957952 | tf_op jit(solution)/shard_map/all_gather | solution.py:729
  291.8 39.1 %collective-permute-start.39 = (bf16[528,384]{1,0:T(8,128)(2,1)S(1)}, bf16[528,384]{1,0:T(8,128)(2,1)S(1)}, u32[]{:S(2)}, u32[]{:S(2)}) collective-permute-start(bf16[528,384]{1,0:T(8,128)(2,1)S(1)} %get-tuple-element.213), channel_id=1, source_target_pairs={{0,3},{1,0},{2,1},{3,2},{4,7},{5,4},{6,5},{7,6},{8,11},{9,8},{10,9... | collective-permute-start | bytes 1216520 | tf_op jit(solution)/shard_map/ppermute | solution.py:21
  315.8 18.8 %collective-permute-start.41 = (bf16[528,384]{1,0:T(8,128)(2,1)S(1)}, bf16[528,384]{1,0:T(8,128)(2,1)}, u32[]{:S(2)}, u32[]{:S(2)}) collective-permute-start(bf16[528,384]{1,0:T(8,128)(2,1)S(1)} %get-tuple-element.215), channel_id=1, source_target_pairs={{0,1},{1,2},{2,3},{3,0},{4,5},{5,6},{6,7},{7,4},{8,9},{9,10},{10,1... | collective-permute-start | bytes 1216520 | tf_op jit(solution)/shard_map/ppermute | solution.py:21
  334.7 25.1 %collective-permute-start.42 = (bf16[2,4,192,896]{3,2,0,1:T(8,128)(2,1)}, bf16[2,4,192,896]{3,2,0,1:T(8,128)(2,1)}, u32[]{:S(2)}, u32[]{:S(2)}) collective-permute-start(bf16[2,4,192,896]{3,2,0,1:T(8,128)(2,1)} %pad_maximum_fusion), channel_id=1, source_target_pairs={{0,8},{8,0},{1,9},{9,1},{2,10},{10,2},{3,11},{11,3},{4,12},{12,4},... | collective-permute-start | bytes 8257544 | tf_op jit(solution)/shard_map/ppermute | solution.py:37
  370.3 71.0 %all-to-all-start.1 = ((bf16[64,24,896]{2,1,0:T(8,128)(2,1)}), bf16[64,24,896]{2,1,0:T(8,128)(2,1)}, u32[]{:S(2)}, u32[]{:S(2)}) async-start(bf16[64,24,896]{2,1,0:T(8,128)(2,1)} %bitcast.189), calls=%async_computation.1 | async-start | bytes 5505024 | tf_op jit(solution)/shard_map/all_to_all | solution.py:732
  378.3 99.2 %all-gather.13.cloned.1.call-start = ((), (), s32[]{:S(2)}) async-start(), calls=%async_computation.4 | async-start | bytes 3096576 | tf_op jit(solution)/shard_map/all_gather | solution.py:754
  381.7 69.7 %collective-permute-start.45 = (bf16[2,512,384]{2,1,0:T(8,128)(2,1)}, bf16[2,512,384]{2,1,0:T(8,128)(2,1)S(1)}, u32[]{:S(2)}, u32[]{:S(2)}) collective-permute-start(bf16[2,512,384]{2,1,0:T(8,128)(2,1)} %get-tuple-element.265), channel_id=1, source_target_pairs={{0,3},{1,0},{2,1},{3,2},{4,7},{5,4},{6,5},{7,6},{8,11},{9,8},{10,9... | collective-permute-start | bytes 2359304 | tf_op jit(solution)/shard_map/ppermute | solution.py:21
  384.5 66.9 %collective-permute-start.46 = (bf16[2,512,384]{2,1,0:T(8,128)(2,1)}, bf16[2,512,384]{2,1,0:T(8,128)(2,1)}, u32[]{:S(2)}, u32[]{:S(2)}) collective-permute-start(bf16[2,512,384]{2,1,0:T(8,128)(2,1)} %get-tuple-element.264), channel_id=1, source_target_pairs={{0,2},{1,3},{2,0},{3,1},{4,6},{5,7},{6,4},{7,5},{8,10},{9,11},{10,... | collective-permute-start | bytes 2359304 | tf_op jit(solution)/shard_map/ppermute | solution.py:21
  385.4 66.1 %collective-permute-start.47 = (bf16[2,512,384]{2,1,0:T(8,128)(2,1)}, bf16[2,512,384]{2,1,0:T(8,128)(2,1)}, u32[]{:S(2)}, u32[]{:S(2)}) collective-permute-start(bf16[2,512,384]{2,1,0:T(8,128)(2,1)} %get-tuple-element.263), channel_id=1, source_target_pairs={{0,1},{1,2},{2,3},{3,0},{4,5},{5,6},{6,7},{7,4},{8,9},{9,10},{10,1... | collective-permute-start | bytes 2359304 | tf_op jit(solution)/shard_map/ppermute | solution.py:21
  (102 other events, 1306.5 us)
Sparse Core Ops, SparseCore 0:
  29.4 37.1 all-gather.8
  68.9 49.1 all-gather.10
  366.8 76.1 all-gather.14
  451.6 25.8 all-gather.12

commit v5 on v4

--- a/solution.py
+++ b/solution.py
@@ -693,7 +693,9 @@
     )
     proj_back = results[:2]
     gain_one_part, *conv_parts = results[6:]
-    one_parts = results[2:6]
+    one_parts = jnp.stack([v.astype(bf16) for v in results[2:6]])
+    one_parts = jnp.stack([pick(one_parts, (b - y) % 4) for b in range(4)])
+    one_sum = lax.psum_scatter(one_parts, "y", scatter_dimension=0, tiled=False)
     tails = []
     for r in range(2):
         taps_part = conv_parts[r].reshape(-1)
@@ -715,11 +717,9 @@
         return jnp.stack(halves)
 
     theirs = tail_half(1 - k)
-    one_terms = yexchange(lambda j: one_parts[j])
-    theirs, ffn, one_terms, block_parts = lax.optimization_barrier(
-        (theirs, ffn, one_terms, block_parts)
-    )
+    theirs, ffn, block_parts = lax.optimization_barrier((theirs, ffn, block_parts))
     mixer = tail_half(k) + kswap(theirs.astype(bf16)).astype(f32)
+    mixer, one_sum = lax.optimization_barrier((mixer, one_sum))
     cols = list(jnp.sum(ffn.reshape(8, 4, 72, FB).astype(f32), axis=0).astype(bf16))
     part = jnp.concatenate(cols[:3] + [cols[3][:, 128:]], axis=1)
     part = gather_zh(part, zh)
@@ -733,7 +733,7 @@
         mixer.reshape(64, 24, FB), ("zh", "x", "zl", "y"), 0, 0, tiled=True
     )
     block_terms = yexchange(lambda j: block_parts[j])
-    one_sum = total_of(one_terms)
+    one_sum = one_sum.astype(f32)
     one_grad = one_sum[:512]
     inner_one = one_sum[512:514].reshape(-1)[:512] + one_sum[514:516].reshape(-1)[:512]
     own_hat = block_in.astype(f32) * inv_one

time: 501 us -> 494 us (0.986)
  starting transfers between devices: 99.7 us -> 89.7 us
    ppermute x36 -> x33, starting transfers between devices: 61.1 us -> 35.9 us  [yshift(): return lax.ppermute(v, 'y', [(i, (i + d) % 4) for i in range(4)])]
    all_to_all x1, starting transfers between devices: 8.01 us -> 19.3 us  [body(): lax.all_to_all(mixer.reshape(64, 24, FB), ('zh', 'x', 'zl', 'y'), 0, 0, t...]
    all_to_all x1, waiting for transfers between devices: 0.01 us -> 7.25 us  [body(): ffn = lax.all_to_all(ffn, ('zh', 'x', 'y'), 0, 0, tiled=True)]
    ppermute x36 -> x33, waiting for transfers between devices: 65.8 us -> 60.6 us  [yshift(): return lax.ppermute(v, 'y', [(i, (i + d) % 4) for i in range(4)])]
    unnamed x162 -> x158, local copies, waits for them, and re-layouts: 24.1 us -> 20.7 us
  transfers between devices with their start and end apart: 55 -> 53, of which waited for: 27 -> 26; matrix products, arithmetic and copies ran while one was open for 18% -> 20% of each run, Pallas kernels for 16% -> 17%
where the time goes in v5:
time: 494 us; the launch traced here: 485 us
  waiting for transfers between devices  171 us (35%)
  starting transfers between devices  89.7 us (18%)
  Pallas kernels  83.1 us (17%)
  local copies, waits for them, and re-layouts  60.8 us (12%)
  other arithmetic  40.1 us (8%)
  matrix products  24.3 us (5%)
  between operations  15.7 us (3%)
    ppermute x33, waiting for transfers between devices, yshift(): return lax.ppermute(v, 'y', [(i, (i + d) % 4) for i in range(4)])  60.6 us
    all_to_all x1, waiting for transfers between devices, body(): lax.all_to_all(mixer.reshape(64, 24, FB), ('zh', 'x', 'zl', 'y'), 0, 0, t...  55.2 us
    ppermute x33, starting transfers between devices, yshift(): return lax.ppermute(v, 'y', [(i, (i + d) % 4) for i in range(4)])  35.9 us
    pallas_call x2, Pallas kernels, ffn_call(): pl.pallas_call(ffn_kernel, grid=(2,), in_specs=[narrow] * 8 + [pl.BlockSp...  28.1 us
    ppermute x5, waiting for transfers between devices, zswap(): return lax.ppermute(v, 'zl', [(0, 1), (1, 0)])  26.8 us
    dot_general x7, matrix products, t_dot(): lax.dot_general(a, b, (((0,), (0,)), ((), ())), preferred_element_type=f32)  24.3 us
    unnamed x158, local copies, waits for them, and re-layouts  20.7 us
    all_to_all x1, starting transfers between devices, body(): lax.all_to_all(mixer.reshape(64, 24, FB), ('zh', 'x', 'zl', 'y'), 0, 0, t...  19.3 us
  transfers between devices with their start and end apart: 53, of which 26 were waited for; matrix products, arithmetic and copies ran while one was open for 20% of the time, Pallas kernels for 17%

profile of v5, /device:TPU:0, one launch (start us, length us, event | category | flops | bytes accessed | tf_op | source)
XLA Modules:
  0.0 485.0 jit_solution(11355786687339102410)
XLA Ops:
  21.0 4.1 collective-permute-start.11
  36.2 5.8 %collective-permute-done.refs_2_.refs_1_ = bf16[528,384]{1,0:T(8,128)(2,1)S(1)} collective-permute-done((bf16[528,384]{1,0:T(8,128)(2,1)S(1)}, bf16[528,384]{1,0:T(8,128)(2,1)S(1)}, u32[]{:S(2)}, u32[]{:S(2)}) %collective-permute-start) | collective-permute-done | bytes 405536 | tf_op jit(solution)/shard_map/ppermute | solution.py:21
  43.9 5.7 %collective-permute-done.2.refs_4_.refs_3_ = bf16[528,384]{1,0:T(8,128)(2,1)} collective-permute-done((bf16[528,384]{1,0:T(8,128)(2,1)S(1)}, bf16[528,384]{1,0:T(8,128)(2,1)}, u32[]{:S(2)}, u32[]{:S(2)}) %collective-permute-start.2) | collective-permute-done | bytes 405536 | tf_op jit(solution)/shard_map/ppermute | solution.py:21
  54.3 4.6 collective-permute-done.3
  61.6 3.5 collective-permute-done.5
  68.6 12.1 %mixer.1 = (bf16[512,1536]{1,0:T(8,128)(2,1)}, f32[512,1]{1,0:T(8,128)S(1)}, f32[512,576]{1,0:T(8,128)}, f32[512,576]{1,0:T(8,128)}, f32[512,192]{1,0:T(8,128)},...) custom-call(s32[1]{0:T(128)} %bitcast.refs_0_, ...), custom_call_target="tpu_custom_call" | custom-call | flops 1000000 | bytes 1000000 | tf_op jit(solution)/shard_map/mixer/pallas_call | solution.py:255
  81.0 6.6 %collective-permute-done.14.refs_7_.refs_11_ = bf16[512,384]{1,0:T(8,128)(2,1)} collective-permute-done((bf16[512,384]{1,0:T(8,128)(2,1)S(1)}, bf16[512,384]{1,0:T(8,128)(2,1)}, u32[]{:S(2)}, u32[]{:S(2)}) %collective-permute-start.14) | collective-permute-done | bytes 393248 | tf_op jit(solution)/shard_map/ppermute | solution.py:21
  94.8 10.0 %collective-permute-done.15 = bf16[512,384]{1,0:T(8,128)(2,1)S(1)} collective-permute-done((bf16[512,384]{1,0:T(8,128)(2,1)S(1)}, bf16[512,384]{1,0:T(8,128)(2,1)S(1)}, u32[]{:S(2)}, u32[]{:S(2)}) %collective-permute-start.15) | collective-permute-done | bytes 393248 | tf_op jit(solution)/shard_map/ppermute | solution.py:21
  107.5 6.1 %collective-permute-done.17 = bf16[512,384]{1,0:T(8,128)(2,1)S(1)} collective-permute-done((bf16[512,384]{1,0:T(8,128)(2,1)S(1)}, bf16[512,384]{1,0:T(8,128)(2,1)S(1)}, u32[]{:S(2)}, u32[]{:S(2)}) %collective-permute-start.17) | collective-permute-done | bytes 393248 | tf_op jit(solution)/shard_map/ppermute | solution.py:21
  119.0 18.0 %collective-permute-done.24.refs_0_ = bf16[512,384]{1,0:T(8,128)(2,1)} collective-permute-done((bf16[512,384]{1,0:T(8,128)(2,1)S(1)}, bf16[512,384]{1,0:T(8,128)(2,1)}, u32[]{:S(2)}, u32[]{:S(2)}) %collective-permute-start.24) | collective-permute-done | bytes 393248 | tf_op jit(solution)/shard_map/ppermute | solution.py:33
  143.8 14.1 %ffn.2 = (bf16[512,1536]{1,0:T(8,128)(2,1)}, bf16[512,896]{1,0:T(8,128)(2,1)}, bf16[512,896]{1,0:T(8,128)(2,1)}, bf16[512,896]{1,0:T(8,128)(2,1)}, f32[512,384]{...) custom-call(bf16[512,384]{1,0:T(8,128)(2,1)S(1)} %fusion.44.refs_0_.refs_4_, ...), custom_call_target="tpu_custom_call" | custom-call | flops 8400000000 | bytes 16000000 | tf_op jit(solution)/shard_map/ffn/pallas_call | solution.py:535
  163.5 14.1 %ffn.3 = (bf16[512,1536]{1,0:T(8,128)(2,1)}, bf16[512,896]{1,0:T(8,128)(2,1)}, bf16[512,896]{1,0:T(8,128)(2,1)}, bf16[512,896]{1,0:T(8,128)(2,1)}, f32[512,384]{...) custom-call(bf16[512,384]{1,0:T(8,128)(2,1)} %collective-permute-done.24.refs, ...), custom_call_target="tpu_custom_call" | custom-call | flops 8400000000 | bytes 16000000 | tf_op jit(solution)/shard_map/ffn/pallas_call | solution.py:535
  183.1 9.2 %block.1 = bf16[4,2,512,384]{3,2,1,0:T(8,128)(2,1)} custom-call(bf16[512,896]{1,0:T(8,128)(2,1)S(1)} %copy-done.5, bf16[512,896]{1,0:T(8,128)(2,1)S(1)} %copy-done.6, bf16[8,4,48,2688]{3,2,1,0:T(8,128)(2,1)} %bitcast.202), custom_call_target="tpu_custom_call" | custom-call | flops 2800000000 | bytes 10000000 | tf_op jit(solution)/shard_map/block/pallas_call | solution.py:564
  193.8 4.8 convolution_convert_fusion
  198.6 7.3 %fusion.3 = f32[1536,896]{1,0:T(8,128)} fusion(bf16[512,1536]{1,0:T(8,128)(2,1)} %collective-permute-done.28, bf16[512,1536]{1,0:T(8,128)(2,1)} %constant_dynamic-update-slice_fusion, bf16[512,896]{1,0:T(8,128)(2,1)S(1)} %copy-done.6, bf16[512,896]{1,0:T(8,128)(2,1)S(1)} %copy-done.5), kind=kOutput, calls=%fused_computation.20 | convolution fusion | flops 2828533760 | bytes 10485760 | tf_op jit(solution)/shard_map/dot_general | solution.py:77
  213.7 8.8 %collective-permute-done.34 = bf16[512,384]{1,0:T(8,128)(2,1)S(1)} collective-permute-done((bf16[512,384]{1,0:T(8,128)(2,1)S(1)}, bf16[512,384]{1,0:T(8,128)(2,1)S(1)}, u32[]{:S(2)}, u32[]{:S(2)}) %collective-permute-start.34) | collective-permute-done | bytes 393248 | tf_op jit(solution)/shard_map/ppermute | solution.py:33
  231.0 5.1 %add_convert_fusion = bf16[1536,896]{1,0:T(8,128)(2,1)S(1)} fusion(bf16[1536,896]{1,0:T(8,128)(2,1)} %collective-permute-done.32, bf16[1024,1536]{1,0:T(8,128)(2,1)S(1)} %copy-done.64, bf16[512,896]{1,0:T(8,128)(2,1)S(1)} %broadcast_select_fusion, bf16[512,896]{1,0:T(8,128)(2,1)S(1)} %broadcast_select_fusion.1), kind=kOutput, calls=%fused_computation.9 | convolution fusion | flops 2826371072 | bytes 10485760 | tf_op jit(solution)/shard_map/dot_general | solution.py:77
  239.5 3.8 collective-permute-done.35.refs_1_
  247.7 9.2 %all-to-all-start = ((bf16[32,72,896]{2,1,0:T(8,128)(2,1)}), bf16[32,72,896]{2,1,0:T(8,128)(2,1)}, u32[]{:S(2)}, u32[]{:S(2)}) async-start(bf16[32,72,896]{2,1,0:T(8,128)(2,1)} %bitcast.197), calls=%async_computation | async-start | bytes 8257536 | tf_op jit(solution)/shard_map/all_to_all | solution.py:685
  261.2 6.3 %stream.1 = (bf16[512,1536]{1,0:T(8,128)(2,1)}, f32[512,192]{1,0:T(8,128)}, f32[512,192]{1,0:T(8,128)}, f32[2,8,192]{2,1,0:T(8,128)S(1)}, f32[512,384]{1,0:T(8,128)}, /*index=5*/f32[1,384]{1,0:T(1,128)S(1)}) custom-call(bf16[512,384]{1,0:T(8,128)(2,1)S(1)} %get-tuple-element.185.refs_0_, bf16[512,384]{1,0:T(8,128)(2,1)S(1)} %copy-done.15, ...), custom_call_target="tpu_custom_call" | custom-call | flops 1000000 | bytes 1000000 | tf_op jit(solution)/shard_map/stream/pallas_call | solution.py:304
  276.2 13.1 %back.1 = (bf16[512,640]{1,0:T(8,128)(2,1)}, bf16[512,640]{1,0:T(8,128)(2,1)}, f32[528,384]{1,0:T(8,128)}, bf16[528,384]{1,0:T(8,128)(2,1)S(1)}, bf16[528,384]{1...) custom-call(bf16[528,384]{1,0:T(8,128)(2,1)S(1)} %maximum_maximum_fu, ...), custom_call_target="tpu_custom_call" | custom-call | flops 1000000 | bytes 1000000 | tf_op jit(solution)/shard_map/back/pallas_call | solution.py:404
  302.6 7.2 %all-to-all-done = bf16[32,72,896]{2,1,0:T(8,128)(2,1)} async-done(((bf16[32,72,896]{2,1,0:T(8,128)(2,1)}), bf16[32,72,896]{2,1,0:T(8,128)(2,1)}, u32[]{:S(2)}, u32[]{:S(2)}) %all-to-all-start) | async-done | bytes 4128800 | tf_op jit(solution)/shard_map/all_to_all | solution.py:685
  317.8 7.1 %collective-permute-start.40 = (bf16[72,3456]{1,0:T(8,128)(2,1)S(1)}, bf16[72,3456]{1,0:T(8,128)(2,1)S(1)}, u32[]{:S(2)}, u32[]{:S(2)}) collective-permute-start(bf16[72,3456]{1,0:T(8,128)(2,1)S(1)} %get-tuple-element.296), channel_id=1, source_target_pairs={{0,64},{64,0},{1,65},{65,1},{2,66},{66,2},{3,67},{67,3},{4,68},{68... | collective-permute-start | bytes 1493000 | tf_op jit(solution)/shard_map/ppermute | solution.py:168
  330.0 6.9 %collective-permute-done.40 = bf16[72,3456]{1,0:T(8,128)(2,1)S(1)} collective-permute-done((bf16[72,3456]{1,0:T(8,128)(2,1)S(1)}, bf16[72,3456]{1,0:T(8,128)(2,1)S(1)}, u32[]{:S(2)}, u32[]{:S(2)}) %collective-permute-start.40) | collective-permute-done | bytes 497696 | tf_op jit(solution)/shard_map/ppermute | solution.py:168
  338.2 5.7 %maximum_add_fusion = bf16[2,4,192,896]{3,2,0,1:T(8,128)(2,1)} fusion(f32[1,4,192,896]{3,2,0,1:T(8,128)} %maximum_bitcast_fusion.1, f32[1,4,192,896]{3,2,0,1:T(8,128)} %maximum_bitcast_fusion, bf16[2,4,192,896]{3,2,0,1:T(8,128)(2,1)} %collective-permute-done.39), kind=kLoop, calls=%fused_computation.6 | loop fusion | flops 5505024 | bytes 11010048 | tf_op jit(solution)/shard_map/add | solution.py:721
  348.5 3.6 copy.59
  352.1 19.3 %all-to-all-start.1 = ((bf16[64,24,896]{2,1,0:T(8,128)(2,1)}), bf16[64,24,896]{2,1,0:T(8,128)(2,1)}, u32[]{:S(2)}, u32[]{:S(2)}) async-start(bf16[64,24,896]{2,1,0:T(8,128)(2,1)} %bitcast.198), calls=%async_computation.2 | async-start | bytes 5505024 | tf_op jit(solution)/shard_map/all_to_all | solution.py:732
  371.5 3.3 slice_bitcast_fusion.1
  379.3 55.2 %all-to-all-done.1 = bf16[64,24,896]{2,1,0:T(8,128)(2,1)} async-done(((bf16[64,24,896]{2,1,0:T(8,128)(2,1)}), bf16[64,24,896]{2,1,0:T(8,128)(2,1)}, u32[]{:S(2)}, u32[]{:S(2)}) %all-to-all-start.1) | async-done | bytes 2752544 | tf_op jit(solution)/shard_map/all_to_all | solution.py:732
  439.2 4.9 %collective-permute-done.41 = bf16[4,24,896]{2,1,0:T(8,128)(2,1)S(1)} collective-permute-done((bf16[4,24,896]{2,1,0:T(8,128)(2,1)S(1)}, bf16[4,24,896]{2,1,0:T(8,128)(2,1)S(1)}, u32[]{:S(2)}, u32[]{:S(2)}) %collective-permute-start.41) | collective-permute-done | bytes 172064 | tf_op jit(solution)/shard_map/ppermute | solution.py:168
  452.2 11.5 %ffn_finish.1 = (f32[2,384,3456]{2,1,0:T(8,128)}, f32[3456,384]{1,0:T(8,128)}) custom-call(bf16[8,2,72,3456]{3,2,1,0:T(8,128)(2,1)} %bitcast.203), custom_call_target="tpu_custom_call" | custom-call | tf_op jit(solution)/shard_map/ffn_finish/pallas_call | solution.py:426
  467.3 3.7 all-gather.13.cloned.1.call-done
  (367 shorter events, 168.5 us)
Async XLA Ops:
  7.2 61.4 %all-gather.9.cloned.1.call-start = ((), (), s32[]{:S(2)}) async-start(), calls=%async_computation.4 | async-start | bytes 6193152 | tf_op jit(solution)/shard_map/all_gather | solution.py:622
  29.3 113.5 %all-gather.11.cloned.1.call-start = ((), (), s32[]{:S(2)}) async-start(), calls=%async_computation.5 | async-start | bytes 9289728 | tf_op jit(solution)/shard_map/all_gather | solution.py:628
  30.6 19.0 %collective-permute-start.2 = (bf16[528,384]{1,0:T(8,128)(2,1)S(1)}, bf16[528,384]{1,0:T(8,128)(2,1)}, u32[]{:S(2)}, u32[]{:S(2)}) collective-permute-start(bf16[528,384]{1,0:T(8,128)(2,1)S(1)} %maximum_maximum_fusion.refs_1_.refs_0_), channel_id=1, source_target_pairs={{0,1},{1,2},{2,3},{3,0},{4,5},{5,6},{6,7},{7,4},{8,9},{9,10},{10,1... | collective-permute-start | bytes 1216520 | tf_op jit(solution)/shard_map/ppermute | solution.py:21
  67.6 20.0 %collective-permute-start.14 = (bf16[512,384]{1,0:T(8,128)(2,1)S(1)}, bf16[512,384]{1,0:T(8,128)(2,1)}, u32[]{:S(2)}, u32[]{:S(2)}) collective-permute-start(bf16[512,384]{1,0:T(8,128)(2,1)S(1)} %copy-done.3), channel_id=1, source_target_pairs={{0,1},{1,2},{2,3},{3,0},{4,5},{5,6},{6,7},{7,4},{8,9},{9,10},{10,1... | collective-permute-start | bytes 1179656 | tf_op jit(solution)/shard_map/ppermute | solution.py:21
  91.9 45.4 %collective-permute-start.28 = (bf16[512,1536]{1,0:T(8,128)(2,1)}, bf16[512,1536]{1,0:T(8,128)(2,1)}, u32[]{:S(2)}, u32[]{:S(2)}) collective-permute-start(bf16[512,1536]{1,0:T(8,128)(2,1)} %constant_dynamic-update-slice_fusion), channel_id=1, source_target_pairs={{0,4},{4,0},{1,5},{5,1},{2,6},{6,2},{3,7},{7,3},{8,12},{12,8},{9,1... | collective-permute-start | bytes 4718600 | tf_op jit(solution)/shard_map/ppermute | solution.py:33
  93.9 19.6 %collective-permute-start.17 = (bf16[512,384]{1,0:T(8,128)(2,1)S(1)}, bf16[512,384]{1,0:T(8,128)(2,1)S(1)}, u32[]{:S(2)}, u32[]{:S(2)}) collective-permute-start(bf16[512,384]{1,0:T(8,128)(2,1)S(1)} %get-tuple-element.141), channel_id=1, source_target_pairs={{0,1},{1,2},{2,3},{3,0},{4,5},{5,6},{6,7},{7,4},{8,9},{9,10},{10,1... | collective-permute-start | bytes 1179656 | tf_op jit(solution)/shard_map/ppermute | solution.py:21
  114.3 22.6 %collective-permute-start.24 = (bf16[512,384]{1,0:T(8,128)(2,1)S(1)}, bf16[512,384]{1,0:T(8,128)(2,1)}, u32[]{:S(2)}, u32[]{:S(2)}) collective-permute-start(bf16[512,384]{1,0:T(8,128)(2,1)S(1)} %fusion.44.refs_0_.refs_4_), channel_id=1, source_target_pairs={{0,4},{4,0},{1,5},{5,1},{2,6},{6,2},{3,7},{7,3},{8,12},{12,8},{9,1... | collective-permute-start | bytes 1179656 | tf_op jit(solution)/shard_map/ppermute | solution.py:33
  116.8 23.4 %collective-permute-start.18 = (bf16[512,384]{1,0:T(8,128)(2,1)S(1)}, bf16[512,384]{1,0:T(8,128)(2,1)S(1)}, u32[]{:S(2)}, u32[]{:S(2)}) collective-permute-start(bf16[512,384]{1,0:T(8,128)(2,1)S(1)} %fusion.44.refs_0_.refs_4_), channel_id=1, source_target_pairs={{0,3},{1,0},{2,1},{3,2},{4,7},{5,4},{6,5},{7,6},{8,11},{9,8},{10,9... | collective-permute-start | bytes 1179656 | tf_op jit(solution)/shard_map/ppermute | solution.py:21
  118.1 23.9 %collective-permute-start.19 = (bf16[512,384]{1,0:T(8,128)(2,1)S(1)}, bf16[512,384]{1,0:T(8,128)(2,1)S(1)}, u32[]{:S(2)}, u32[]{:S(2)}) collective-permute-start(bf16[512,384]{1,0:T(8,128)(2,1)S(1)} %fusion.44.refs_0_.refs_4_), channel_id=1, source_target_pairs={{0,2},{1,3},{2,0},{3,1},{4,6},{5,7},{6,4},{7,5},{8,10},{9,11},{10,... | collective-permute-start | bytes 1179656 | tf_op jit(solution)/shard_map/ppermute | solution.py:21
  118.1 23.9 %collective-permute-start.20 = (bf16[512,384]{1,0:T(8,128)(2,1)S(1)}, bf16[512,384]{1,0:T(8,128)(2,1)S(1)}, u32[]{:S(2)}, u32[]{:S(2)}) collective-permute-start(bf16[512,384]{1,0:T(8,128)(2,1)S(1)} %fusion.44.refs_0_.refs_4_), channel_id=1, source_target_pairs={{0,1},{1,2},{2,3},{3,0},{4,5},{5,6},{6,7},{7,4},{8,9},{9,10},{10,1... | collective-permute-start | bytes 1179656 | tf_op jit(solution)/shard_map/ppermute | solution.py:21
  136.9 25.1 %collective-permute-start.25 = (bf16[512,384]{1,0:T(8,128)(2,1)}, bf16[512,384]{1,0:T(8,128)(2,1)}, u32[]{:S(2)}, u32[]{:S(2)}) collective-permute-start(bf16[512,384]{1,0:T(8,128)(2,1)} %collective-permute-done.24.refs_0_), channel_id=1, source_target_pairs={{0,3},{1,0},{2,1},{3,2},{4,7},{5,4},{6,5},{7,6},{8,11},{9,8},{10,9... | collective-permute-start | bytes 1179656 | tf_op jit(solution)/shard_map/ppermute | solution.py:21
  137.2 26.2 %collective-permute-start.26 = (bf16[512,384]{1,0:T(8,128)(2,1)}, bf16[512,384]{1,0:T(8,128)(2,1)}, u32[]{:S(2)}, u32[]{:S(2)}) collective-permute-start(bf16[512,384]{1,0:T(8,128)(2,1)} %collective-permute-done.24.refs_0_), channel_id=1, source_target_pairs={{0,2},{1,3},{2,0},{3,1},{4,6},{5,7},{6,4},{7,5},{8,10},{9,11},{10,... | collective-permute-start | bytes 1179656 | tf_op jit(solution)/shard_map/ppermute | solution.py:21
  140.2 23.2 %collective-permute-start.27 = (bf16[512,384]{1,0:T(8,128)(2,1)}, bf16[512,384]{1,0:T(8,128)(2,1)}, u32[]{:S(2)}, u32[]{:S(2)}) collective-permute-start(bf16[512,384]{1,0:T(8,128)(2,1)} %collective-permute-done.24.refs_0_), channel_id=1, source_target_pairs={{0,1},{1,2},{2,3},{3,0},{4,5},{5,6},{6,7},{7,4},{8,9},{9,10},{10,1... | collective-permute-start | bytes 1179656 | tf_op jit(solution)/shard_map/ppermute | solution.py:21
  157.9 21.0 %collective-permute-start.21 = (bf16[512,384]{1,0:T(8,128)(2,1)S(1)}, bf16[512,384]{1,0:T(8,128)(2,1)S(1)}, u32[]{:S(2)}, u32[]{:S(2)}) collective-permute-start(bf16[512,384]{1,0:T(8,128)(2,1)S(1)} %get-tuple-element.149), channel_id=1, source_target_pairs={{0,3},{1,0},{2,1},{3,2},{4,7},{5,4},{6,5},{7,6},{8,11},{9,8},{10,9... | collective-permute-start | bytes 1179656 | tf_op jit(solution)/shard_map/ppermute | solution.py:21
  160.6 18.3 %collective-permute-start.22 = (bf16[512,384]{1,0:T(8,128)(2,1)S(1)}, bf16[512,384]{1,0:T(8,128)(2,1)S(1)}, u32[]{:S(2)}, u32[]{:S(2)}) collective-permute-start(bf16[512,384]{1,0:T(8,128)(2,1)S(1)} %get-tuple-element.150), channel_id=1, source_target_pairs={{0,2},{1,3},{2,0},{3,1},{4,6},{5,7},{6,4},{7,5},{8,10},{9,11},{10,... | collective-permute-start | bytes 1179656 | tf_op jit(solution)/shard_map/ppermute | solution.py:21
  180.0 26.0 %collective-permute-start.29 = (bf16[512,384]{1,0:T(8,128)(2,1)S(1)}, bf16[512,384]{1,0:T(8,128)(2,1)}, u32[]{:S(2)}, u32[]{:S(2)}) collective-permute-start(bf16[512,384]{1,0:T(8,128)(2,1)S(1)} %get-tuple-element.162), channel_id=1, source_target_pairs={{0,3},{1,0},{2,1},{3,2},{4,7},{5,4},{6,5},{7,6},{8,11},{9,8},{10,9... | collective-permute-start | bytes 1179656 | tf_op jit(solution)/shard_map/ppermute | solution.py:21
  180.8 25.1 %collective-permute-start.30 = (bf16[512,384]{1,0:T(8,128)(2,1)S(1)}, bf16[512,384]{1,0:T(8,128)(2,1)}, u32[]{:S(2)}, u32[]{:S(2)}) collective-permute-start(bf16[512,384]{1,0:T(8,128)(2,1)S(1)} %get-tuple-element.163), channel_id=1, source_target_pairs={{0,2},{1,3},{2,0},{3,1},{4,6},{5,7},{6,4},{7,5},{8,10},{9,11},{10,... | collective-permute-start | bytes 1179656 | tf_op jit(solution)/shard_map/ppermute | solution.py:21
  182.1 23.9 %collective-permute-start.31 = (bf16[512,384]{1,0:T(8,128)(2,1)S(1)}, bf16[512,384]{1,0:T(8,128)(2,1)}, u32[]{:S(2)}, u32[]{:S(2)}) collective-permute-start(bf16[512,384]{1,0:T(8,128)(2,1)S(1)} %get-tuple-element.164), channel_id=1, source_target_pairs={{0,1},{1,2},{2,3},{3,0},{4,5},{5,6},{6,7},{7,4},{8,9},{9,10},{10,1... | collective-permute-start | bytes 1179656 | tf_op jit(solution)/shard_map/ppermute | solution.py:21
  206.0 25.0 %collective-permute-start.32 = (bf16[1536,896]{1,0:T(8,128)(2,1)}, bf16[1536,896]{1,0:T(8,128)(2,1)}, u32[]{:S(2)}, u32[]{:S(2)}) collective-permute-start(bf16[1536,896]{1,0:T(8,128)(2,1)} %convolution_convert_fusion), channel_id=1, source_target_pairs={{0,8},{8,0},{1,9},{9,1},{2,10},{10,2},{3,11},{11,3},{4,12},{12,4},... | collective-permute-start | bytes 8257544 | tf_op jit(solution)/shard_map/ppermute | solution.py:37
  209.1 20.2 %collective-permute-start.33 = (bf16[4,192,896]{2,1,0:T(8,128)(2,1)}, bf16[4,192,896]{2,1,0:T(8,128)(2,1)}, u32[]{:S(2)}, u32[]{:S(2)}) collective-permute-start(bf16[4,192,896]{2,1,0:T(8,128)(2,1)} %fusion.17), channel_id=1, source_target_pairs={{0,8},{8,0},{1,9},{9,1},{2,10},{10,2},{3,11},{11,3},{4,12},{12,4},... | collective-permute-start | bytes 4128776 | tf_op jit(solution)/shard_map/ppermute | solution.py:37
  224.7 18.6 %collective-permute-start.35 = (bf16[512,384]{1,0:T(8,128)(2,1)S(1)}, bf16[512,384]{1,0:T(8,128)(2,1)S(1)}, u32[]{:S(2)}, u32[]{:S(2)}) collective-permute-start(bf16[512,384]{1,0:T(8,128)(2,1)S(1)} %get-tuple-element.185.refs_0_), channel_id=1, source_target_pairs={{0,3},{1,0},{2,1},{3,2},{4,7},{5,4},{6,5},{7,6},{8,11},{9,8},{10,9... | collective-permute-start | bytes 1179656 | tf_op jit(solution)/shard_map/ppermute | solution.py:21
  228.2 18.8 %collective-permute-start.37 = (bf16[512,384]{1,0:T(8,128)(2,1)S(1)}, bf16[512,384]{1,0:T(8,128)(2,1)S(1)}, u32[]{:S(2)}, u32[]{:S(2)}) collective-permute-start(bf16[512,384]{1,0:T(8,128)(2,1)S(1)} %get-tuple-element.185.refs_0_), channel_id=1, source_target_pairs={{0,1},{1,2},{2,3},{3,0},{4,5},{5,6},{6,7},{7,4},{8,9},{9,10},{10,1... | collective-permute-start | bytes 1179656 | tf_op jit(solution)/shard_map/ppermute | solution.py:21
  247.7 62.2 %all-to-all-start = ((bf16[32,72,896]{2,1,0:T(8,128)(2,1)}), bf16[32,72,896]{2,1,0:T(8,128)(2,1)}, u32[]{:S(2)}, u32[]{:S(2)}) async-start(bf16[32,72,896]{2,1,0:T(8,128)(2,1)} %bitcast.197), calls=%async_computation | async-start | bytes 8257536 | tf_op jit(solution)/shard_map/all_to_all | solution.py:685
  257.0 87.0 %reduce-scatter.2.cloned.1.call-start = ((), (), s32[]{:S(2)}) async-start(), calls=%async_computation.3 | async-start | bytes 2027520 | tf_op jit(solution)/shard_map/reduce_scatter | solution.py:698
  292.6 159.5 %all-gather.15.cloned.1.call-start = ((), (), s32[]{:S(2)}) async-start(), calls=%async_computation.7 | async-start | bytes 8957952 | tf_op jit(solution)/shard_map/all_gather | solution.py:729
  309.9 28.3 %collective-permute-start.39 = (bf16[2,4,192,896]{3,2,0,1:T(8,128)(2,1)}, bf16[2,4,192,896]{3,2,0,1:T(8,128)(2,1)}, u32[]{:S(2)}, u32[]{:S(2)}) collective-permute-start(bf16[2,4,192,896]{3,2,0,1:T(8,128)(2,1)} %pad_maximum_fusion), channel_id=1, source_target_pairs={{0,8},{8,0},{1,9},{9,1},{2,10},{10,2},{3,11},{11,3},{4,12},{12,4},... | collective-permute-start | bytes 8257544 | tf_op jit(solution)/shard_map/ppermute | solution.py:37
  317.8 19.1 %collective-permute-start.40 = (bf16[72,3456]{1,0:T(8,128)(2,1)S(1)}, bf16[72,3456]{1,0:T(8,128)(2,1)S(1)}, u32[]{:S(2)}, u32[]{:S(2)}) collective-permute-start(bf16[72,3456]{1,0:T(8,128)(2,1)S(1)} %get-tuple-element.296), channel_id=1, source_target_pairs={{0,64},{64,0},{1,65},{65,1},{2,66},{66,2},{3,67},{67,3},{4,68},{68... | collective-permute-start | bytes 1493000 | tf_op jit(solution)/shard_map/ppermute | solution.py:168
  352.1 82.4 %all-to-all-start.1 = ((bf16[64,24,896]{2,1,0:T(8,128)(2,1)}), bf16[64,24,896]{2,1,0:T(8,128)(2,1)}, u32[]{:S(2)}, u32[]{:S(2)}) async-start(bf16[64,24,896]{2,1,0:T(8,128)(2,1)} %bitcast.198), calls=%async_computation.2 | async-start | bytes 5505024 | tf_op jit(solution)/shard_map/all_to_all | solution.py:732
  371.5 99.5 %all-gather.13.cloned.1.call-start = ((), (), s32[]{:S(2)}) async-start(), calls=%async_computation.6 | async-start | bytes 3096576 | tf_op jit(solution)/shard_map/all_gather | solution.py:754
  374.9 70.0 %collective-permute-start.42 = (bf16[2,512,384]{2,1,0:T(8,128)(2,1)}, bf16[2,512,384]{2,1,0:T(8,128)(2,1)S(1)}, u32[]{:S(2)}, u32[]{:S(2)}) collective-permute-start(bf16[2,512,384]{2,1,0:T(8,128)(2,1)} %get-tuple-element.261), channel_id=1, source_target_pairs={{0,3},{1,0},{2,1},{3,2},{4,7},{5,4},{6,5},{7,6},{8,11},{9,8},{10,9... | collective-permute-start | bytes 2359304 | tf_op jit(solution)/shard_map/ppermute | solution.py:21
  377.6 67.3 %collective-permute-start.43 = (bf16[2,512,384]{2,1,0:T(8,128)(2,1)}, bf16[2,512,384]{2,1,0:T(8,128)(2,1)S(1)}, u32[]{:S(2)}, u32[]{:S(2)}) collective-permute-start(bf16[2,512,384]{2,1,0:T(8,128)(2,1)} %get-tuple-element.260), channel_id=1, source_target_pairs={{0,2},{1,3},{2,0},{3,1},{4,6},{5,7},{6,4},{7,5},{8,10},{9,11},{10,... | collective-permute-start | bytes 2359304 | tf_op jit(solution)/shard_map/ppermute | solution.py:21
  378.4 66.5 %collective-permute-start.44 = (bf16[2,512,384]{2,1,0:T(8,128)(2,1)}, bf16[2,512,384]{2,1,0:T(8,128)(2,1)}, u32[]{:S(2)}, u32[]{:S(2)}) collective-permute-start(bf16[2,512,384]{2,1,0:T(8,128)(2,1)} %get-tuple-element.259), channel_id=1, source_target_pairs={{0,1},{1,2},{2,3},{3,0},{4,5},{5,6},{6,7},{7,4},{8,9},{9,10},{10,1... | collective-permute-start | bytes 2359304 | tf_op jit(solution)/shard_map/ppermute | solution.py:21
  (98 other events, 1205.4 us)
Sparse Core Ops, SparseCore 0:
  29.4 37.1 all-gather.8
  68.9 49.1 all-gather.10
  292.7 46.9 reduce-scatter.1
  348.6 87.4 all-gather.14
  445.1 25.8 all-gather.12
